TPU v7x, 32 devices: a whole 2x2x4 slice. The times are simulated.
32 devices in a mesh: stream: 2 (over x), frames: 16 (over z, y, core).
Axes of the slice: x: 2, y: 2, z: 4, core: 2. Of those that a mesh axis runs over, the one named last changes fastest.
Arguments:
- tokens: bfloat16 [2, 2048, 8, 1024], P('stream', 'frames'), may hold values from -6 to 6
- context: bfloat16 [2048, 1024], P('frames', 'stream'), may hold values from -6 to 6
- ctx_weight: bfloat16 [1024, 1024], P(('stream', 'frames')), may hold values from -0.1875 to 0.1875
- delay: int32 [8], replicated, may hold values from 0 to 2, as said below
- lengths: int32 [3], replicated, may hold values from 1 to 1024, 2048 in all
- attn_gain: bfloat16 [2, 8, 1024], P('stream'), may hold values from 0.5 to 1.5
- ffn_gain: bfloat16 [2, 8, 1024], P('stream'), may hold values from 0.5 to 1.5
- qkv_weight: bfloat16 [2, 1024, 3072], P('stream', 'frames'), may hold values from -0.1875 to 0.1875
- out_weight: bfloat16 [2, 1024, 1024], P('stream', 'frames'), may hold values from -0.375 to 0.375
- gate_weight: bfloat16 [2, 1024, 2816], P('stream', 'frames'), may hold values from -0.1875 to 0.1875
- up_weight: bfloat16 [2, 1024, 2816], P('stream', 'frames'), may hold values from -0.1875 to 0.1875
- down_weight: bfloat16 [2, 2816, 1024], P('stream', 'frames'), may hold values from -0.1875 to 0.1875
- cotangent: bfloat16 [2, 2048, 8, 1024], P('stream', 'frames'), may hold values from -6 to 6
Outputs:
- mixed_out: bfloat16 [2, 2048, 8, 1024], P('stream', 'frames')
- d_tokens: float32 [2, 2048, 8, 1024], P('stream', 'frames')
- d_context: float32 [2048, 1024], P('frames', 'stream')
- d_ctx_weight: float32 [1024, 1024], P(('stream', 'frames'))
- d_attn_gain: float32 [2, 8, 1024], P('stream')
- d_ffn_gain: float32 [2, 8, 1024], P('stream')
- d_qkv: float32 [2, 1024, 3072], P('stream', 'frames')
- d_out: float32 [2, 1024, 1024], P('stream', 'frames')
- d_gate: float32 [2, 1024, 2816], P('stream', 'frames')
- d_up: float32 [2, 1024, 2816], P('stream', 'frames')
- d_down: float32 [2, 2816, 1024], P('stream', 'frames')
Inputs may be any that keep to these rules, and one draw needn't show every extreme that they name: Position 0 has delay 0, position 7 has delay 2, every other position 1 or 2. Item lengths in frames, in order, summing to 2048; the longest has 1024.
All inputs are finite; a program needn't handle non-finite values.
Results may differ from a plain program's by a relative error of at most 0.014.
Values may be sent and summed in bfloat16 or wider, within the bound.
A program may use at most 256 MiB of HBM per device.

v0:
```python
import jax
import jax.numpy as jnp
from jax import lax
from jax.sharding import PartitionSpec as P

HEADS = 16
HEAD = 64


epsilon = 1e-05


def shifted(x, axis, by):
    length = lax.axis_size(axis)
    pairs = [(i, i + by) for i in range(length) if 0 <= i + by < length]
    return lax.ppermute(x, axis, pairs)


def flat_dot(left, right):
    return jnp.dot(left, right, preferred_element_type=jnp.float32)


def trans_dot(left, right):
    return lax.dot_general(
        left, right, (((0,), (0,)), ((), ())), preferred_element_type=jnp.float32
    )


def back_dot(left, right):
    return lax.dot_general(
        left, right, (((1,), (1,)), ((), ())), preferred_element_type=jnp.float32
    )


def norm_rows(rows, gain):
    return rows * lax.rsqrt(jnp.mean(rows * rows, axis=-1, keepdims=True) + epsilon) * gain


def norm_back(grad_normed, rows, gain):
    scale = lax.rsqrt(jnp.mean(rows * rows, axis=-1, keepdims=True) + epsilon)
    unit = rows * scale
    grad_gain = jnp.sum(grad_normed * unit, axis=0)
    grad_unit = grad_normed * gain
    grad_rows = scale * (grad_unit - unit * jnp.mean(grad_unit * unit, axis=-1, keepdims=True))
    return (grad_rows, grad_gain)


def shift_tables(delay, lengths, frame_ids):
    starts = jnp.cumsum(lengths) - lengths
    at_start = jnp.any(frame_ids[:, None] == starts[None, :], axis=1)
    after_start = jnp.any(frame_ids[:, None] - 1 == starts[None, :], axis=1)
    keep_one = jnp.logical_not(at_start)
    keep_two = jnp.logical_and(keep_one, jnp.logical_not(after_start))
    valid_rows = jnp.stack([jnp.ones_like(keep_one), keep_one, keep_two]).astype(jnp.float32)
    chosen = (delay[None, :] == jnp.arange(3, dtype=jnp.int32)[:, None]).astype(jnp.float32)
    return (chosen, valid_rows)


def body(
    tokens,
    context,
    ctx_weight,
    delay,
    lengths,
    attn_gain,
    ffn_gain,
    qkv_weight,
    out_weight,
    gate_weight,
    up_weight,
    down_weight,
    cotangent,
):
    frame_count = tokens.shape[1]
    positions = tokens.shape[2]
    model_width = tokens.shape[3]
    token_rows = frame_count * positions
    head_scale = HEAD ** (-0.5)
    ctx_full = lax.all_gather(context, "stream", axis=1, tiled=True)
    ctx_rows = lax.all_gather(ctx_weight, ("stream", "frames"), axis=0, tiled=True)
    shift_term = flat_dot(ctx_full, ctx_rows)
    inputs = tokens[0]
    rim_rows = shifted(inputs[frame_count - 2 :], "frames", 1)
    extended = jnp.concatenate([rim_rows, inputs], axis=0).astype(jnp.float32)
    frame_ids = lax.axis_index("frames") * frame_count + jnp.arange(frame_count, dtype=jnp.int32)
    chosen, valid_rows = shift_tables(delay, lengths, frame_ids)
    layer_in = jnp.broadcast_to(shift_term[:, None, :], (frame_count, positions, model_width))
    for offset in range(3):
        piece = extended[2 - offset : 2 - offset + frame_count]
        layer_in = (
            layer_in + chosen[offset][None, :, None] * valid_rows[offset][:, None, None] * piece
        )
    weights = (
        lax.all_gather(qkv_weight[0], "frames", axis=0, tiled=True),
        lax.all_gather(out_weight[0], "frames", axis=0, tiled=True),
        lax.all_gather(gate_weight[0], "frames", axis=0, tiled=True),
        lax.all_gather(up_weight[0], "frames", axis=0, tiled=True),
        lax.all_gather(down_weight[0], "frames", axis=0, tiled=True),
    )
    w_qkv, w_out, w_gate, w_up, w_down = weights
    gain_one = attn_gain[0].astype(jnp.float32)
    gain_two = ffn_gain[0].astype(jnp.float32)
    normed = norm_rows(layer_in, gain_one).astype(jnp.bfloat16).reshape(token_rows, model_width)
    qkv = (
        flat_dot(normed, w_qkv).astype(jnp.bfloat16).reshape(frame_count, positions, 3, HEADS, HEAD)
    )
    queries = qkv[:, :, 0]
    key_part = qkv[:, :, 1]
    values = qkv[:, :, 2]
    scores = (
        jnp.einsum("fqhd,fkhd->fhqk", queries, key_part, preferred_element_type=jnp.float32)
        * head_scale
    )
    causal = jnp.arange(positions)[:, None] >= jnp.arange(positions)[None, :]
    scores = jnp.where(causal[None, None], scores, -1e30)
    probs = jax.nn.softmax(scores, axis=-1)
    probs_low = probs.astype(jnp.bfloat16)
    mixed = jnp.einsum("fhqk,fkhd->fqhd", probs_low, values, preferred_element_type=jnp.float32)
    mixed = mixed.astype(jnp.bfloat16).reshape(token_rows, model_width)
    after_attn = layer_in + flat_dot(mixed, w_out).reshape(frame_count, positions, model_width)
    normed_two = (
        norm_rows(after_attn, gain_two).astype(jnp.bfloat16).reshape(token_rows, model_width)
    )
    gate_pre = flat_dot(normed_two, w_gate)
    up_pre = flat_dot(normed_two, w_up)
    hidden = (jax.nn.silu(gate_pre) * up_pre).astype(jnp.bfloat16)
    out_full = after_attn + flat_dot(hidden, w_down).reshape(frame_count, positions, model_width)
    back_weights = (
        lax.all_gather(qkv_weight[0], "frames", axis=0, tiled=True),
        lax.all_gather(out_weight[0], "frames", axis=0, tiled=True),
        lax.all_gather(gate_weight[0], "frames", axis=0, tiled=True),
        lax.all_gather(up_weight[0], "frames", axis=0, tiled=True),
        lax.all_gather(down_weight[0], "frames", axis=0, tiled=True),
    )
    b_qkv, b_out, b_gate, b_up, b_down = back_weights
    grad_out = cotangent[0].astype(jnp.float32)
    grad_ff = grad_out.reshape(token_rows, model_width).astype(jnp.bfloat16)
    grad_down = trans_dot(hidden, grad_ff)
    grad_hidden = back_dot(grad_ff, b_down)
    sigmoid_gate = jax.nn.sigmoid(gate_pre)
    grad_gate = (
        grad_hidden * up_pre * sigmoid_gate * (1.0 + gate_pre * (1.0 - sigmoid_gate))
    ).astype(jnp.bfloat16)
    grad_up = (grad_hidden * gate_pre * sigmoid_gate).astype(jnp.bfloat16)
    grad_gate_w = trans_dot(normed_two, grad_gate)
    grad_up_w = trans_dot(normed_two, grad_up)
    grad_normed_two = (back_dot(grad_gate, b_gate) + back_dot(grad_up, b_up)).reshape(
        frame_count, positions, model_width
    )
    grad_after_norm, grad_gain_two = norm_back(grad_normed_two, after_attn, gain_two)
    grad_after = grad_out + grad_after_norm
    grad_branch = grad_after.reshape(token_rows, model_width).astype(jnp.bfloat16)
    grad_out_w = trans_dot(mixed, grad_branch)
    grad_mixed = (
        back_dot(grad_branch, b_out)
        .astype(jnp.bfloat16)
        .reshape(frame_count, positions, HEADS, HEAD)
    )
    grad_values = jnp.einsum(
        "fhqk,fqhd->fkhd", probs_low, grad_mixed, preferred_element_type=jnp.float32
    )
    grad_probs = jnp.einsum(
        "fqhd,fkhd->fhqk", grad_mixed, values, preferred_element_type=jnp.float32
    )
    grad_scores = (
        probs * (grad_probs - jnp.sum(grad_probs * probs, axis=-1, keepdims=True))
    ).astype(jnp.bfloat16)
    grad_queries = (
        jnp.einsum("fhqk,fkhd->fqhd", grad_scores, key_part, preferred_element_type=jnp.float32)
        * head_scale
    )
    grad_keys = (
        jnp.einsum("fhqk,fqhd->fkhd", grad_scores, queries, preferred_element_type=jnp.float32)
        * head_scale
    )
    grad_qkv = jnp.stack([grad_queries, grad_keys, grad_values], axis=2).astype(jnp.bfloat16)
    grad_qkv = grad_qkv.reshape(token_rows, 3 * model_width)
    grad_qkv_w = trans_dot(normed, grad_qkv)
    all_parts = (
        lax.psum_scatter(grad_qkv_w, "frames", scatter_dimension=0, tiled=True),
        lax.psum_scatter(grad_out_w, "frames", scatter_dimension=0, tiled=True),
        lax.psum_scatter(grad_gate_w, "frames", scatter_dimension=0, tiled=True),
        lax.psum_scatter(grad_up_w, "frames", scatter_dimension=0, tiled=True),
        lax.psum_scatter(grad_down, "frames", scatter_dimension=0, tiled=True),
    )
    d_qkv_rows, d_out_rows, d_gate_rows, d_up_rows, d_down_rows = all_parts
    grad_normed = back_dot(grad_qkv, b_qkv).reshape(frame_count, positions, model_width)
    grad_in_norm, grad_gain_one = norm_back(grad_normed, layer_in, gain_one)
    grad_in = grad_after + grad_in_norm
    gain_sums = lax.psum((grad_gain_one, grad_gain_two), "frames")
    grad_shift = jnp.sum(grad_in, axis=1).astype(jnp.bfloat16)
    grad_ctx_w = trans_dot(ctx_full, grad_shift)
    ctx_w_rows = lax.psum_scatter(grad_ctx_w, ("stream", "frames"), scatter_dimension=0, tiled=True)
    grad_context = back_dot(grad_shift, ctx_rows)
    context_half = lax.psum_scatter(
        grad_context.astype(jnp.bfloat16), "stream", scatter_dimension=1, tiled=True
    ).astype(jnp.float32)
    grad_ext = jnp.zeros((frame_count + 2, positions, model_width), jnp.float32)
    for offset in range(3):
        term = chosen[offset][None, :, None] * valid_rows[offset][:, None, None] * grad_in
        grad_ext = grad_ext + jnp.pad(term, ((2 - offset, offset), (0, 0), (0, 0)))
    back_rows = shifted(grad_ext[:2].astype(jnp.bfloat16), "frames", -1).astype(jnp.float32)
    grad_tokens = grad_ext[2:].at[frame_count - 2 :].add(back_rows)
    return (
        out_full.astype(jnp.bfloat16)[None],
        grad_tokens[None],
        context_half,
        ctx_w_rows,
        gain_sums[0][None],
        gain_sums[1][None],
        d_qkv_rows[None],
        d_out_rows[None],
        d_gate_rows[None],
        d_up_rows[None],
        d_down_rows[None],
    )


def solution(mesh):
    return jax.shard_map(
        body,
        mesh=mesh,
        in_specs=(
            P("stream", "frames", None, None),
            P("frames", "stream"),
            P(("stream", "frames"), None),
            P(),
            P(),
            P("stream", None, None),
            P("stream", None, None),
            P("stream", "frames", None),
            P("stream", "frames", None),
            P("stream", "frames", None),
            P("stream", "frames", None),
            P("stream", "frames", None),
            P("stream", "frames", None, None),
        ),
        out_specs=(
            P("stream", "frames", None, None),
            P("stream", "frames", None, None),
            P("frames", "stream"),
            P(("stream", "frames"), None),
            P("stream", None, None),
            P("stream", None, None),
            P("stream", "frames", None),
            P("stream", "frames", None),
            P("stream", "frames", None),
            P("stream", "frames", None),
            P("stream", "frames", None),
        ),
        check_vma=False,
    )
```

profile of v0, /device:TPU:0, one launch (start us, length us, event | category | flops | bytes accessed | tf_op | source)
XLA Modules:
  0.0 1377.6 jit_solution(9648438000005541496)
XLA Ops:
  16.6 6.1 all_gather.26
  25.5 44.6 %all-gather.12.cloned.1.call-done = bf16[1024,1024]{1,0:T(8,128)(2,1)} async-done(((bf16[32,1024]{1,0:T(8,128)(2,1)}), bf16[1024,1024]{1,0:T(8,128)(2,1)}) %all-gather.12.cloned.1.call-update) | async-done | bytes 2097168 | tf_op jit(solution)/shard_map/all_gather | solution.py:80
  72.2 6.6 multiply_reduce_fusion.6
  82.8 47.5 %all-gather.22.cloned.1.call-done = bf16[1,2816,1024]{2,1,0:T(8,128)(2,1)} async-done(((bf16[1,176,1024]{2,1,0:T(8,128)(2,1)}), bf16[1,2816,1024]{2,1,0:T(8,128)(2,1)}) %all-gather.22.cloned.1.call-update) | async-done | bytes 5767184 | tf_op jit(solution)/shard_map/all_gather | solution.py:98
  130.3 11.5 fusion.6
  141.8 51.2 %all-gather.14.cloned.1.call-done = bf16[1,1024,3072]{2,1,0:T(8,128)(2,1)} async-done(((bf16[1,64,3072]{2,1,0:T(8,128)(2,1)}), bf16[1,1024,3072]{2,1,0:T(8,128)(2,1)}) %all-gather.14.cloned.1.call-update) | async-done | bytes 6291472 | tf_op jit(solution)/shard_map/all_gather | solution.py:94
  193.1 12.2 fusion.18
  205.2 16.0 %reshape.316 = bf16[128,8,3,16,64]{4,3,2,1,0:T(8,128)(2,1)} reshape(bf16[1024,3072]{1,0:T(8,128)(2,1)} %fusion.18) | data formatting | bytes 12582912 | tf_op jit(solution)/shard_map/reshape | solution.py:105
  221.2 7.9 fusion.89
  234.7 7.3 fusion.91
  242.0 8.9 convert_bitcast_fusion
  250.9 5.5 copy.119
  256.4 5.4 multiply_reduce_fusion.5
  264.3 30.8 %all-gather.20.cloned.1.call-done = bf16[1,1024,2816]{2,1,0:T(8,128)(2,1)} async-done(((bf16[1,64,2816]{2,1,0:T(8,128)(2,1)}), bf16[1,1024,2816]{2,1,0:T(8,128)(2,1)}) %all-gather.20.cloned.1.call-update) | async-done | bytes 5767184 | tf_op jit(solution)/shard_map/all_gather | solution.py:97
  295.1 13.6 fusion.12
  308.7 46.2 %all-gather.18.cloned.1.call-done = bf16[1,1024,2816]{2,1,0:T(8,128)(2,1)} async-done(((bf16[1,64,2816]{2,1,0:T(8,128)(2,1)}), bf16[1,1024,2816]{2,1,0:T(8,128)(2,1)}) %all-gather.18.cloned.1.call-update) | async-done | bytes 5767184 | tf_op jit(solution)/shard_map/all_gather | solution.py:96
  354.9 21.1 %multiply_convert_fusion.1 = (bf16[1024,2816]{1,0:T(8,128)(2,1)}, bf16[1024,2816]{1,0:T(8,128)(2,1)}, bf16[1024,2816]{1,0:T(8,128)(2,1)}) fusion(f32[1024,2816]{1,0:T(8,128)} %fusion.6, f32[1024,2816]{1,0:T(8,128)} %fusion.12, bf16[1,1024,2816]{2,1,0:T(8,128)(2,1)} %all-gather.18.cloned.1.call-done, bf16[128,8,1024]{2,0,1:T(8,128)(2,1)S(1)} %multiply_convert_fusion.4), kind=kOutput, calls=%fused_computation.3 | convolution fusion | flops 5951717376 | bytes 48234496 | tf_op jit(solution)/shard_map/dot_general | solution.py:20
  376.0 10.0 fusion.10
  386.1 6.1 add_bitcast_fusion
  395.9 7.0 fusion.79
  410.8 9.0 fusion.33
  419.8 10.1 multiply_reduce_fusion
  429.9 7.7 multiply_convert_fusion.3
  437.6 5.6 fusion.30
  443.2 4.8 fusion.32
  448.0 5.5 copy.131
  453.5 8.0 copy.129
  465.6 8.0 copy.128
  480.1 12.0 multiply_reduce_fusion.2
  492.2 11.3 fusion.36
  503.5 13.0 fusion.87
  518.1 5.6 copy.136
  523.7 6.7 reshape.321
  530.5 6.8 fusion.40
  541.0 5.5 copy.144
  546.5 11.9 fusion.44
  558.5 12.6 fusion.49
  571.2 13.1 fusion.47
  584.4 18.5 %copy.135 = bf16[128,8,3,16,64]{4,3,2,1,0:T(8,128)(2,1)} copy(bf16[128,8,3,16,64]{0,4,3,2,1:T(8,128)(2,1)} %copy-done.11) | data formatting | bytes 12582912 | tf_op jit(solution)/shard_map/convert_element_type | solution.py:176
  602.9 16.3 %convert_element_type.125 = bf16[1024,3072]{1,0:T(8,128)(2,1)} reshape(bf16[128,8,3,16,64]{4,3,2,1,0:T(8,128)(2,1)} %copy.135) | data formatting | bytes 12582912 | tf_op jit(solution)/shard_map/convert_element_type | solution.py:176
  619.2 13.4 fusion.56
  642.8 4.4 copy.138
  648.9 47.4 %reduce-scatter.14.cloned.1.call-done = f32[64,1024]{1,0:T(8,128)} async-done(((f32[1024,1024]{1,0:T(8,128)}), f32[64,1024]{1,0:T(8,128)}) %reduce-scatter.14.cloned.1.call-update) | async-done | bytes 262160 | tf_op jit(solution)/shard_map/reduce_scatter | solution.py:181
  696.4 143.3 %reduce-scatter.22.cloned.1.call-done = f32[32,1024]{1,0:T(8,128)} async-done(((f32[1024,1024]{1,0:T(8,128)}), f32[32,1024]{1,0:T(8,128)}) %reduce-scatter.22.cloned.1.call-update) | async-done | bytes 131088
  839.7 127.5 %reduce-scatter.20.cloned.1.call-done = f32[176,1024]{1,0:T(8,128)} async-done(((f32[2816,1024]{1,0:T(8,128)}), f32[176,1024]{1,0:T(8,128)}) %reduce-scatter.20.cloned.1.call-update) | async-done | bytes 720912 | tf_op jit(solution)/shard_map/reduce_scatter | solution.py:184
  967.2 130.6 %reduce-scatter.16.cloned.1.call-done = f32[64,2816]{1,0:T(8,128)} async-done(((f32[1024,2816]{1,0:T(8,128)}), f32[64,2816]{1,0:T(8,128)}) %reduce-scatter.16.cloned.1.call-update) | async-done | bytes 720912 | tf_op jit(solution)/shard_map/reduce_scatter | solution.py:182
  1097.8 131.3 %reduce-scatter.18.cloned.1.call-done = f32[64,2816]{1,0:T(8,128)} async-done(((f32[1024,2816]{1,0:T(8,128)}), f32[64,2816]{1,0:T(8,128)}) %reduce-scatter.18.cloned.1.call-update) | async-done | bytes 720912 | tf_op jit(solution)/shard_map/reduce_scatter | solution.py:183
  1229.1 139.0 %reduce-scatter.12.cloned.1.call-done = f32[64,3072]{1,0:T(8,128)} async-done(((f32[1024,3072]{1,0:T(8,128)}), f32[64,3072]{1,0:T(8,128)}) %reduce-scatter.12.cloned.1.call-update) | async-done | bytes 786448 | tf_op jit(solution)/shard_map/reduce_scatter | solution.py:180
  (157 shorter events, 68.2 us)
Async XLA Ops:
  7.2 8.7 copy-start.37
  7.2 9.1 copy-start.35
  7.2 9.3 copy-start.33
  7.2 9.3 copy-start.34
  7.2 9.3 copy-start.24
  7.2 62.9 %all-gather.12.cloned.1.call-start = ((), (), s32[]{:S(2)}) async-start(), calls=%async_computation.7 | async-start | bytes 2162688 | tf_op jit(solution)/shard_map/all_gather | solution.py:80
  8.0 122.3 %all-gather.22.cloned.1.call-start = ((), (), s32[]{:S(2)}) async-start(), calls=%async_computation.18 | async-start | bytes 6127616 | tf_op jit(solution)/shard_map/all_gather | solution.py:98
  8.7 184.4 %all-gather.14.cloned.1.call-start = ((), (), s32[]{:S(2)}) async-start(), calls=%async_computation.14 | async-start | bytes 6684672 | tf_op jit(solution)/shard_map/all_gather | solution.py:94
  9.4 247.0 %all-gather.16.cloned.1.call-start = ((), (), s32[]{:S(2)}) async-start(), calls=%async_computation.15 | async-start | bytes 2228224 | tf_op jit(solution)/shard_map/all_gather | solution.py:95
  10.0 285.1 %all-gather.20.cloned.1.call-start = ((), (), s32[]{:S(2)}) async-start(), calls=%async_computation.17 | async-start | bytes 6127616 | tf_op jit(solution)/shard_map/all_gather | solution.py:97
  10.6 344.3 %all-gather.18.cloned.1.call-start = ((), (), s32[]{:S(2)}) async-start(), calls=%async_computation.16 | async-start | bytes 6127616 | tf_op jit(solution)/shard_map/all_gather | solution.py:96
  13.4 9.3 collective-permute-start
  15.8 631.4 %reduce-scatter.10.cloned.1.call-start = ((), (), s32[]{:S(2)}) async-start(), calls=%async_computation.8 | async-start | bytes 393216 | tf_op jit(solution)/shard_map/reduce_scatter | solution.py:195
  16.4 55.7 %copy-start.25 = (f32[128,8]{0,1:T(8,128)}, f32[128,8]{0,1:T(8,128)S(1)}, u32[]{:S(2)}) copy-start(f32[128,8]{0,1:T(8,128)S(1)} %broadcast_multiply_fusion.7) | copy-start | bytes 12292
  16.5 55.7 %copy-start.27 = (f32[128,8]{0,1:T(8,128)}, f32[128,8]{0,1:T(8,128)S(1)}, u32[]{:S(2)}) copy-start(f32[128,8]{0,1:T(8,128)S(1)} %broadcast_multiply_fusion.5) | copy-start | bytes 12292
  16.5 55.6 %copy-start.29 = (f32[128,8]{0,1:T(8,128)}, f32[128,8]{0,1:T(8,128)S(1)}, u32[]{:S(2)}) copy-start(f32[128,8]{0,1:T(8,128)S(1)} %broadcast_multiply_fusion.6) | copy-start | bytes 12292
  16.6 62.2 %copy-start.22 = (f32[8,1024]{1,0:T(8,128)}, f32[8,1024]{1,0:T(8,128)S(1)}, u32[]{:S(2)}) copy-start(f32[8,1024]{1,0:T(8,128)S(1)} %get-tuple-element.118) | copy-start | bytes 98308
  22.7 49.5 %copy-start.17 = (bf16[128,1024]{1,0:T(8,128)(2,1)}, bf16[128,1024]{1,0:T(8,128)(2,1)S(1)}, u32[]{:S(2)}) copy-start(bf16[128,1024]{1,0:T(8,128)(2,1)S(1)} %all_gather.26) | copy-start | bytes 786436
  78.7 2.2 copy-start.3
  78.7 51.5 %copy-start.13 = (bf16[1,128,8,1024]{3,2,1,0:T(8,128)(2,1)S(1)}, bf16[1,128,8,1024]{3,2,1,0:T(8,128)(2,1)}, u32[]{:S(2)}) copy-start(bf16[1,128,8,1024]{3,2,1,0:T(8,128)(2,1)} %param.27) | copy-start | bytes 6291460
  78.8 63.1 %copy-start.31 = (f32[128,8]{0,1:T(8,128)}, f32[128,8]{0,1:T(8,128)S(1)}, u32[]{:S(2)}) copy-start(f32[128,8]{0,1:T(8,128)S(1)} %add_rsqrt_fusion.1) | copy-start | bytes 12292
  229.1 3.3 copy-start.9
  264.3 90.7 %copy-start.19 = (bf16[128,8,1024]{2,0,1:T(8,128)(2,1)}, bf16[128,8,1024]{2,0,1:T(8,128)(2,1)S(1)}, u32[]{:S(2)}) copy-start(bf16[128,8,1024]{2,0,1:T(8,128)(2,1)S(1)} %multiply_convert_fusion.4) | copy-start | bytes 6291460
  376.0 10.0 copy-start.36
  376.0 10.0 copy-start.38
  386.1 6.2 copy-start.1
  392.2 3.6 copy-start.7
  392.3 3.6 copy-start.14
  395.9 8.4 copy-start.21
  429.9 7.7 copy-start.10
  437.6 5.6 copy-start.6
  473.7 2.9 copy-start.16
  476.6 3.5 copy-start.4
  476.6 3.5 copy-start.23
  476.6 3.5 copy-start.32
  477.3 14.8 %copy-start.11 = (bf16[128,8,3,16,64]{0,4,3,2,1:T(8,128)(2,1)}, bf16[128,8,3,16,64]{0,4,3,2,1:T(8,128)(2,1)S(1)}, u32[]{:S(2)}) copy-start(bf16[128,8,3,16,64]{0,4,3,2,1:T(8,128)(2,1)S(1)} %maximum_convert_fusion) | copy-start | bytes 18874372
  492.1 11.3 copy-start.2
  492.1 11.3 copy-start.8
  492.1 11.3 copy-start.15
  503.5 13.0 copy-start.12
  518.0 130.9 %all-reduce.6.cloned.1.call-start = ((), (), s32[]{:S(2)}) async-start(), calls=%async_computation.20 | async-start | bytes 131072 | tf_op jit(solution)/shard_map/psum | solution.py:190
  530.5 165.9 %reduce-scatter.14.cloned.1.call-start = ((), (), s32[]{:S(2)}) async-start(), calls=%async_computation.10 | async-start | bytes 4456448 | tf_op jit(solution)/shard_map/reduce_scatter | solution.py:181
  537.4 302.4 %reduce-scatter.22.cloned.1.call-start = ((), (), s32[]{:S(2)}) async-start(), calls=%async_computation.19 | async-start | bytes 4325376
  546.5 420.7 %reduce-scatter.20.cloned.1.call-start = ((), (), s32[]{:S(2)}) async-start(), calls=%async_computation.13 | async-start | bytes 12255232 | tf_op jit(solution)/shard_map/reduce_scatter | solution.py:184
  558.4 539.4 %reduce-scatter.16.cloned.1.call-start = ((), (), s32[]{:S(2)}) async-start(), calls=%async_computation.11 | async-start | bytes 12255232 | tf_op jit(solution)/shard_map/reduce_scatter | solution.py:182
  571.1 658.0 %reduce-scatter.18.cloned.1.call-start = ((), (), s32[]{:S(2)}) async-start(), calls=%async_computation.12 | async-start | bytes 12255232 | tf_op jit(solution)/shard_map/reduce_scatter | solution.py:183
  584.3 783.8 %reduce-scatter.12.cloned.1.call-start = ((), (), s32[]{:S(2)}) async-start(), calls=%async_computation.9 | async-start | bytes 13369344 | tf_op jit(solution)/shard_map/reduce_scatter | solution.py:180
  638.3 4.5 collective-permute-start.1
  (7 other events, 8.3 us)
Sparse Core Ops, SparseCore 0:
  10.9 59.1 all-gather.11
  72.4 57.8 all-gather.21
  132.6 60.4 all-gather.13
  195.1 39.9 all-gather.15
  237.3 57.7 all-gather.19
  297.2 57.6 all-gather.17
  518.2 10.2 reduce-scatter.9
  533.0 84.6 all-reduce.5
  622.2 74.1 reduce-scatter.13
  699.2 140.5 reduce-scatter.21
  844.9 122.2 reduce-scatter.19
  971.7 126.0 reduce-scatter.15
  1103.0 126.0 reduce-scatter.17
  1233.6 134.5 reduce-scatter.11
where the time goes:
time: 1380 us
  waiting for transfers between devices  943 us (68%)
  matrix products  211 us (15%)
  local copies, waits for them, and re-layouts  134 us (10%)
  other arithmetic  65.2 us (5%)
  between operations  14.7 us (1%)
    unnamed x15, waiting for transfers between devices  147 us
    reduce_scatter x1, waiting for transfers between devices, body(): lax.psum_scatter(grad_qkv_w, 'frames', scatter_dimension=0, tiled=True)  139 us
    reduce_scatter x1, waiting for transfers between devices, body(): lax.psum_scatter(grad_up_w, 'frames', scatter_dimension=0, tiled=True)  131 us
    reduce_scatter x1, waiting for transfers between devices, body(): lax.psum_scatter(grad_gate_w, 'frames', scatter_dimension=0, tiled=True)  131 us
    reduce_scatter x1, waiting for transfers between devices, body(): lax.psum_scatter(grad_down, 'frames', scatter_dimension=0, tiled=True)  127 us
    dot_general x6, matrix products, flat_dot(): return jnp.dot(left, right, preferred_element_type=jnp.float32)  65.6 us
    dot_general x6, matrix products, trans_dot(): lax.dot_general(left, right, (((0,), (0,)), ((), ())), preferred_element_...  60.5 us
    all_gather x1, waiting for transfers between devices, body(): lax.all_gather(qkv_weight[0], 'frames', axis=0, tiled=True)  51.2 us
  transfers between devices with their start and end apart: 16, of which 11 were waited for; matrix products, arithmetic and copies ran while one was open for 17% of the time, Pallas kernels for 0%

commit v1 on v0

--- a/solution.py
+++ b/solution.py
@@ -1,6 +1,8 @@
 import jax
 import jax.numpy as jnp
 from jax import lax
+from jax.experimental import pallas as pl
+from jax.experimental.pallas import tpu as pltpu
 from jax.sharding import PartitionSpec as P
 
 HEADS = 16
@@ -54,6 +56,729 @@
     valid_rows = jnp.stack([jnp.ones_like(keep_one), keep_one, keep_two]).astype(jnp.float32)
     chosen = (delay[None, :] == jnp.arange(3, dtype=jnp.int32)[:, None]).astype(jnp.float32)
     return (chosen, valid_rows)
+
+
+MESH = pl.DeviceIdType.MESH
+CHUNKS = 17
+FEED = 11
+WIDE = 768
+ROUNDS = 4
+
+
+def mm(a, b):
+    return jnp.dot(a, b, preferred_element_type=jnp.float32)
+
+
+def nt(a, b):
+    return lax.dot_general(a, b, (((1,), (1,)), ((), ())), preferred_element_type=jnp.float32)
+
+
+def tn(a, b):
+    return lax.dot_general(a, b, (((0,), (0,)), ((), ())), preferred_element_type=jnp.float32)
+
+
+def either(cond, fn):
+    if isinstance(cond, bool):
+        if cond:
+            fn()
+    else:
+        pl.when(cond)(fn)
+
+
+def within(t, low, high):
+    if isinstance(t, int):
+        return low <= t < high
+    return jnp.logical_and(t >= low, t < high)
+
+
+def layer_kernel(
+    tok,
+    ctx,
+    gains,
+    cot,
+    w_own,
+    mixed_hbm,
+    gin_hbm,
+    dctx,
+    gain_out,
+    dw_hbm,
+    gathered,
+    lin,
+    n1,
+    n1t,
+    qkv,
+    mixed,
+    mixt,
+    aft,
+    n2,
+    n2t,
+    oacc,
+    gn,
+    wbuf,
+    part,
+    gg,
+    hidt,
+    shift,
+    bias,
+    gacc,
+    gsend,
+    grecv,
+    xsend,
+    xrecv,
+    r_c,
+    r_y,
+    r_zl,
+    r_zh,
+    t_keep,
+    t_send,
+    u_keep,
+    u_send,
+    v_keep,
+    v_send,
+    fin,
+    ag_ss,
+    ag_rs,
+    rs_ss,
+    rs_rs,
+    x_ss,
+    x_rs,
+    g_ss,
+    g_rs,
+    own_sem,
+    load_sem,
+    fin_sem,
+    out_sem,
+):
+    s = lax.axis_index("stream")
+    f = lax.axis_index("frames")
+    c = f % 2
+    y = (f // 2) % 2
+    zl = (f // 4) % 2
+    zh = f // 8
+    d_c = (s, f + 1 - 2 * c)
+    d_y = (s, f + 2 - 4 * y)
+    d_zl = (s, f + 4 - 8 * zl)
+    d_zh = (s, f + 8 - 16 * zh)
+    d_x = (1 - s, f)
+    partners = (d_zh, d_zl, d_y, d_c)
+
+    own_copy = pltpu.make_async_copy(w_own, gathered.at[:, zh, zl, y, c], own_sem)
+    own_copy.start()
+
+    barrier = pltpu.get_barrier_semaphore()
+    for device in partners + (d_x,):
+        pl.semaphore_signal(barrier, inc=1, device_id=device, device_id_type=MESH)
+    pl.semaphore_wait(barrier, 5)
+
+    def remote(src, dst, ss, rs, device):
+        return pltpu.make_async_remote_copy(
+            src_ref=src, dst_ref=dst, send_sem=ss, recv_sem=rs, device_id=device, device_id_type=MESH
+        )
+
+    def ag_copy(stage, k):
+        if stage == 0:
+            src = dst = gathered.at[k, zh, zl, y, c]
+        elif stage == 1:
+            src = dst = gathered.at[k, :, zl, y, c]
+        elif stage == 2:
+            src = dst = gathered.at[k, :, :, y, c]
+        else:
+            src = dst = gathered.at[k, :, :, :, c]
+        return remote(src, dst, ag_ss.at[stage, k], ag_rs.at[stage, k], partners[stage])
+
+    def ag_tick(t):
+        for stage in range(4):
+            def step(stage=stage):
+                k = t - stage
+                if stage > 0:
+                    ag_copy(stage - 1, k).wait_recv()
+                ag_copy(stage, k).start()
+            either(within(t, stage, stage + CHUNKS), step)
+        def ready():
+            ag_copy(3, t - 4).wait_recv()
+        either(within(t, 4, 4 + CHUNKS), ready)
+
+    def load(k, slot):
+        cp = pltpu.make_async_copy(gathered.at[k], wbuf.at[slot], load_sem.at[slot])
+        cp.start()
+        cp.wait()
+
+    def rs_copy(stage, r):
+        two, four = r % 2, r % ROUNDS
+        if stage == 0:
+            src, dst = part.at[two, :, :, :, 1 - c], r_c.at[four]
+        elif stage == 1:
+            src, dst = t_send.at[two], r_y.at[four]
+        elif stage == 2:
+            src, dst = u_send.at[two], r_zl.at[four]
+        else:
+            src, dst = v_send.at[two], r_zh.at[four]
+        return remote(src, dst, rs_ss.at[stage, two], rs_rs.at[stage, four], partners[3 - stage])
+
+    def add(a, b):
+        return a.astype(jnp.float32) + b.astype(jnp.float32)
+
+    def fin_copy(r):
+        return pltpu.make_async_copy(fin.at[r % 2], dw_hbm.at[r], fin_sem.at[r % 2])
+
+    def rs_tick(r, static_first=False):
+        def start_c():
+            rs_copy(0, r).start()
+        either(within(r, 0, CHUNKS), start_c)
+
+        def stage_y():
+            k = r - 1
+            rs_copy(0, k).wait_recv()
+            either(within(k, 2, CHUNKS), lambda: rs_copy(1, k - 2).wait_send())
+            two, four = k % 2, k % ROUNDS
+            def piece(i, _):
+                a, b = i // 2, i % 2
+                t_send[two, i] = add(part[two, a, b, 1 - y, c], r_c[four, a, b, 1 - y]).astype(jnp.bfloat16)
+                t_keep[two, i] = add(part[two, a, b, y, c], r_c[four, a, b, y]).astype(jnp.bfloat16)
+                return 0
+            lax.fori_loop(0, 4, piece, 0)
+            rs_copy(1, k).start()
+        either(within(r, 1, CHUNKS + 1), stage_y)
+
+        def stage_zl():
+            k = r - 2
+            rs_copy(1, k).wait_recv()
+            either(within(k, 2, CHUNKS), lambda: rs_copy(2, k - 2).wait_send())
+            two, four = k % 2, k % ROUNDS
+            for a in range(2):
+                far, near = a * 2 + 1 - zl, a * 2 + zl
+                u_send[two, a] = add(t_keep[two, far], r_y[four, far]).astype(jnp.bfloat16)
+                u_keep[two, a] = add(t_keep[two, near], r_y[four, near]).astype(jnp.bfloat16)
+            rs_copy(2, k).start()
+        either(within(r, 2, CHUNKS + 2), stage_zl)
+
+        def stage_zh():
+            k = r - 3
+            rs_copy(2, k).wait_recv()
+            either(within(k, 2, CHUNKS), lambda: rs_copy(3, k - 2).wait_send())
+            two, four = k % 2, k % ROUNDS
+            v_send[two] = add(u_keep[two, 1 - zh], r_zl[four, 1 - zh]).astype(jnp.bfloat16)
+            v_keep[two] = add(u_keep[two, zh], r_zl[four, zh]).astype(jnp.bfloat16)
+            rs_copy(3, k).start()
+        either(within(r, 3, CHUNKS + 3), stage_zh)
+
+        def last():
+            k = r - 4
+            rs_copy(3, k).wait_recv()
+            either(within(k, 2, CHUNKS), lambda: fin_copy(k - 2).wait())
+            fin[k % 2] = add(v_keep[k % 2], r_zh[k % ROUNDS])
+            fin_copy(k).start()
+        either(within(r, 4, CHUNKS + 4), last)
+
+    def part_free(r):
+        either(within(r, 2, CHUNKS), lambda: rs_copy(0, r - 2).wait_send())
+
+    row_id = lax.broadcasted_iota(jnp.int32, (128, 256), 0)
+    col_id = lax.broadcasted_iota(jnp.int32, (128, 256), 1) % 128
+    seen = jnp.logical_and(row_id // 8 == col_id // 8, col_id <= row_id)
+    bias[...] = jnp.where(seen, 0.0, -1e30)
+
+    def zero_gain(i, _):
+        gacc[...] = jnp.zeros_like(gacc)
+        return 0
+    lax.fori_loop(0, 1, zero_gain, 0)
+
+    ag_tick_first(ag_tick, own_copy)
+
+    load(0, 0)
+    half = shift.shape[1] // 2
+    for h in range(2):
+        w_half = wbuf[0, :, :, :, :, h * 32 : h * 32 + 32, 0:512].reshape(512, 512)
+        shift[:, h * half : (h + 1) * half] = mm(ctx[...], w_half)
+    xsend[0] = shift[...].astype(jnp.bfloat16)
+
+    def x_copy(i):
+        return remote(xsend.at[i], xrecv.at[i], x_ss.at[i], x_rs.at[i], d_x)
+
+    x_copy(0).start()
+    ag_tick(5)
+    x_copy(0).wait_recv()
+    shift[...] = shift[...] + xrecv[0].astype(jnp.float32)
+
+    def rows_of(i, size):
+        return pl.ds(pl.multiple_of(i * size, size), size)
+
+    def norm1(i, _):
+        rows = rows_of(i, 128)
+        sh = shift[rows_of(i, 16), :]
+        x = tok[rows, :].astype(jnp.float32).reshape(16, 8, 1024) + sh[:, None, :]
+        r = lax.rsqrt(jnp.mean(x * x, axis=-1, keepdims=True) + epsilon)
+        n = (x * r * gains[0][None]).reshape(128, 1024).astype(jnp.bfloat16)
+        lin[rows, :] = x.reshape(128, 1024)
+        n1[rows, :] = n
+        n1t[:, rows] = n.T
+        return 0
+
+    lax.fori_loop(0, 8, norm1, 0)
+
+    lane_low = lax.broadcasted_iota(jnp.int32, (128, 128), 1) < 64
+    head_scale = HEAD ** (-0.5)
+
+    def both(v):
+        zero = jnp.zeros_like(v)
+        return jnp.concatenate([jnp.where(lane_low, v, zero), jnp.where(lane_low, zero, v)], axis=0)
+
+    def softmax(sc):
+        parts = []
+        for h in range(2):
+            p = sc[:, h * 128 : h * 128 + 128]
+            e = jnp.exp(p - jnp.max(p, axis=-1, keepdims=True))
+            parts.append(e / jnp.sum(e, axis=-1, keepdims=True))
+        return parts
+
+    def attn_fwd(g):
+        def rows_step(i, _):
+            rows = rows_of(i, 256)
+            for u in range(2):
+                sub = rows_of(i * 2 + u, 128)
+                for p in range(2):
+                    lo = p * 128
+                    q = qkv[g, sub, lo : lo + 128]
+                    k = qkv[g, sub, 256 + lo : 384 + lo]
+                    v = qkv[g, sub, 512 + lo : 640 + lo]
+                    sc = nt(q, both(k)) * head_scale + bias[...]
+                    pr = jnp.concatenate([x.astype(jnp.bfloat16) for x in softmax(sc)], axis=1)
+                    out = mm(pr, both(v)).astype(jnp.bfloat16)
+                    mixed[sub, pl.ds(pl.multiple_of(g * 256 + lo, 128), 128)] = out
+            return 0
+        lax.fori_loop(0, 4, rows_step, 0)
+
+    def attn_bwd(g):
+        def rows_step(i, _):
+            for u in range(2):
+                sub = rows_of(i * 2 + u, 128)
+                for p in range(2):
+                    lo = p * 128
+                    q = qkv[g, sub, lo : lo + 128]
+                    k = qkv[g, sub, 256 + lo : 384 + lo]
+                    v = qkv[g, sub, 512 + lo : 640 + lo]
+                    do = mixed[sub, pl.ds(pl.multiple_of(g * 256 + lo, 128), 128)]
+                    kk = both(k)
+                    sc = nt(q, kk) * head_scale + bias[...]
+                    pr = softmax(sc)
+                    dp = nt(do, both(v))
+                    ds = []
+                    for h in range(2):
+                        d = dp[:, h * 128 : h * 128 + 128]
+                        ds.append((pr[h] * (d - jnp.sum(d * pr[h], axis=-1, keepdims=True))).astype(jnp.bfloat16))
+                    ds = jnp.concatenate(ds, axis=1)
+                    pl_low = jnp.concatenate([x.astype(jnp.bfloat16) for x in pr], axis=1)
+                    dq = mm(ds, kk) * head_scale
+                    dk = tn(ds, q)
+                    dv = tn(pl_low, do)
+                    qkv[g, sub, lo : lo + 128] = dq.astype(jnp.bfloat16)
+                    qkv[g, sub, 256 + lo : 384 + lo] = (
+                        jnp.where(lane_low, dk[:128], dk[128:]) * head_scale
+                    ).astype(jnp.bfloat16)
+                    qkv[g, sub, 512 + lo : 640 + lo] = jnp.where(lane_low, dv[:128], dv[128:]).astype(jnp.bfloat16)
+            return 0
+        lax.fori_loop(0, 4, rows_step, 0)
+
+    def qkv_group(g, _):
+        either(g > 0, lambda: ag_tick(5 + g))
+        load(1 + g, 0)
+        def rows_step(i, _):
+            rows = rows_of(i, 256)
+            qkv[g, rows, :] = mm(n1[rows, :], wbuf[0].reshape(1024, WIDE)).astype(jnp.bfloat16)
+            return 0
+        lax.fori_loop(0, 4, rows_step, 0)
+        attn_fwd(g)
+        return 0
+
+    lax.fori_loop(0, 4, qkv_group, 0)
+
+    ag_tick(9)
+    load(5, 0)
+    load(0, 1)
+
+    def after(i, _):
+        rows = rows_of(i, 256)
+        m = mixed[rows, :]
+        a = lin[rows, 0:WIDE] + mm(m, wbuf[0].reshape(1024, WIDE))
+        b = lin[rows, WIDE:1024] + mm(m, wbuf[1, :, :, :, :, :, 512:768].reshape(1024, 256))
+        x = jnp.concatenate([a, b], axis=1)
+        aft[rows, :] = x
+        oacc[rows, :] = x
+        x3 = x.reshape(32, 8, 1024)
+        r = lax.rsqrt(jnp.mean(x3 * x3, axis=-1, keepdims=True) + epsilon)
+        n = (x3 * r * gains[1][None]).reshape(256, 1024).astype(jnp.bfloat16)
+        n2[rows, :] = n
+        n2t[:, rows] = n.T
+        mixt[:, rows] = m.T
+        return 0
+
+    lax.fori_loop(0, 4, after, 0)
+
+    def feed(j, _):
+        ag_tick(10 + j)
+        load(6 + j, 0)
+        part_free(j)
+        two = j % 2
+
+        def rows_step(i, _):
+            rows = rows_of(i, 256)
+            w_gu = wbuf[0, :, :, :, :, :, 0:512].reshape(1024, 512)
+            pre = mm(n2[rows, :], w_gu)
+            gate, up = pre[:, :256], pre[:, 256:]
+            g_hid = jnp.zeros((256, 256), jnp.float32)
+            for q in range(4):
+                w_q = wbuf[0, :, :, :, :, q * 16 : q * 16 + 16, 512:768].reshape(256, 256)
+                g_hid = g_hid + nt(cot[rows, q * 256 : q * 256 + 256], w_q)
+            sig = jax.nn.sigmoid(gate)
+            silu = gate * sig
+            hid = (silu * up).astype(jnp.bfloat16)
+            g_gate = (g_hid * up * sig * (1.0 + gate * (1.0 - sig))).astype(jnp.bfloat16)
+            g_up = (g_hid * silu).astype(jnp.bfloat16)
+            for q in range(4):
+                w_q = wbuf[0, :, :, :, :, q * 16 : q * 16 + 16, 512:768].reshape(256, 256)
+                oacc[rows, q * 256 : q * 256 + 256] += mm(hid, w_q)
+            both_g = jnp.concatenate([g_gate, g_up], axis=1)
+            gg[rows, :] = both_g
+            hidt[:, rows] = hid.T
+            back = nt(both_g, w_gu)
+            @pl.when(j == 0)
+            def _():
+                gn[rows, :] = back
+            @pl.when(j > 0)
+            def _():
+                gn[rows, :] += back
+            return 0
+
+        lax.fori_loop(0, 4, rows_step, 0)
+
+        def weight_step(m, _):
+            res = mm(n2t[rows_of(m, 256), :], gg[...]).astype(jnp.bfloat16).reshape(2, 2, 64, 512)
+            part[two, m // 2, m % 2, :, :, :, 0:512] = res
+            return 0
+
+        lax.fori_loop(0, 4, weight_step, 0)
+        for q in range(4):
+            res = mm(hidt[...], cot[:, q * 256 : q * 256 + 256]).astype(jnp.bfloat16)
+            part[two, :, :, :, :, q * 16 : q * 16 + 16, 512:768] = res.reshape(2, 2, 2, 2, 16, 256)
+        rs_tick(j)
+        return 0
+
+    lax.fori_loop(0, FEED, feed, 0)
+
+    def norm2_back(i, _):
+        rows = rows_of(i, 128)
+        n1[rows, :] = oacc[rows, :].astype(jnp.bfloat16)
+        x = aft[rows, :].reshape(16, 8, 1024)
+        g = gn[rows, :].reshape(16, 8, 1024)
+        r = lax.rsqrt(jnp.mean(x * x, axis=-1, keepdims=True) + epsilon)
+        unit = x * r
+        gacc[8:16, :] += jnp.sum(g * unit, axis=0)
+        gu = g * gains[1][None]
+        back = r * (gu - unit * jnp.mean(gu * unit, axis=-1, keepdims=True))
+        total = cot[rows, :].astype(jnp.float32) + back.reshape(128, 1024)
+        oacc[rows, :] = total
+        n2[rows, :] = total.astype(jnp.bfloat16)
+        return 0
+
+    lax.fori_loop(0, 8, norm2_back, 0)
+    mixed_copy = pltpu.make_async_copy(n1, mixed_hbm, out_sem.at[0])
+    mixed_copy.start()
+
+    load(5, 0)
+    load(0, 1)
+    part_free(11)
+
+    def out_weight_step(m, _):
+        res = mm(mixt[rows_of(m, 256), :], n2[:, 0:WIDE]).astype(jnp.bfloat16)
+        part[1, m // 2, m % 2] = res.reshape(2, 2, 64, WIDE)
+        return 0
+
+    lax.fori_loop(0, 4, out_weight_step, 0)
+    rs_tick(11)
+
+    def mixed_back(i, _):
+        rows = rows_of(i, 256)
+        g = n2[rows, :]
+        res = nt(g[:, 0:WIDE], wbuf[0].reshape(1024, WIDE)) + nt(
+            g[:, WIDE:1024], wbuf[1, :, :, :, :, :, 512:768].reshape(1024, 256)
+        )
+        mixed[rows, :] = res.astype(jnp.bfloat16)
+        return 0
+
+    lax.fori_loop(0, 4, mixed_back, 0)
+
+    def qkv_back(g, _):
+        load(1 + g, 0)
+        attn_bwd(g)
+        part_free(12 + g)
+        two = g % 2
+
+        def weight_step(m, _):
+            res = mm(n1t[rows_of(m, 256), :], qkv[g]).astype(jnp.bfloat16)
+            part[two, m // 2, m % 2] = res.reshape(2, 2, 64, WIDE)
+            return 0
+
+        lax.fori_loop(0, 4, weight_step, 0)
+        rs_tick(12 + g)
+
+        def rows_step(i, _):
+            rows = rows_of(i, 256)
+            back = nt(qkv[g, rows, :], wbuf[0].reshape(1024, WIDE))
+            @pl.when(g == 0)
+            def _():
+                gn[rows, :] = back
+            @pl.when(g > 0)
+            def _():
+                gn[rows, :] += back
+            return 0
+
+        lax.fori_loop(0, 4, rows_step, 0)
+        return 0
+
+    lax.fori_loop(0, 4, qkv_back, 0)
+
+    def norm1_back(i, _):
+        rows = rows_of(i, 128)
+        x = lin[rows, :].reshape(16, 8, 1024)
+        g = gn[rows, :].reshape(16, 8, 1024)
+        r = lax.rsqrt(jnp.mean(x * x, axis=-1, keepdims=True) + epsilon)
+        unit = x * r
+        gacc[0:8, :] += jnp.sum(g * unit, axis=0)
+        gu = g * gains[0][None]
+        back = r * (gu - unit * jnp.mean(gu * unit, axis=-1, keepdims=True))
+        total = oacc[rows, :].reshape(16, 8, 1024) + back
+        oacc[rows, :] = total.reshape(128, 1024)
+        shift[rows_of(i, 16), :] = jnp.sum(total, axis=1)
+        return 0
+
+    lax.fori_loop(0, 8, norm1_back, 0)
+    gin_copy = pltpu.make_async_copy(oacc, gin_hbm, out_sem.at[1])
+    gin_copy.start()
+
+    xsend[1] = shift[...].astype(jnp.bfloat16)
+    x_copy(1).start()
+
+    def gain_copy(i):
+        return remote(gsend.at[i], grecv.at[i], g_ss.at[i], g_rs.at[i], partners[i])
+
+    gsend[0] = gacc[...]
+    gain_copy(0).start()
+
+    load(0, 1)
+    part_free(16)
+
+    def out_tail_step(m, _):
+        res = mm(mixt[rows_of(m, 256), :], n2[:, WIDE:1024]).astype(jnp.bfloat16)
+        part[0, m // 2, m % 2, :, :, :, 512:768] = res.reshape(2, 2, 64, 256)
+        return 0
+
+    lax.fori_loop(0, 4, out_tail_step, 0)
+
+    x_copy(1).wait_recv()
+    g_low = (shift[...] + xrecv[1].astype(jnp.float32)).astype(jnp.bfloat16)
+    ctx_t = ctx[...].T
+    for h in range(2):
+        gh = g_low[:, h * 512 : (h + 1) * 512]
+        res = mm(ctx_t, gh).astype(jnp.bfloat16).reshape(2, 2, 2, 2, 32, 512)
+        part[0, :, :, :, :, h * 32 : h * 32 + 32, 0:512] = res
+    rs_tick(16)
+    w0 = wbuf[1, :, :, :, :, 0:32, 0:512].reshape(512, 512)
+    w1 = wbuf[1, :, :, :, :, 32:64, 0:512].reshape(512, 512)
+    dctx[...] = nt(g_low[:, :512], w0) + nt(g_low[:, 512:], w1)
+
+    for i in range(4):
+        gain_copy(i).wait_recv()
+        if i < 3:
+            gsend[i + 1] = gsend[i] + grecv[i]
+            gain_copy(i + 1).start()
+        else:
+            gain_out[...] = gsend[i] + grecv[i]
+        rs_tick(17 + i)
+
+    for i in range(4):
+        gain_copy(i).wait_send()
+    for i in range(2):
+        x_copy(i).wait_send()
+
+    for stage in range(4):
+        for k in (CHUNKS - 2, CHUNKS - 1):
+            rs_copy(stage, k).wait_send()
+
+    def drain(k, _):
+        for stage in range(4):
+            ag_copy(stage, k).wait_send()
+        return 0
+
+    lax.fori_loop(0, CHUNKS, drain, 0)
+    fin_copy(CHUNKS - 2).wait()
+    fin_copy(CHUNKS - 1).wait()
+    mixed_copy.wait()
+    gin_copy.wait()
+
+
+def ag_tick_first(ag_tick, own_copy):
+    own_copy.wait()
+
+    def step(t, _):
+        ag_tick(t)
+        return 0
+
+    lax.fori_loop(0, 5, step, 0)
+
+
+def call_layer(tok, ctx, gains, cot, w_own):
+    f32, bf16 = jnp.float32, jnp.bfloat16
+    vm, dma = pltpu.VMEM, pltpu.SemaphoreType.DMA
+    shape = jax.ShapeDtypeStruct
+    return pl.pallas_call(
+        layer_kernel,
+        name="layer",
+        out_shape=(
+            shape((1024, 1024), bf16),
+            shape((1024, 1024), f32),
+            shape((128, 512), f32),
+            shape((16, 1024), f32),
+            shape((CHUNKS, 64, WIDE), f32),
+            shape((CHUNKS, 2, 2, 2, 2, 64, WIDE), bf16),
+        ),
+        in_specs=[pl.BlockSpec(memory_space=pltpu.VMEM)] * 4 + [pl.BlockSpec(memory_space=pltpu.HBM)],
+        out_specs=(
+            pl.BlockSpec(memory_space=pltpu.HBM),
+            pl.BlockSpec(memory_space=pltpu.HBM),
+            pl.BlockSpec(memory_space=pltpu.VMEM),
+            pl.BlockSpec(memory_space=pltpu.VMEM),
+            pl.BlockSpec(memory_space=pltpu.HBM),
+            pl.BlockSpec(memory_space=pltpu.HBM),
+        ),
+        scratch_shapes=[
+            vm((1024, 1024), f32),
+            vm((1024, 1024), bf16),
+            vm((1024, 1024), bf16),
+            vm((4, 1024, WIDE), bf16),
+            vm((1024, 1024), bf16),
+            vm((1024, 1024), bf16),
+            vm((1024, 1024), f32),
+            vm((1024, 1024), bf16),
+            vm((1024, 1024), bf16),
+            vm((1024, 1024), f32),
+            vm((1024, 1024), f32),
+            vm((2, 2, 2, 2, 2, 64, WIDE), bf16),
+            vm((2, 2, 2, 2, 2, 64, WIDE), bf16),
+            vm((1024, 512), bf16),
+            vm((256, 1024), bf16),
+            vm((128, 1024), f32),
+            vm((128, 256), f32),
+            vm((16, 1024), f32),
+            vm((4, 16, 1024), f32),
+            vm((4, 16, 1024), f32),
+            vm((2, 128, 1024), bf16),
+            vm((2, 128, 1024), bf16),
+            vm((ROUNDS, 2, 2, 2, 64, WIDE), bf16),
+            vm((ROUNDS, 4, 64, WIDE), bf16),
+            vm((ROUNDS, 2, 64, WIDE), bf16),
+            vm((ROUNDS, 64, WIDE), bf16),
+            vm((2, 4, 64, WIDE), bf16),
+            vm((2, 4, 64, WIDE), bf16),
+            vm((2, 2, 64, WIDE), bf16),
+            vm((2, 2, 64, WIDE), bf16),
+            vm((2, 64, WIDE), bf16),
+            vm((2, 64, WIDE), bf16),
+            vm((2, 64, WIDE), f32),
+            dma((4, CHUNKS)),
+            dma((4, CHUNKS)),
+            dma((4, 2)),
+            dma((4, ROUNDS)),
+            dma((2,)),
+            dma((2,)),
+            dma((4,)),
+            dma((4,)),
+            dma,
+            dma((2,)),
+            dma((2,)),
+            dma((2,)),
+        ],
+        compiler_params=pltpu.CompilerParams(
+            collective_id=0, has_side_effects=True, vmem_limit_bytes=63 * 1024 * 1024
+        ),
+    )(tok, ctx, gains, cot, w_own)
+
+
+def pack_weights(ctx_weight, qkv_weight, out_weight, gate_weight, up_weight, down_weight):
+    qkv = qkv_weight.reshape(64, 3, 4, 256).transpose(2, 0, 1, 3).reshape(4, 64, WIDE)
+    gate = gate_weight.reshape(64, 16, FEED, 16).transpose(2, 0, 1, 3).reshape(FEED, 64, 256)
+    up = up_weight.reshape(64, 16, FEED, 16).transpose(2, 0, 1, 3).reshape(FEED, 64, 256)
+    down = down_weight.reshape(FEED, 16, 4, 256).transpose(0, 2, 1, 3).reshape(FEED, 64, 256)
+    feed = jnp.concatenate([gate, up, down], axis=-1)
+    ctx = ctx_weight.reshape(32, 2, 512).transpose(1, 0, 2).reshape(64, 512)
+    first = jnp.concatenate([ctx, out_weight[:, WIDE:]], axis=-1)
+    return jnp.concatenate([first[None], qkv, out_weight[None, :, :WIDE], feed], axis=0)
+
+
+def unpack_grads(dw):
+    feed = dw[:FEED]
+    gate = feed[:, :, 0:256].reshape(FEED, 64, 16, 16).transpose(1, 2, 0, 3).reshape(64, 2816)
+    up = feed[:, :, 256:512].reshape(FEED, 64, 16, 16).transpose(1, 2, 0, 3).reshape(64, 2816)
+    down = feed[:, :, 512:768].reshape(FEED, 4, 16, 256).transpose(0, 2, 1, 3).reshape(176, 1024)
+    out = jnp.concatenate([dw[11], dw[16][:, 512:]], axis=-1)
+    qkv = dw[12:16].reshape(4, 64, 3, 256).transpose(1, 2, 0, 3).reshape(64, 3072)
+    ctx = dw[16][:, :512].reshape(2, 32, 512).transpose(1, 0, 2).reshape(32, 1024)
+    return (qkv, out, gate, up, down, ctx)
+
+
+def body_kernel(
+    tokens,
+    context,
+    ctx_weight,
+    delay,
+    lengths,
+    attn_gain,
+    ffn_gain,
+    qkv_weight,
+    out_weight,
+    gate_weight,
+    up_weight,
+    down_weight,
+    cotangent,
+):
+    frame_count, positions, width = tokens.shape[1:]
+    inputs = tokens[0]
+    rim_rows = shifted(inputs[frame_count - 2 :], "frames", 1)
+    extended = jnp.concatenate([rim_rows, inputs], axis=0)
+    frame_ids = lax.axis_index("frames") * frame_count + jnp.arange(frame_count, dtype=jnp.int32)
+    chosen, valid_rows = shift_tables(delay, lengths, frame_ids)
+    tok = jnp.zeros((frame_count, positions, width), jnp.float32)
+    for offset in range(3):
+        piece = extended[2 - offset : 2 - offset + frame_count].astype(jnp.float32)
+        tok = tok + chosen[offset][None, :, None] * valid_rows[offset][:, None, None] * piece
+    tok = tok.astype(jnp.bfloat16).reshape(frame_count * positions, width)
+    gains = jnp.stack([attn_gain[0], ffn_gain[0]]).astype(jnp.float32)
+    w_own = pack_weights(
+        ctx_weight, qkv_weight[0], out_weight[0], gate_weight[0], up_weight[0], down_weight[0]
+    )
+    mixed_out, grad_in, d_context, gain_sums, dw, _ = call_layer(
+        tok, context, gains, cotangent[0].reshape(frame_count * positions, width), w_own
+    )
+    d_qkv, d_out, d_gate, d_up, d_down, d_ctx = unpack_grads(dw)
+    grad_in = grad_in.reshape(frame_count, positions, width)
+    grad_ext = jnp.zeros((frame_count + 2, positions, width), jnp.float32)
+    for offset in range(3):
+        term = chosen[offset][None, :, None] * valid_rows[offset][:, None, None] * grad_in
+        grad_ext = grad_ext + jnp.pad(term, ((2 - offset, offset), (0, 0), (0, 0)))
+    back_rows = shifted(grad_ext[:2].astype(jnp.bfloat16), "frames", -1).astype(jnp.float32)
+    grad_tokens = grad_ext[2:].at[frame_count - 2 :].add(back_rows)
+    return (
+        mixed_out.reshape(frame_count, positions, width)[None],
+        grad_tokens[None],
+        d_context,
+        d_ctx,
+        gain_sums[:8][None],
+        gain_sums[8:][None],
+        d_qkv[None],
+        d_out[None],
+        d_gate[None],
+        d_up[None],
+        d_down[None],
+    )
 
 
 def body(
@@ -125,14 +850,7 @@
     up_pre = flat_dot(normed_two, w_up)
     hidden = (jax.nn.silu(gate_pre) * up_pre).astype(jnp.bfloat16)
     out_full = after_attn + flat_dot(hidden, w_down).reshape(frame_count, positions, model_width)
-    back_weights = (
-        lax.all_gather(qkv_weight[0], "frames", axis=0, tiled=True),
-        lax.all_gather(out_weight[0], "frames", axis=0, tiled=True),
-        lax.all_gather(gate_weight[0], "frames", axis=0, tiled=True),
-        lax.all_gather(up_weight[0], "frames", axis=0, tiled=True),
-        lax.all_gather(down_weight[0], "frames", axis=0, tiled=True),
-    )
-    b_qkv, b_out, b_gate, b_up, b_down = back_weights
+    b_qkv, b_out, b_gate, b_up, b_down = weights
     grad_out = cotangent[0].astype(jnp.float32)
     grad_ff = grad_out.reshape(token_rows, model_width).astype(jnp.bfloat16)
     grad_down = trans_dot(hidden, grad_ff)
@@ -217,8 +935,9 @@
 
 
 def solution(mesh):
+    fits = mesh.shape["frames"] == 16 and mesh.shape["stream"] == 2
     return jax.shard_map(
-        body,
+        body_kernel if fits else body,
         mesh=mesh,
         in_specs=(
             P("stream", "frames", None, None),

time: 1380 us -> 479 us (0.35)
  waiting for transfers between devices: 943 us -> 0.01 us
  Pallas kernels: 0 us -> 418 us
  matrix products: 211 us -> 0 us
  local copies, waits for them, and re-layouts: 134 us -> 34.7 us
  other arithmetic: 65.2 us -> 18.2 us
    reduce_scatter x6 -> x0, waiting for transfers between devices: 576 us -> none  [the longest x1 139 us: body(): lax.psum_scatter(grad_qkv_w, 'frames', scatter_dimension=0, tiled=True)]
    pallas_call x0 -> x1, Pallas kernels: none -> 418 us  [call_layer(): pl.pallas_call(layer_kernel, name='layer', out_shape=(shape((1024, 1024),...]
    all_gather x6 -> x0, waiting for transfers between devices: 220 us -> none  [the longest x1 51.2 us: body(): lax.all_gather(qkv_weight[0], 'frames', axis=0, tiled=True)]
    dot_general x24 -> x0, matrix products: 211 us -> none  [the longest x6 65.6 us: flat_dot(): return jnp.dot(left, right, preferred_element_type=jnp.float32)]
    unnamed x15 -> x0, waiting for transfers between devices: 147 us -> none
    convert_element_type x4 -> x0, local copies, waits for them, and re-layouts: 45.9 us -> none  [the longest x2 34.8 us: body(): jnp.stack([grad_queries, grad_keys, grad_values], axis=2)]
    unnamed x84 -> x34, local copies, waits for them, and re-layouts: 31 us -> 7.87 us
    reduce_sum x3 -> x0, other arithmetic: 23.1 us -> none  [the longest x1 13 us: body(): grad_shift = jnp.sum(grad_in, axis=1).astype(jnp.bfloat16)]
  transfers between devices with their start and end apart: 16 -> 2, of which waited for: 11 -> 0; matrix products, arithmetic and copies ran while one was open for 17% -> 7% of each run, Pallas kernels for 0% -> 0%
where the time goes in v1:
time: 479 us; the launch traced here: 476 us
  Pallas kernels  418 us (87%)
  local copies, waits for them, and re-layouts  34.7 us (7%)
  other arithmetic  18.2 us (4%)
    pallas_call x1, Pallas kernels, call_layer(): pl.pallas_call(layer_kernel, name='layer', out_shape=(shape((1024, 1024),...  418 us
  transfers between devices with their start and end apart: 2, of which 0 were waited for; matrix products, arithmetic and copies ran while one was open for 7% of the time, Pallas kernels for 0%

profile of v1, /device:TPU:0, one launch (start us, length us, event | category | flops | bytes accessed | tf_op | source)
XLA Modules:
  0.0 476.3 jit_solution(17335019085390726251)
XLA Ops:
  0.7 1.4 slice_bitcast_fusion.6
  2.1 2.9 collective-permute-start
  5.0 0.8 reduce-window.9
  5.9 0.7 bitcast_subtract_fusion
  6.7 0.5 slice_bitcast_fusion.11
  7.2 0.7 fusion.4
  7.9 0.6 slice_bitcast_fusion.12
  8.5 1.4 slice.136
  9.9 1.5 copy.92
  11.3 1.2 reshape_squeeze.19
  12.6 0.8 copy.75
  13.4 1.3 reshape_squeeze.16
  14.9 1.2 reshape.276
  16.1 0.4 copy.71
  16.6 1.0 copy.76
  17.6 0.4 copy.73
  18.2 0.3 copy.77
  18.5 0.9 broadcast_multiply_fusion.2
  19.4 0.8 broadcast_multiply_fusion
  20.2 0.8 broadcast_multiply_fusion.1
  21.0 0.9 slice_bitcast_fusion.3
  22.0 2.5 maximum_maximum_fusion.w_own
  24.5 1.4 maximum_convert_fusion.gains
  25.9 3.4 fusion.1.tok
  29.3 418.1 %layer.1 = (bf16[1024,1024]{1,0:T(8,128)(2,1)}, f32[1024,1024]{1,0:T(8,128)}, f32[128,512]{1,0:T(8,128)}, f32[16,1024]{1,0:T(8,128)}, f32[17,64,768]{2,1,0:T(8,1...) custom-call(bf16[1024,1024]{1,0:T(8,128)(2,1)} %fusion.1.tok, bf16[128,512]{1,0:T(8,128)(2,1)} %ctx.1, ...), custom_call_target="tpu_custom_call" | custom-call | tf_op jit(solution)/shard_map/layer/pallas_call | solution.py:633
  447.5 1.2 slice_bitcast_fusion.1
  448.7 2.8 fusion.5
  451.6 1.0 bitcast_multiply_fusion.2
  452.6 1.9 pad_add_fusion
  454.6 2.5 slice_bitcast_fusion
  457.1 0.7 copy-done
  457.8 0.6 slice_bitcast_fusion.4
  458.4 1.3 collective-permute-start.1
  459.7 0.7 maximum_bitcast_fusion
  460.5 1.2 slice.128
  461.7 0.7 copy.88
  462.3 0.5 copy.84
  462.8 1.2 broadcast_in_dim_reshape.19
  464.0 0.4 reshape.283
  464.5 0.5 copy.79
  465.0 1.3 broadcast_in_dim_reshape.16
  466.3 0.4 copy.82
  466.8 1.3 copy.86
  468.1 1.5 copy.80
  469.7 1.3 copy.85
  471.0 1.5 fusion.3
  472.5 3.1 copy.96
  475.6 0.7 copy.97
  (43 shorter events, 1.0 us)
Async XLA Ops:
  0.6 15.4 %copy-start.9 = (bf16[1,64,2816]{2,1,0:T(8,128)(2,1)S(1)}, bf16[1,64,2816]{2,1,0:T(8,128)(2,1)}, u32[]{:S(2)}) copy-start(bf16[1,64,2816]{2,1,0:T(8,128)(2,1)} %param.24) | copy-start | bytes 1081348
  2.1 23.8 %collective-permute-start = (bf16[2,8,1024]{2,1,0:T(8,128)(2,1)}, bf16[2,8,1024]{2,1,0:T(8,128)(2,1)}, u32[]{:S(2)}, u32[]{:S(2)}) collective-permute-start(bf16[2,8,1024]{2,1,0:T(8,128)(2,1)} %slice_bitcast_fusion.6), channel_id=1, source_target_pairs={{0,1},{1,2},{2,3},{3,4},{4,5},{5,6},{6,7},{7,8},{8,9},{9,10},{10,1... | collective-permute-start | bytes 98312 | tf_op jit(solution)/shard_map/ppermute | solution.py:18
  12.6 5.0 %copy-start.10 = (bf16[1,64,2816]{2,1,0:T(8,128)(2,1)S(1)}, bf16[1,64,2816]{2,1,0:T(8,128)(2,1)}, u32[]{:S(2)}) copy-start(bf16[1,64,2816]{2,1,0:T(8,128)(2,1)} %param.25) | copy-start | bytes 1081348
  18.0 6.5 %copy-start.13 = (bf16[1,8,1024]{2,1,0:T(8,128)(2,1)S(1)}, bf16[1,8,1024]{2,1,0:T(8,128)(2,1)}, u32[]{:S(2)}) copy-start(bf16[1,8,1024]{2,1,0:T(8,128)(2,1)} %param.21) | copy-start | bytes 49156
  18.0 7.9 %copy-start.2 = (bf16[1,128,8,1024]{3,2,1,0:T(8,128)(2,1)S(1)}, bf16[1,128,8,1024]{3,2,1,0:T(8,128)(2,1)}, u32[]{:S(2)}) copy-start(bf16[1,128,8,1024]{3,2,1,0:T(8,128)(2,1)} %param.15) | copy-start | bytes 6291460
  19.4 9.9 %copy-start.3 = (f32[128,8]{1,0:T(8,128)}, f32[128,8]{1,0:T(8,128)S(1)}, u32[]{:S(2)}) copy-start(f32[128,8]{1,0:T(8,128)S(1)} %broadcast_multiply_fusion.2) | copy-start | bytes 12292
  20.2 9.1 %copy-start.5 = (f32[128,8]{1,0:T(8,128)}, f32[128,8]{1,0:T(8,128)S(1)}, u32[]{:S(2)}) copy-start(f32[128,8]{1,0:T(8,128)S(1)} %broadcast_multiply_fusion) | copy-start | bytes 12292
  21.0 8.3 %copy-start.7 = (f32[128,8]{1,0:T(8,128)}, f32[128,8]{1,0:T(8,128)S(1)}, u32[]{:S(2)}) copy-start(f32[128,8]{1,0:T(8,128)S(1)} %broadcast_multiply_fusion.1) | copy-start | bytes 12292
  447.4 4.1 copy-start.1
  447.5 4.1 copy-start.4
  447.5 4.1 copy-start.6
  447.5 4.1 copy-start.8
  454.5 3.3 copy-start
  454.5 3.3 copy-start.12
  458.4 12.6 %collective-permute-start.1 = (bf16[2,8,1024]{2,1,0:T(8,128)(2,1)S(1)}, bf16[2,8,1024]{2,1,0:T(8,128)(2,1)S(1)}, u32[]{:S(2)}, u32[]{:S(2)}) collective-permute-start(bf16[2,8,1024]{2,1,0:T(8,128)(2,1)S(1)} %slice.174), channel_id=1, source_target_pairs={{1,0},{2,1},{3,2},{4,3},{5,4},{6,5},{7,6},{8,7},{9,8},{10,9},{11,1... | collective-permute-start | bytes 98312 | tf_op jit(solution)/shard_map/ppermute | solution.py:18
  469.7 5.9 %copy-start.11 = (f32[128,512]{1,0:T(8,128)S(1)}, f32[128,512]{1,0:T(8,128)}, u32[]{:S(2)}) copy-start(f32[128,512]{1,0:T(8,128)} %get-tuple-element.101) | copy-start | bytes 786436

commit v2 on v1

--- a/solution.py
+++ b/solution.py
@@ -62,7 +62,7 @@
 CHUNKS = 17
 FEED = 11
 WIDE = 768
-ROUNDS = 4
+ROUNDS = 5
 
 
 def mm(a, b):
@@ -92,17 +92,32 @@
 
 
 def layer_kernel(
-    tok,
+    tok_hbm,
     ctx,
-    gains,
+    gain_one,
+    gain_two,
     cot,
+    ctx_own,
+    qkv_own,
+    out_own,
+    gate_own,
+    up_own,
+    down_own,
+    delay,
+    lengths,
+    mixed_hbm,
+    dtok_hbm,
+    dctx,
+    dctxw_hbm,
+    dgain_one,
+    dgain_two,
+    dqkv_hbm,
+    dout_hbm,
+    dgate_hbm,
+    dup_hbm,
+    ddown_hbm,
+    gathered,
     w_own,
-    mixed_hbm,
-    gin_hbm,
-    dctx,
-    gain_out,
-    dw_hbm,
-    gathered,
     lin,
     n1,
     n1t,
@@ -115,8 +130,8 @@
     oacc,
     gn,
     wbuf,
+    wtail,
     part,
-    gg,
     hidt,
     shift,
     bias,
@@ -146,7 +161,9 @@
     g_rs,
     own_sem,
     load_sem,
-    fin_sem,
+    tok_sem,
+    rim_ss,
+    rim_rs,
     out_sem,
 ):
     s = lax.axis_index("stream")
@@ -162,91 +179,200 @@
     d_x = (1 - s, f)
     partners = (d_zh, d_zl, d_y, d_c)
 
-    own_copy = pltpu.make_async_copy(w_own, gathered.at[:, zh, zl, y, c], own_sem)
-    own_copy.start()
+    frames = lax.axis_size("frames")
+    has_next, has_prev = f < frames - 1, f > 0
+    d_next, d_prev = (s, f + 1), (s, f - 1)
+
+    tokext = n2t
+    tok_copy = pltpu.make_async_copy(tok_hbm, tokext.at[16:1040], tok_sem)
+    tok_copy.start()
 
     barrier = pltpu.get_barrier_semaphore()
+
+    def greet(device):
+        pl.semaphore_signal(barrier, inc=1, device_id=device, device_id_type=MESH)
+
     for device in partners + (d_x,):
-        pl.semaphore_signal(barrier, inc=1, device_id=device, device_id_type=MESH)
-    pl.semaphore_wait(barrier, 5)
+        greet(device)
+    pl.when(has_next)(lambda: greet(d_next))
+    pl.when(has_prev)(lambda: greet(d_prev))
+
+    w_own[0, 0:32, 0:512] = ctx_own[:, 0:512]
+    w_own[0, 32:64, 0:512] = ctx_own[:, 512:1024]
+    w_own[0, :, 512:768] = out_own[:, 768:1024]
+    w_own[5] = out_own[:, 0:768]
+    for g in range(4):
+        for part_id in range(3):
+            at = part_id * 1024 + g * 256
+            w_own[1 + g, :, part_id * 256 : part_id * 256 + 256] = qkv_own[:, at : at + 256]
+
+    def own_copy(low, high, i):
+        return pltpu.make_async_copy(
+            w_own.at[low:high], gathered.at[low:high, zh, zl, y, c], own_sem.at[i]
+        )
+
+    own_copy(0, 6, 0).start()
+
+    pl.semaphore_wait(barrier, 5 + has_next.astype(jnp.int32) + has_prev.astype(jnp.int32))
 
     def remote(src, dst, ss, rs, device):
         return pltpu.make_async_remote_copy(
             src_ref=src, dst_ref=dst, send_sem=ss, recv_sem=rs, device_id=device, device_id_type=MESH
         )
 
-    def ag_copy(stage, k):
+    def crossed(k):
+        return k % 4 == 2
+
+    def ag_copy(stage, k, cross):
         if stage == 0:
             src = dst = gathered.at[k, zh, zl, y, c]
         elif stage == 1:
             src = dst = gathered.at[k, :, zl, y, c]
         elif stage == 2:
-            src = dst = gathered.at[k, :, :, y, c]
+            src = dst = gathered.at[k, :, zl, :, c] if cross else gathered.at[k, :, :, y, c]
         else:
             src = dst = gathered.at[k, :, :, :, c]
-        return remote(src, dst, ag_ss.at[stage, k], ag_rs.at[stage, k], partners[stage])
+        if stage == 0:
+            src = w_own.at[k]
+        order = (d_zh, d_y, d_zl, d_c) if cross else (d_zh, d_zl, d_y, d_c)
+        return remote(src, dst, ag_ss.at[stage, k], ag_rs.at[stage, k], order[stage])
+
+    def ag_start(stage, k):
+        if stage in (0, 3):
+            ag_copy(stage, k, False).start()
+        elif isinstance(k, int):
+            ag_copy(stage, k, crossed(k)).start()
+        else:
+            pl.when(crossed(k))(lambda: ag_copy(stage, k, True).start())
+            pl.when(jnp.logical_not(crossed(k)))(lambda: ag_copy(stage, k, False).start())
+
+    def load_copy(k, slot):
+        return pltpu.make_async_copy(gathered.at[k], wbuf.at[slot], load_sem.at[slot])
 
     def ag_tick(t):
         for stage in range(4):
             def step(stage=stage):
                 k = t - stage
                 if stage > 0:
-                    ag_copy(stage - 1, k).wait_recv()
-                ag_copy(stage, k).start()
+                    ag_copy(stage - 1, k, False).wait_recv()
+                ag_start(stage, k)
             either(within(t, stage, stage + CHUNKS), step)
         def ready():
-            ag_copy(3, t - 4).wait_recv()
+            ag_copy(3, t - 4, False).wait_recv()
+            load_copy(t - 4, t % 2).start()
         either(within(t, 4, 4 + CHUNKS), ready)
-
-    def load(k, slot):
-        cp = pltpu.make_async_copy(gathered.at[k], wbuf.at[slot], load_sem.at[slot])
-        cp.start()
-        cp.wait()
 
     def rs_copy(stage, r):
         two, four = r % 2, r % ROUNDS
         if stage == 0:
-            src, dst = part.at[two, :, :, :, 1 - c], r_c.at[four]
+            src, dst = part.at[two, :, :, :, 1 - c], r_c.at[two]
         elif stage == 1:
             src, dst = t_send.at[two], r_y.at[four]
         elif stage == 2:
             src, dst = u_send.at[two], r_zl.at[four]
         else:
             src, dst = v_send.at[two], r_zh.at[four]
-        return remote(src, dst, rs_ss.at[stage, two], rs_rs.at[stage, four], partners[3 - stage])
+        cross = flag(r)
+        to_y, to_zl = f + 2 - 4 * y, f + 4 - 8 * zl
+        if stage == 1:
+            device = (s, to_y * (1 - cross) + to_zl * cross)
+        elif stage == 2:
+            device = (s, to_zl * (1 - cross) + to_y * cross)
+        else:
+            device = partners[3 - stage]
+        return remote(src, dst, rs_ss.at[stage, two], rs_rs.at[stage, four], device)
+
+    def flag(r):
+        return int(crossed(r)) if isinstance(r, int) else crossed(r).astype(jnp.int32)
 
     def add(a, b):
         return a.astype(jnp.float32) + b.astype(jnp.float32)
 
-    def fin_copy(r):
-        return pltpu.make_async_copy(fin.at[r % 2], dw_hbm.at[r], fin_sem.at[r % 2])
+    def place_result(k, res):
+        if not isinstance(k, int):
+            @pl.when(k < FEED)
+            def _():
+                fin[k] = res
+            pl.when(k == FEED)(lambda: place_result(FEED, res))
+            return
+        if k < FEED:
+            fin[k] = res
+        elif k == FEED:
+            aft[384:448, 0:768] = res
+        elif k < CHUNKS - 1:
+            g = k - FEED - 1
+            for p in range(3):
+                aft[192 + 64 * p : 256 + 64 * p, g * 256 : g * 256 + 256] = res[:, p * 256 : p * 256 + 256]
+        else:
+            aft[384:448, 768:1024] = res[:, 512:768]
+            aft[448:480, 0:512] = res[0:32, 0:512]
+            aft[448:480, 512:1024] = res[32:64, 0:512]
+
+    def out_copies():
+        pairs = [(aft.at[384:448], dout_hbm), (aft.at[448:480], dctxw_hbm)]
+        for p in range(3):
+            pairs.append((aft.at[192 + 64 * p : 256 + 64 * p], dqkv_hbm.at[:, p * 1024 : p * 1024 + 1024]))
+        return pairs
+
+    def feed_copies():
+        pairs = [(aft.at[512:688], ddown_hbm)]
+        for i, hbm in enumerate((dgate_hbm, dup_hbm)):
+            at = i * 768
+            if i == 1:
+                at = 704
+            for p in range(3):
+                n = 1024 if p < 2 else 768
+                pairs.append((aft.at[at + 64 * p : at + 64 * p + 64, 0:n], hbm.at[:, p * 1024 : p * 1024 + n]))
+        return pairs
+
+    def out_copy(pair, i):
+        return pltpu.make_async_copy(pair[0], pair[1], out_sem.at[i])
+
+    def unpack_feed():
+        for j in range(FEED):
+            for q in range(4):
+                aft[512 + j * 16 : 528 + j * 16, q * 256 : q * 256 + 256] = fin[j, q * 16 : q * 16 + 16, 512:768]
+        for i, at in enumerate((0, 704)):
+            cols = [
+                fin[j, :, i * 256 + d * 16 : i * 256 + d * 16 + 16] for d in range(16) for j in range(FEED)
+            ]
+            for p in range(22):
+                piece = jnp.concatenate(cols[p * 8 : p * 8 + 8], axis=1)
+                row, col = at + 64 * (p // 8), (p % 8) * 128
+                aft[row : row + 64, col : col + 128] = piece
 
     def rs_tick(r, static_first=False):
-        def start_c():
-            rs_copy(0, r).start()
-        either(within(r, 0, CHUNKS), start_c)
-
         def stage_y():
             k = r - 1
             rs_copy(0, k).wait_recv()
             either(within(k, 2, CHUNKS), lambda: rs_copy(1, k - 2).wait_send())
             two, four = k % 2, k % ROUNDS
+            cross = flag(k)
+
             def piece(i, _):
                 a, b = i // 2, i % 2
-                t_send[two, i] = add(part[two, a, b, 1 - y, c], r_c[four, a, b, 1 - y]).astype(jnp.bfloat16)
-                t_keep[two, i] = add(part[two, a, b, y, c], r_c[four, a, b, y]).astype(jnp.bfloat16)
+                near = b * (1 - cross) + (1 - zl) * cross
+                side = (1 - y) * (1 - cross) + b * cross
+                t_send[two, i] = add(part[two, a, near, side, c], r_c[two, a, near, side]).astype(jnp.bfloat16)
+                near = b * (1 - cross) + zl * cross
+                side = y * (1 - cross) + b * cross
+                t_keep[two, i] = add(part[two, a, near, side, c], r_c[two, a, near, side]).astype(jnp.bfloat16)
                 return 0
+
             lax.fori_loop(0, 4, piece, 0)
             rs_copy(1, k).start()
         either(within(r, 1, CHUNKS + 1), stage_y)
+        either(within(r, 0, CHUNKS), lambda: rs_copy(0, r).start())
 
         def stage_zl():
             k = r - 2
             rs_copy(1, k).wait_recv()
             either(within(k, 2, CHUNKS), lambda: rs_copy(2, k - 2).wait_send())
             two, four = k % 2, k % ROUNDS
+            cross = flag(k)
+            mine = zl * (1 - cross) + y * cross
             for a in range(2):
-                far, near = a * 2 + 1 - zl, a * 2 + zl
+                far, near = a * 2 + 1 - mine, a * 2 + mine
                 u_send[two, a] = add(t_keep[two, far], r_y[four, far]).astype(jnp.bfloat16)
                 u_keep[two, a] = add(t_keep[two, near], r_y[four, near]).astype(jnp.bfloat16)
             rs_copy(2, k).start()
@@ -265,27 +391,76 @@
         def last():
             k = r - 4
             rs_copy(3, k).wait_recv()
-            either(within(k, 2, CHUNKS), lambda: fin_copy(k - 2).wait())
-            fin[k % 2] = add(v_keep[k % 2], r_zh[k % ROUNDS])
-            fin_copy(k).start()
+            place_result(k, add(v_keep[k % 2], r_zh[k % ROUNDS]))
         either(within(r, 4, CHUNKS + 4), last)
 
     def part_free(r):
         either(within(r, 2, CHUNKS), lambda: rs_copy(0, r - 2).wait_send())
+
+    rim_copy = remote(tok_hbm.at[1008:1024], tokext.at[0:16], rim_ss.at[0], rim_rs.at[0], d_next)
+    halo_copy = remote(oacc.at[0:16], oacc.at[1024:1040], rim_ss.at[1], rim_rs.at[1], d_prev)
+    pl.when(has_next)(lambda: rim_copy.start())
+
+    @pl.when(jnp.logical_not(has_prev))
+    def _():
+        tokext[0:16, :] = jnp.zeros((16, 1024), jnp.bfloat16)
+
+    @pl.when(jnp.logical_not(has_next))
+    def _():
+        oacc[1024:1040, :] = jnp.zeros((16, 1024), jnp.float32)
 
     row_id = lax.broadcasted_iota(jnp.int32, (128, 256), 0)
     col_id = lax.broadcasted_iota(jnp.int32, (128, 256), 1) % 128
     seen = jnp.logical_and(row_id // 8 == col_id // 8, col_id <= row_id)
     bias[...] = jnp.where(seen, 0.0, -1e30)
 
-    def zero_gain(i, _):
-        gacc[...] = jnp.zeros_like(gacc)
-        return 0
-    lax.fori_loop(0, 1, zero_gain, 0)
-
-    ag_tick_first(ag_tick, own_copy)
-
-    load(0, 0)
+    gacc[...] = jnp.zeros_like(gacc)
+
+    place = lax.broadcasted_iota(jnp.int32, (16, 8, 1), 1)
+    wait = jnp.zeros((16, 8, 1), jnp.int32)
+    for p in range(8):
+        wait = jnp.where(place == p, delay[p], wait)
+
+    def starts_at(frame):
+        start = jnp.int32(0)
+        hit = frame == start
+        for i in range(lengths.shape[0] - 1):
+            start = start + lengths[i]
+            hit = jnp.logical_or(hit, frame == start)
+        return hit
+
+    def same_item(frame, j):
+        ok = jnp.logical_not(starts_at(frame))
+        if j == 2:
+            ok = jnp.logical_and(ok, jnp.logical_not(starts_at(frame - 1)))
+        return ok
+
+    def frame_of(i):
+        return f * 128 + i * 16 + lax.broadcasted_iota(jnp.int32, (16, 8, 1), 0)
+
+    def pack_feed(own, at):
+        for j in range(FEED):
+            cols = [own[:, d * 176 + j * 16 : d * 176 + j * 16 + 16] for d in range(16)]
+            w_own[6 + j, :, at : at + 256] = jnp.concatenate(cols, axis=1)
+
+    ag_tick(0)
+    own_copy(0, 6, 0).wait()
+    ag_tick(1)
+    for j in range(FEED):
+        for q in range(4):
+            w_own[6 + j, q * 16 : q * 16 + 16, 512:768] = down_own[
+                j * 16 : j * 16 + 16, q * 256 : q * 256 + 256
+            ]
+    pack_feed(gate_own, 0)
+    ag_tick(2)
+    pack_feed(up_own, 256)
+    own_copy(6, CHUNKS, 1).start()
+    ag_tick(3)
+    ag_tick(4)
+    own_copy(6, CHUNKS, 1).wait()
+
+    load_copy(0, 0).wait()
+    wtail[...] = wbuf[0, :, :, :, :, :, 512:768].reshape(1024, 256)
     half = shift.shape[1] // 2
     for h in range(2):
         w_half = wbuf[0, :, :, :, :, h * 32 : h * 32 + 32, 0:512].reshape(512, 512)
@@ -306,14 +481,25 @@
     def norm1(i, _):
         rows = rows_of(i, 128)
         sh = shift[rows_of(i, 16), :]
-        x = tok[rows, :].astype(jnp.float32).reshape(16, 8, 1024) + sh[:, None, :]
+        near = tokext[pl.ds(pl.multiple_of(i * 128, 128), 144), :].astype(jnp.float32)
+        frame = frame_of(i)
+        x = jnp.zeros((16, 8, 1024), jnp.float32)
+        for j in range(3):
+            keep = wait == j
+            if j > 0:
+                keep = jnp.logical_and(keep, same_item(frame, j))
+            piece = near[16 - 8 * j : 144 - 8 * j].reshape(16, 8, 1024)
+            x = jnp.where(keep, piece, x)
+        x = x + sh[:, None, :]
         r = lax.rsqrt(jnp.mean(x * x, axis=-1, keepdims=True) + epsilon)
-        n = (x * r * gains[0][None]).reshape(128, 1024).astype(jnp.bfloat16)
+        n = (x * r * gain_one[...].astype(jnp.float32)[None]).reshape(128, 1024).astype(jnp.bfloat16)
         lin[rows, :] = x.reshape(128, 1024)
         n1[rows, :] = n
         n1t[:, rows] = n.T
         return 0
 
+    tok_copy.wait()
+    pl.when(has_prev)(lambda: rim_copy.wait_recv())
     lax.fori_loop(0, 8, norm1, 0)
 
     lane_low = lax.broadcasted_iota(jnp.int32, (128, 128), 1) < 64
@@ -380,54 +566,56 @@
         lax.fori_loop(0, 4, rows_step, 0)
 
     def qkv_group(g, _):
-        either(g > 0, lambda: ag_tick(5 + g))
-        load(1 + g, 0)
+        slot = (1 + g) % 2
+        load_copy(1 + g, slot).wait()
+
         def rows_step(i, _):
             rows = rows_of(i, 256)
-            qkv[g, rows, :] = mm(n1[rows, :], wbuf[0].reshape(1024, WIDE)).astype(jnp.bfloat16)
+            qkv[g, rows, :] = mm(n1[rows, :], wbuf[slot].reshape(1024, WIDE)).astype(jnp.bfloat16)
             return 0
+
         lax.fori_loop(0, 4, rows_step, 0)
         attn_fwd(g)
+        ag_tick(6 + g)
         return 0
 
     lax.fori_loop(0, 4, qkv_group, 0)
 
-    ag_tick(9)
-    load(5, 0)
-    load(0, 1)
+    load_copy(5, 1).wait()
 
     def after(i, _):
         rows = rows_of(i, 256)
         m = mixed[rows, :]
-        a = lin[rows, 0:WIDE] + mm(m, wbuf[0].reshape(1024, WIDE))
-        b = lin[rows, WIDE:1024] + mm(m, wbuf[1, :, :, :, :, :, 512:768].reshape(1024, 256))
+        a = lin[rows, 0:WIDE] + mm(m, wbuf[1].reshape(1024, WIDE))
+        b = lin[rows, WIDE:1024] + mm(m, wtail[...])
         x = jnp.concatenate([a, b], axis=1)
         aft[rows, :] = x
         oacc[rows, :] = x
         x3 = x.reshape(32, 8, 1024)
         r = lax.rsqrt(jnp.mean(x3 * x3, axis=-1, keepdims=True) + epsilon)
-        n = (x3 * r * gains[1][None]).reshape(256, 1024).astype(jnp.bfloat16)
+        n = (x3 * r * gain_two[...].astype(jnp.float32)[None]).reshape(256, 1024).astype(jnp.bfloat16)
         n2[rows, :] = n
-        n2t[:, rows] = n.T
+        n2t[0:1024, rows] = n.T
         mixt[:, rows] = m.T
         return 0
 
     lax.fori_loop(0, 4, after, 0)
+    ag_tick(10)
 
     def feed(j, _):
-        ag_tick(10 + j)
-        load(6 + j, 0)
+        slot = j % 2
+        load_copy(6 + j, slot).wait()
         part_free(j)
         two = j % 2
 
         def rows_step(i, _):
             rows = rows_of(i, 256)
-            w_gu = wbuf[0, :, :, :, :, :, 0:512].reshape(1024, 512)
+            w_gu = wbuf[slot, :, :, :, :, :, 0:512].reshape(1024, 512)
             pre = mm(n2[rows, :], w_gu)
             gate, up = pre[:, :256], pre[:, 256:]
             g_hid = jnp.zeros((256, 256), jnp.float32)
             for q in range(4):
-                w_q = wbuf[0, :, :, :, :, q * 16 : q * 16 + 16, 512:768].reshape(256, 256)
+                w_q = wbuf[slot, :, :, :, :, q * 16 : q * 16 + 16, 512:768].reshape(256, 256)
                 g_hid = g_hid + nt(cot[rows, q * 256 : q * 256 + 256], w_q)
             sig = jax.nn.sigmoid(gate)
             silu = gate * sig
@@ -435,10 +623,10 @@
             g_gate = (g_hid * up * sig * (1.0 + gate * (1.0 - sig))).astype(jnp.bfloat16)
             g_up = (g_hid * silu).astype(jnp.bfloat16)
             for q in range(4):
-                w_q = wbuf[0, :, :, :, :, q * 16 : q * 16 + 16, 512:768].reshape(256, 256)
+                w_q = wbuf[slot, :, :, :, :, q * 16 : q * 16 + 16, 512:768].reshape(256, 256)
                 oacc[rows, q * 256 : q * 256 + 256] += mm(hid, w_q)
             both_g = jnp.concatenate([g_gate, g_up], axis=1)
-            gg[rows, :] = both_g
+            n1[rows, 0:512] = both_g
             hidt[:, rows] = hid.T
             back = nt(both_g, w_gu)
             @pl.when(j == 0)
@@ -452,7 +640,7 @@
         lax.fori_loop(0, 4, rows_step, 0)
 
         def weight_step(m, _):
-            res = mm(n2t[rows_of(m, 256), :], gg[...]).astype(jnp.bfloat16).reshape(2, 2, 64, 512)
+            res = mm(n2t[rows_of(m, 256), :], n1[:, 0:512]).astype(jnp.bfloat16).reshape(2, 2, 64, 512)
             part[two, m // 2, m % 2, :, :, :, 0:512] = res
             return 0
 
@@ -460,20 +648,23 @@
         for q in range(4):
             res = mm(hidt[...], cot[:, q * 256 : q * 256 + 256]).astype(jnp.bfloat16)
             part[two, :, :, :, :, q * 16 : q * 16 + 16, 512:768] = res.reshape(2, 2, 2, 2, 16, 256)
+        ag_tick(11 + j)
         rs_tick(j)
         return 0
 
     lax.fori_loop(0, FEED, feed, 0)
+    load_copy(5, 1).start()
+    load_copy(1, 0).start()
 
     def norm2_back(i, _):
         rows = rows_of(i, 128)
-        n1[rows, :] = oacc[rows, :].astype(jnp.bfloat16)
+        n2t[rows, :] = oacc[rows, :].astype(jnp.bfloat16)
         x = aft[rows, :].reshape(16, 8, 1024)
         g = gn[rows, :].reshape(16, 8, 1024)
         r = lax.rsqrt(jnp.mean(x * x, axis=-1, keepdims=True) + epsilon)
         unit = x * r
         gacc[8:16, :] += jnp.sum(g * unit, axis=0)
-        gu = g * gains[1][None]
+        gu = g * gain_two[...].astype(jnp.float32)[None]
         back = r * (gu - unit * jnp.mean(gu * unit, axis=-1, keepdims=True))
         total = cot[rows, :].astype(jnp.float32) + back.reshape(128, 1024)
         oacc[rows, :] = total
@@ -481,11 +672,9 @@
         return 0
 
     lax.fori_loop(0, 8, norm2_back, 0)
-    mixed_copy = pltpu.make_async_copy(n1, mixed_hbm, out_sem.at[0])
+    mixed_copy = pltpu.make_async_copy(n2t.at[0:1024], mixed_hbm, out_sem.at[0])
     mixed_copy.start()
 
-    load(5, 0)
-    load(0, 1)
     part_free(11)
 
     def out_weight_step(m, _):
@@ -499,16 +688,16 @@
     def mixed_back(i, _):
         rows = rows_of(i, 256)
         g = n2[rows, :]
-        res = nt(g[:, 0:WIDE], wbuf[0].reshape(1024, WIDE)) + nt(
-            g[:, WIDE:1024], wbuf[1, :, :, :, :, :, 512:768].reshape(1024, 256)
-        )
+        res = nt(g[:, 0:WIDE], wbuf[1].reshape(1024, WIDE)) + nt(g[:, WIDE:1024], wtail[...])
         mixed[rows, :] = res.astype(jnp.bfloat16)
         return 0
 
+    load_copy(5, 1).wait()
     lax.fori_loop(0, 4, mixed_back, 0)
+    load_copy(2, 1).start()
 
     def qkv_back(g, _):
-        load(1 + g, 0)
+        slot = g % 2
         attn_bwd(g)
         part_free(12 + g)
         two = g % 2
@@ -523,7 +712,7 @@
 
         def rows_step(i, _):
             rows = rows_of(i, 256)
-            back = nt(qkv[g, rows, :], wbuf[0].reshape(1024, WIDE))
+            back = nt(qkv[g, rows, :], wbuf[slot].reshape(1024, WIDE))
             @pl.when(g == 0)
             def _():
                 gn[rows, :] = back
@@ -532,7 +721,10 @@
                 gn[rows, :] += back
             return 0
 
+        load_copy(1 + g, slot).wait()
         lax.fori_loop(0, 4, rows_step, 0)
+        pl.when(g < 2)(lambda: load_copy(3 + g, slot).start())
+        pl.when(g == 2)(lambda: load_copy(0, 0).start())
         return 0
 
     lax.fori_loop(0, 4, qkv_back, 0)
@@ -544,7 +736,7 @@
         r = lax.rsqrt(jnp.mean(x * x, axis=-1, keepdims=True) + epsilon)
         unit = x * r
         gacc[0:8, :] += jnp.sum(g * unit, axis=0)
-        gu = g * gains[0][None]
+        gu = g * gain_one[...].astype(jnp.float32)[None]
         back = r * (gu - unit * jnp.mean(gu * unit, axis=-1, keepdims=True))
         total = oacc[rows, :].reshape(16, 8, 1024) + back
         oacc[rows, :] = total.reshape(128, 1024)
@@ -552,9 +744,7 @@
         return 0
 
     lax.fori_loop(0, 8, norm1_back, 0)
-    gin_copy = pltpu.make_async_copy(oacc, gin_hbm, out_sem.at[1])
-    gin_copy.start()
-
+    pl.when(has_prev)(lambda: halo_copy.start())
     xsend[1] = shift[...].astype(jnp.bfloat16)
     x_copy(1).start()
 
@@ -564,7 +754,7 @@
     gsend[0] = gacc[...]
     gain_copy(0).start()
 
-    load(0, 1)
+    load_copy(0, 0).wait()
     part_free(16)
 
     def out_tail_step(m, _):
@@ -582,18 +772,48 @@
         res = mm(ctx_t, gh).astype(jnp.bfloat16).reshape(2, 2, 2, 2, 32, 512)
         part[0, :, :, :, :, h * 32 : h * 32 + 32, 0:512] = res
     rs_tick(16)
-    w0 = wbuf[1, :, :, :, :, 0:32, 0:512].reshape(512, 512)
-    w1 = wbuf[1, :, :, :, :, 32:64, 0:512].reshape(512, 512)
+    w0 = wbuf[0, :, :, :, :, 0:32, 0:512].reshape(512, 512)
+    w1 = wbuf[0, :, :, :, :, 32:64, 0:512].reshape(512, 512)
     dctx[...] = nt(g_low[:, :512], w0) + nt(g_low[:, 512:], w1)
 
+    def dtok(i, _):
+        rows = rows_of(i, 128)
+        near = oacc[pl.ds(pl.multiple_of(i * 128, 128), 144), :]
+        frame = frame_of(i)
+        x = jnp.zeros((16, 8, 1024), jnp.float32)
+        for j in range(3):
+            keep = wait == j
+            if j > 0:
+                keep = jnp.logical_and(keep, same_item(frame + j, j))
+            x = jnp.where(keep, near[8 * j : 128 + 8 * j].reshape(16, 8, 1024), x)
+        gn[rows, :] = x.reshape(128, 1024)
+        return 0
+
+    dtok_copy = pltpu.make_async_copy(gn, dtok_hbm, out_sem.at[1])
+    feed_out = [out_copy(pair, 2 + i) for i, pair in enumerate(feed_copies())]
     for i in range(4):
         gain_copy(i).wait_recv()
         if i < 3:
             gsend[i + 1] = gsend[i] + grecv[i]
             gain_copy(i + 1).start()
         else:
-            gain_out[...] = gsend[i] + grecv[i]
+            total = gsend[i] + grecv[i]
+            dgain_one[...] = total[0:8]
+            dgain_two[...] = total[8:16]
         rs_tick(17 + i)
+        if i == 0:
+            unpack_feed()
+            for cp in feed_out:
+                cp.start()
+            pl.when(has_next)(lambda: halo_copy.wait_recv())
+            lax.fori_loop(0, 8, dtok, 0)
+            dtok_copy.start()
+
+    last_out = [out_copy(pair, 9 + i) for i, pair in enumerate(out_copies())]
+    for cp in last_out:
+        cp.start()
+    pl.when(has_next)(lambda: rim_copy.wait_send())
+    pl.when(has_prev)(lambda: halo_copy.wait_send())
 
     for i in range(4):
         gain_copy(i).wait_send()
@@ -606,30 +826,21 @@
 
     def drain(k, _):
         for stage in range(4):
-            ag_copy(stage, k).wait_send()
+            ag_copy(stage, k, False).wait_send()
         return 0
 
     lax.fori_loop(0, CHUNKS, drain, 0)
-    fin_copy(CHUNKS - 2).wait()
-    fin_copy(CHUNKS - 1).wait()
     mixed_copy.wait()
-    gin_copy.wait()
-
-
-def ag_tick_first(ag_tick, own_copy):
-    own_copy.wait()
-
-    def step(t, _):
-        ag_tick(t)
-        return 0
-
-    lax.fori_loop(0, 5, step, 0)
-
-
-def call_layer(tok, ctx, gains, cot, w_own):
+    dtok_copy.wait()
+    for cp in feed_out + last_out:
+        cp.wait()
+
+
+def call_layer(tok, ctx, gain_one, gain_two, cot, weights, delay, lengths):
     f32, bf16 = jnp.float32, jnp.bfloat16
     vm, dma = pltpu.VMEM, pltpu.SemaphoreType.DMA
     shape = jax.ShapeDtypeStruct
+    in_vmem, in_hbm, in_smem = (pl.BlockSpec(memory_space=m) for m in (pltpu.VMEM, pltpu.HBM, pltpu.SMEM))
     return pl.pallas_call(
         layer_kernel,
         name="layer",
@@ -637,20 +848,20 @@
             shape((1024, 1024), bf16),
             shape((1024, 1024), f32),
             shape((128, 512), f32),
-            shape((16, 1024), f32),
-            shape((CHUNKS, 64, WIDE), f32),
+            shape((32, 1024), f32),
+            shape((8, 1024), f32),
+            shape((8, 1024), f32),
+            shape((64, 3072), f32),
+            shape((64, 1024), f32),
+            shape((64, 2816), f32),
+            shape((64, 2816), f32),
+            shape((176, 1024), f32),
             shape((CHUNKS, 2, 2, 2, 2, 64, WIDE), bf16),
         ),
-        in_specs=[pl.BlockSpec(memory_space=pltpu.VMEM)] * 4 + [pl.BlockSpec(memory_space=pltpu.HBM)],
-        out_specs=(
-            pl.BlockSpec(memory_space=pltpu.HBM),
-            pl.BlockSpec(memory_space=pltpu.HBM),
-            pl.BlockSpec(memory_space=pltpu.VMEM),
-            pl.BlockSpec(memory_space=pltpu.VMEM),
-            pl.BlockSpec(memory_space=pltpu.HBM),
-            pl.BlockSpec(memory_space=pltpu.HBM),
-        ),
+        in_specs=[in_hbm] + [in_vmem] * 10 + [in_smem] * 2,
+        out_specs=(in_hbm, in_hbm, in_vmem, in_hbm, in_vmem, in_vmem) + (in_hbm,) * 6,
         scratch_shapes=[
+            vm((CHUNKS, 64, WIDE), bf16),
             vm((1024, 1024), f32),
             vm((1024, 1024), bf16),
             vm((1024, 1024), bf16),
@@ -659,12 +870,12 @@
             vm((1024, 1024), bf16),
             vm((1024, 1024), f32),
             vm((1024, 1024), bf16),
-            vm((1024, 1024), bf16),
-            vm((1024, 1024), f32),
+            vm((1040, 1024), bf16),
+            vm((1040, 1024), f32),
             vm((1024, 1024), f32),
             vm((2, 2, 2, 2, 2, 64, WIDE), bf16),
+            vm((1024, 256), bf16),
             vm((2, 2, 2, 2, 2, 64, WIDE), bf16),
-            vm((1024, 512), bf16),
             vm((256, 1024), bf16),
             vm((128, 1024), f32),
             vm((128, 256), f32),
@@ -673,7 +884,7 @@
             vm((4, 16, 1024), f32),
             vm((2, 128, 1024), bf16),
             vm((2, 128, 1024), bf16),
-            vm((ROUNDS, 2, 2, 2, 64, WIDE), bf16),
+            vm((2, 2, 2, 2, 64, WIDE), bf16),
             vm((ROUNDS, 4, 64, WIDE), bf16),
             vm((ROUNDS, 2, 64, WIDE), bf16),
             vm((ROUNDS, 64, WIDE), bf16),
@@ -683,7 +894,7 @@
             vm((2, 2, 64, WIDE), bf16),
             vm((2, 64, WIDE), bf16),
             vm((2, 64, WIDE), bf16),
-            vm((2, 64, WIDE), f32),
+            vm((FEED, 64, WIDE), f32),
             dma((4, CHUNKS)),
             dma((4, CHUNKS)),
             dma((4, 2)),
@@ -692,37 +903,17 @@
             dma((2,)),
             dma((4,)),
             dma((4,)),
+            dma((2,)),
+            dma((2,)),
             dma,
             dma((2,)),
             dma((2,)),
-            dma((2,)),
+            dma((14,)),
         ],
         compiler_params=pltpu.CompilerParams(
             collective_id=0, has_side_effects=True, vmem_limit_bytes=63 * 1024 * 1024
         ),
-    )(tok, ctx, gains, cot, w_own)
-
-
-def pack_weights(ctx_weight, qkv_weight, out_weight, gate_weight, up_weight, down_weight):
-    qkv = qkv_weight.reshape(64, 3, 4, 256).transpose(2, 0, 1, 3).reshape(4, 64, WIDE)
-    gate = gate_weight.reshape(64, 16, FEED, 16).transpose(2, 0, 1, 3).reshape(FEED, 64, 256)
-    up = up_weight.reshape(64, 16, FEED, 16).transpose(2, 0, 1, 3).reshape(FEED, 64, 256)
-    down = down_weight.reshape(FEED, 16, 4, 256).transpose(0, 2, 1, 3).reshape(FEED, 64, 256)
-    feed = jnp.concatenate([gate, up, down], axis=-1)
-    ctx = ctx_weight.reshape(32, 2, 512).transpose(1, 0, 2).reshape(64, 512)
-    first = jnp.concatenate([ctx, out_weight[:, WIDE:]], axis=-1)
-    return jnp.concatenate([first[None], qkv, out_weight[None, :, :WIDE], feed], axis=0)
-
-
-def unpack_grads(dw):
-    feed = dw[:FEED]
-    gate = feed[:, :, 0:256].reshape(FEED, 64, 16, 16).transpose(1, 2, 0, 3).reshape(64, 2816)
-    up = feed[:, :, 256:512].reshape(FEED, 64, 16, 16).transpose(1, 2, 0, 3).reshape(64, 2816)
-    down = feed[:, :, 512:768].reshape(FEED, 4, 16, 256).transpose(0, 2, 1, 3).reshape(176, 1024)
-    out = jnp.concatenate([dw[11], dw[16][:, 512:]], axis=-1)
-    qkv = dw[12:16].reshape(4, 64, 3, 256).transpose(1, 2, 0, 3).reshape(64, 3072)
-    ctx = dw[16][:, :512].reshape(2, 32, 512).transpose(1, 0, 2).reshape(32, 1024)
-    return (qkv, out, gate, up, down, ctx)
+    )(tok, ctx, gain_one, gain_two, cot, *weights, delay, lengths)
 
 
 def body_kernel(
@@ -741,38 +932,26 @@
     cotangent,
 ):
     frame_count, positions, width = tokens.shape[1:]
-    inputs = tokens[0]
-    rim_rows = shifted(inputs[frame_count - 2 :], "frames", 1)
-    extended = jnp.concatenate([rim_rows, inputs], axis=0)
-    frame_ids = lax.axis_index("frames") * frame_count + jnp.arange(frame_count, dtype=jnp.int32)
-    chosen, valid_rows = shift_tables(delay, lengths, frame_ids)
-    tok = jnp.zeros((frame_count, positions, width), jnp.float32)
-    for offset in range(3):
-        piece = extended[2 - offset : 2 - offset + frame_count].astype(jnp.float32)
-        tok = tok + chosen[offset][None, :, None] * valid_rows[offset][:, None, None] * piece
-    tok = tok.astype(jnp.bfloat16).reshape(frame_count * positions, width)
-    gains = jnp.stack([attn_gain[0], ffn_gain[0]]).astype(jnp.float32)
-    w_own = pack_weights(
-        ctx_weight, qkv_weight[0], out_weight[0], gate_weight[0], up_weight[0], down_weight[0]
-    )
-    mixed_out, grad_in, d_context, gain_sums, dw, _ = call_layer(
-        tok, context, gains, cotangent[0].reshape(frame_count * positions, width), w_own
-    )
-    d_qkv, d_out, d_gate, d_up, d_down, d_ctx = unpack_grads(dw)
-    grad_in = grad_in.reshape(frame_count, positions, width)
-    grad_ext = jnp.zeros((frame_count + 2, positions, width), jnp.float32)
-    for offset in range(3):
-        term = chosen[offset][None, :, None] * valid_rows[offset][:, None, None] * grad_in
-        grad_ext = grad_ext + jnp.pad(term, ((2 - offset, offset), (0, 0), (0, 0)))
-    back_rows = shifted(grad_ext[:2].astype(jnp.bfloat16), "frames", -1).astype(jnp.float32)
-    grad_tokens = grad_ext[2:].at[frame_count - 2 :].add(back_rows)
+    rows = frame_count * positions
+    weights = (ctx_weight, qkv_weight[0], out_weight[0], gate_weight[0], up_weight[0], down_weight[0])
+    mixed_out, d_tokens, d_context, d_ctx, d_gain_one, d_gain_two, *grads = call_layer(
+        tokens.reshape(rows, width),
+        context,
+        attn_gain[0],
+        ffn_gain[0],
+        cotangent.reshape(rows, width),
+        weights,
+        delay,
+        lengths,
+    )
+    d_qkv, d_out, d_gate, d_up, d_down, _ = grads
     return (
-        mixed_out.reshape(frame_count, positions, width)[None],
-        grad_tokens[None],
+        mixed_out.reshape(tokens.shape),
+        d_tokens.reshape(tokens.shape),
         d_context,
         d_ctx,
-        gain_sums[:8][None],
-        gain_sums[8:][None],
+        d_gain_one[None],
+        d_gain_two[None],
         d_qkv[None],
         d_out[None],
         d_gate[None],

time: 479 us -> 366 us (0.76)
  Pallas kernels: 418 us -> 352 us
  local copies, waits for them, and re-layouts: 34.7 us -> 12 us
  other arithmetic: 18.2 us -> 0 us
    pallas_call x1, Pallas kernels: 418 us -> 352 us  [call_layer(): pl.pallas_call(layer_kernel, name='layer', out_shape=(shape((1024, 1024),...]
    slice x9 -> x0, local copies, waits for them, and re-layouts: 8.82 us -> none  [the longest x1 2.85 us: unpack_grads(): feed[:, :, 512:768].reshape(FEED, 4, 16, 256).transpose(0, 2, 1, 3)]
    another operation x7 -> x0, local copies, waits for them, and re-layouts: 6.04 us -> none  [the longest x2 2.03 us: pack_weights(): down_weight.reshape(FEED, 16, 4, 256).transpose(0, 2, 1, 3)]
    reshape x6 -> x0, local copies, waits for them, and re-layouts: 5.02 us -> none  [the longest x1 1.47 us: pack_weights(): ctx = ctx_weight.reshape(32, 2, 512).transpose(1, 0, 2).reshape(64, 512)]
    unnamed x34 -> x31, local copies, waits for them, and re-layouts: 7.87 us -> 12 us
  transfers between devices with their start and end apart: 2 -> 0, of which waited for: 0 -> 0; matrix products, arithmetic and copies ran while one was open for 7% -> 0% of each run, Pallas kernels for 0% -> 0%
where the time goes in v2:
time: 366 us; the launch traced here: 364 us
  Pallas kernels  352 us (96%)
  local copies, waits for them, and re-layouts  12 us (3%)
    pallas_call x1, Pallas kernels, call_layer(): pl.pallas_call(layer_kernel, name='layer', out_shape=(shape((1024, 1024),...  352 us
    unnamed x31, local copies, waits for them, and re-layouts  12 us

profile of v2, /device:TPU:0, one launch (start us, length us, event | category | flops | bytes accessed | tf_op | source)
XLA Modules:
  0.0 364.5 jit_solution(16579714271898120261)
XLA Ops:
  0.6 351.7 %layer.1 = (bf16[1024,1024]{1,0:T(8,128)(2,1)}, f32[1024,1024]{1,0:T(8,128)}, f32[128,512]{1,0:T(8,128)}, f32[32,1024]{1,0:T(8,128)}, f32[8,1024]{1,0:T(8,128)},...) custom-call(bf16[1024,1024]{1,0:T(8,128)(2,1)} %bitcast.19, ...), custom_call_target="tpu_custom_call" | custom-call | tf_op jit(solution)/shard_map/layer/pallas_call | solution.py:844
  352.4 0.0 copy-start
  352.4 3.2 copy.35
  355.6 0.0 copy-done
  355.6 0.0 copy-start.6
  355.6 0.0 copy-start.7
  355.6 0.0 copy-start.9
  355.7 0.0 copy-start.8
  355.7 0.0 copy-start.1
  355.7 2.0 copy.36
  357.7 0.0 copy-done.6
  357.7 0.0 copy-start.5
  357.7 0.0 copy-start.4
  357.7 0.7 copy.37
  358.4 0.0 copy-done.7
  358.4 0.0 copy-start.3
  358.4 0.7 copy.38
  359.1 0.0 copy-done.9
  359.1 0.6 copy.39
  359.7 0.0 copy-done.8
  359.7 0.6 copy.40
  360.3 0.0 copy-done.1
  360.3 0.9 copy.41
  361.2 0.0 copy-done.5
  361.2 0.0 copy-start.2
  361.2 0.7 copy.42
  361.9 0.0 copy-done.4
  361.9 0.9 copy.43
  362.7 0.0 copy-done.3
  362.8 0.9 copy.44
  363.6 0.0 copy-done.2
  363.6 0.9 copy.45
Async XLA Ops:
  352.4 3.2 copy-start
  355.6 2.0 copy-start.6
  355.6 2.8 copy-start.7
  355.6 3.4 copy-start.9
  355.7 4.0 %copy-start.8 = (f32[8,1024]{1,0:T(8,128)S(1)}, f32[8,1024]{1,0:T(8,128)}, u32[]{:S(2)}) copy-start(f32[8,1024]{1,0:T(8,128)} %get-tuple-element.27) | copy-start | bytes 98308
  355.7 4.6 %copy-start.1 = (f32[64,3072]{1,0:T(8,128)S(1)}, f32[64,3072]{1,0:T(8,128)}, u32[]{:S(2)}) copy-start(f32[64,3072]{1,0:T(8,128)} %get-tuple-element.28) | copy-start | bytes 2359300
  357.7 3.5 copy-start.5
  357.7 4.2 %copy-start.4 = (f32[64,2816]{1,0:T(8,128)S(1)}, f32[64,2816]{1,0:T(8,128)}, u32[]{:S(2)}) copy-start(f32[64,2816]{1,0:T(8,128)} %get-tuple-element.30) | copy-start | bytes 2162692
  358.4 4.3 %copy-start.3 = (f32[64,2816]{1,0:T(8,128)S(1)}, f32[64,2816]{1,0:T(8,128)}, u32[]{:S(2)}) copy-start(f32[64,2816]{1,0:T(8,128)} %get-tuple-element.31) | copy-start | bytes 2162692
  361.2 2.4 copy-start.2

commit v3 on v2

--- a/solution.py
+++ b/solution.py
@@ -63,6 +63,8 @@
 FEED = 11
 WIDE = 768
 ROUNDS = 5
+MOST = 48
+SPLIT = ((0, MOST), (MOST, 64))
 
 
 def mm(a, b):
@@ -134,7 +136,6 @@
     part,
     hidt,
     shift,
-    bias,
     gacc,
     gsend,
     grecv,
@@ -220,31 +221,35 @@
             src_ref=src, dst_ref=dst, send_sem=ss, recv_sem=rs, device_id=device, device_id_type=MESH
         )
 
-    def crossed(k):
-        return k % 4 == 2
-
-    def ag_copy(stage, k, cross):
+    def ag_copies(stage, k):
         if stage == 0:
-            src = dst = gathered.at[k, zh, zl, y, c]
+            triples = [(w_own.at[k], gathered.at[k, zh, zl, y, c], d_zh)]
         elif stage == 1:
-            src = dst = gathered.at[k, :, zl, y, c]
+            near, side = gathered.at[k, :, zl, y, c, 0:MOST], gathered.at[k, :, zl, y, c, MOST:64]
+            triples = [(near, near, d_zl), (side, side, d_y)]
         elif stage == 2:
-            src = dst = gathered.at[k, :, zl, :, c] if cross else gathered.at[k, :, :, y, c]
+            side, near = gathered.at[k, :, :, y, c, 0:MOST], gathered.at[k, :, zl, :, c, MOST:64]
+            triples = [(side, side, d_y), (near, near, d_zl)]
         else:
-            src = dst = gathered.at[k, :, :, :, c]
-        if stage == 0:
-            src = w_own.at[k]
-        order = (d_zh, d_y, d_zl, d_c) if cross else (d_zh, d_zl, d_y, d_c)
-        return remote(src, dst, ag_ss.at[stage, k], ag_rs.at[stage, k], order[stage])
-
-    def ag_start(stage, k):
-        if stage in (0, 3):
-            ag_copy(stage, k, False).start()
-        elif isinstance(k, int):
-            ag_copy(stage, k, crossed(k)).start()
-        else:
-            pl.when(crossed(k))(lambda: ag_copy(stage, k, True).start())
-            pl.when(jnp.logical_not(crossed(k)))(lambda: ag_copy(stage, k, False).start())
+            own = gathered.at[k, :, :, :, c]
+            triples = [(own, own, d_c)]
+        first = (0, 1, 3, 5)[stage]
+        return [
+            remote(src, dst, ag_ss.at[first + i, k], ag_rs.at[first + i, k], device)
+            for i, (src, dst, device) in enumerate(triples)
+        ]
+
+    def start_all(copies):
+        for cp in copies:
+            cp.start()
+
+    def wait_recv_all(copies):
+        for cp in copies:
+            cp.wait_recv()
+
+    def wait_send_all(copies):
+        for cp in copies:
+            cp.wait_send()
 
     def load_copy(k, slot):
         return pltpu.make_async_copy(gathered.at[k], wbuf.at[slot], load_sem.at[slot])
@@ -254,36 +259,32 @@
             def step(stage=stage):
                 k = t - stage
                 if stage > 0:
-                    ag_copy(stage - 1, k, False).wait_recv()
-                ag_start(stage, k)
+                    wait_recv_all(ag_copies(stage - 1, k))
+                start_all(ag_copies(stage, k))
             either(within(t, stage, stage + CHUNKS), step)
         def ready():
-            ag_copy(3, t - 4, False).wait_recv()
+            wait_recv_all(ag_copies(3, t - 4))
             load_copy(t - 4, t % 2).start()
         either(within(t, 4, 4 + CHUNKS), ready)
 
-    def rs_copy(stage, r):
-        two, four = r % 2, r % ROUNDS
+    def rs_copies(stage, r):
+        two, slot = r % 2, r % ROUNDS
         if stage == 0:
-            src, dst = part.at[two, :, :, :, 1 - c], r_c.at[two]
-        elif stage == 1:
-            src, dst = t_send.at[two], r_y.at[four]
-        elif stage == 2:
-            src, dst = u_send.at[two], r_zl.at[four]
+            triples = [(part.at[two, :, :, :, 1 - c], r_c.at[two], d_c)]
+        elif stage == 3:
+            triples = [(v_send.at[two], r_zh.at[slot], d_zh)]
         else:
-            src, dst = v_send.at[two], r_zh.at[four]
-        cross = flag(r)
-        to_y, to_zl = f + 2 - 4 * y, f + 4 - 8 * zl
-        if stage == 1:
-            device = (s, to_y * (1 - cross) + to_zl * cross)
-        elif stage == 2:
-            device = (s, to_zl * (1 - cross) + to_y * cross)
-        else:
-            device = partners[3 - stage]
-        return remote(src, dst, rs_ss.at[stage, two], rs_rs.at[stage, four], device)
-
-    def flag(r):
-        return int(crossed(r)) if isinstance(r, int) else crossed(r).astype(jnp.int32)
+            src, dst = ((t_send, r_y), (u_send, r_zl))[stage - 1]
+            devices = ((d_y, d_zl), (d_zl, d_y))[stage - 1]
+            triples = [
+                (src.at[two, :, low:high], dst.at[slot, :, low:high], device)
+                for (low, high), device in zip(SPLIT, devices)
+            ]
+        first = (0, 1, 3, 5)[stage]
+        return [
+            remote(src, dst, rs_ss.at[first + i, two], rs_rs.at[first + i, slot], device)
+            for i, (src, dst, device) in enumerate(triples)
+        ]
 
     def add(a, b):
         return a.astype(jnp.float32) + b.astype(jnp.float32)
@@ -344,58 +345,58 @@
     def rs_tick(r, static_first=False):
         def stage_y():
             k = r - 1
-            rs_copy(0, k).wait_recv()
-            either(within(k, 2, CHUNKS), lambda: rs_copy(1, k - 2).wait_send())
+            wait_recv_all(rs_copies(0, k))
+            either(within(k, 2, CHUNKS), lambda: wait_send_all(rs_copies(1, k - 2)))
             two, four = k % 2, k % ROUNDS
-            cross = flag(k)
 
             def piece(i, _):
                 a, b = i // 2, i % 2
-                near = b * (1 - cross) + (1 - zl) * cross
-                side = (1 - y) * (1 - cross) + b * cross
-                t_send[two, i] = add(part[two, a, near, side, c], r_c[two, a, near, side]).astype(jnp.bfloat16)
-                near = b * (1 - cross) + zl * cross
-                side = y * (1 - cross) + b * cross
-                t_keep[two, i] = add(part[two, a, near, side, c], r_c[two, a, near, side]).astype(jnp.bfloat16)
+                for (low, high), send, keep in zip(
+                    SPLIT, ((b, 1 - y), (1 - zl, b)), ((b, y), (zl, b))
+                ):
+                    for out, (m, n) in ((t_send, send), (t_keep, keep)):
+                        out[two, i, low:high] = add(
+                            part[two, a, m, n, c, low:high], r_c[two, a, m, n, low:high]
+                        ).astype(jnp.bfloat16)
                 return 0
 
             lax.fori_loop(0, 4, piece, 0)
-            rs_copy(1, k).start()
+            start_all(rs_copies(1, k))
         either(within(r, 1, CHUNKS + 1), stage_y)
-        either(within(r, 0, CHUNKS), lambda: rs_copy(0, r).start())
+        either(within(r, 0, CHUNKS), lambda: start_all(rs_copies(0, r)))
 
         def stage_zl():
             k = r - 2
-            rs_copy(1, k).wait_recv()
-            either(within(k, 2, CHUNKS), lambda: rs_copy(2, k - 2).wait_send())
+            wait_recv_all(rs_copies(1, k))
+            either(within(k, 2, CHUNKS), lambda: wait_send_all(rs_copies(2, k - 2)))
             two, four = k % 2, k % ROUNDS
-            cross = flag(k)
-            mine = zl * (1 - cross) + y * cross
             for a in range(2):
-                far, near = a * 2 + 1 - mine, a * 2 + mine
-                u_send[two, a] = add(t_keep[two, far], r_y[four, far]).astype(jnp.bfloat16)
-                u_keep[two, a] = add(t_keep[two, near], r_y[four, near]).astype(jnp.bfloat16)
-            rs_copy(2, k).start()
+                for (low, high), mine in zip(SPLIT, (zl, y)):
+                    for out, at in ((u_send, a * 2 + 1 - mine), (u_keep, a * 2 + mine)):
+                        out[two, a, low:high] = add(
+                            t_keep[two, at, low:high], r_y[four, at, low:high]
+                        ).astype(jnp.bfloat16)
+            start_all(rs_copies(2, k))
         either(within(r, 2, CHUNKS + 2), stage_zl)
 
         def stage_zh():
             k = r - 3
-            rs_copy(2, k).wait_recv()
-            either(within(k, 2, CHUNKS), lambda: rs_copy(3, k - 2).wait_send())
+            wait_recv_all(rs_copies(2, k))
+            either(within(k, 2, CHUNKS), lambda: wait_send_all(rs_copies(3, k - 2)))
             two, four = k % 2, k % ROUNDS
             v_send[two] = add(u_keep[two, 1 - zh], r_zl[four, 1 - zh]).astype(jnp.bfloat16)
             v_keep[two] = add(u_keep[two, zh], r_zl[four, zh]).astype(jnp.bfloat16)
-            rs_copy(3, k).start()
+            start_all(rs_copies(3, k))
         either(within(r, 3, CHUNKS + 3), stage_zh)
 
         def last():
             k = r - 4
-            rs_copy(3, k).wait_recv()
+            wait_recv_all(rs_copies(3, k))
             place_result(k, add(v_keep[k % 2], r_zh[k % ROUNDS]))
         either(within(r, 4, CHUNKS + 4), last)
 
     def part_free(r):
-        either(within(r, 2, CHUNKS), lambda: rs_copy(0, r - 2).wait_send())
+        either(within(r, 2, CHUNKS), lambda: wait_send_all(rs_copies(0, r - 2)))
 
     rim_copy = remote(tok_hbm.at[1008:1024], tokext.at[0:16], rim_ss.at[0], rim_rs.at[0], d_next)
     halo_copy = remote(oacc.at[0:16], oacc.at[1024:1040], rim_ss.at[1], rim_rs.at[1], d_prev)
@@ -408,11 +409,6 @@
     @pl.when(jnp.logical_not(has_next))
     def _():
         oacc[1024:1040, :] = jnp.zeros((16, 1024), jnp.float32)
-
-    row_id = lax.broadcasted_iota(jnp.int32, (128, 256), 0)
-    col_id = lax.broadcasted_iota(jnp.int32, (128, 256), 1) % 128
-    seen = jnp.logical_and(row_id // 8 == col_id // 8, col_id <= row_id)
-    bias[...] = jnp.where(seen, 0.0, -1e30)
 
     gacc[...] = jnp.zeros_like(gacc)
 
@@ -509,61 +505,72 @@
         zero = jnp.zeros_like(v)
         return jnp.concatenate([jnp.where(lane_low, v, zero), jnp.where(lane_low, zero, v)], axis=0)
 
-    def softmax(sc):
-        parts = []
+    own_frame = [
+        lax.broadcasted_iota(jnp.int32, (8, 128), 1) // 8 == fr for fr in range(16)
+    ]
+    key_seen = lax.broadcasted_iota(jnp.int32, (8, 128), 0) <= lax.broadcasted_iota(jnp.int32, (8, 128), 1) % 8
+
+    def compact(full, h):
+        out = full[h * 128 : h * 128 + 8]
+        for fr in range(1, 16):
+            at = h * 128 + fr * 8
+            out = jnp.where(own_frame[fr], full[at : at + 8], out)
+        return out
+
+    def spread(pair):
+        zero = jnp.zeros((8, 128), jnp.float32)
+        rows = [jnp.where(own_frame[fr], x, zero) for x in pair for fr in range(16)]
+        return jnp.concatenate(rows, axis=0).astype(jnp.bfloat16)
+
+    def probabilities(q, kk):
+        full = nt(kk, q)
+        pair = []
         for h in range(2):
-            p = sc[:, h * 128 : h * 128 + 128]
-            e = jnp.exp(p - jnp.max(p, axis=-1, keepdims=True))
-            parts.append(e / jnp.sum(e, axis=-1, keepdims=True))
-        return parts
+            sc = jnp.where(key_seen, compact(full, h) * head_scale, -1e30)
+            e = jnp.exp(sc - jnp.max(sc, axis=0, keepdims=True))
+            pair.append(e / jnp.sum(e, axis=0, keepdims=True))
+        return pair
+
+    def pair_of(g, sub, lo):
+        return [qkv[g, sub, at + lo : at + lo + 128] for at in (0, 256, 512)]
 
     def attn_fwd(g):
         def rows_step(i, _):
-            rows = rows_of(i, 256)
-            for u in range(2):
-                sub = rows_of(i * 2 + u, 128)
-                for p in range(2):
-                    lo = p * 128
-                    q = qkv[g, sub, lo : lo + 128]
-                    k = qkv[g, sub, 256 + lo : 384 + lo]
-                    v = qkv[g, sub, 512 + lo : 640 + lo]
-                    sc = nt(q, both(k)) * head_scale + bias[...]
-                    pr = jnp.concatenate([x.astype(jnp.bfloat16) for x in softmax(sc)], axis=1)
-                    out = mm(pr, both(v)).astype(jnp.bfloat16)
+            for u in range(4):
+                sub = rows_of(i * 4 + u, 128)
+                for lo in (0, 128):
+                    q, k, v = pair_of(g, sub, lo)
+                    pr = spread(probabilities(q, both(k)))
+                    out = tn(pr, both(v)).astype(jnp.bfloat16)
                     mixed[sub, pl.ds(pl.multiple_of(g * 256 + lo, 128), 128)] = out
             return 0
-        lax.fori_loop(0, 4, rows_step, 0)
+        lax.fori_loop(0, 2, rows_step, 0)
 
     def attn_bwd(g):
         def rows_step(i, _):
-            for u in range(2):
-                sub = rows_of(i * 2 + u, 128)
-                for p in range(2):
-                    lo = p * 128
-                    q = qkv[g, sub, lo : lo + 128]
-                    k = qkv[g, sub, 256 + lo : 384 + lo]
-                    v = qkv[g, sub, 512 + lo : 640 + lo]
+            for u in range(4):
+                sub = rows_of(i * 4 + u, 128)
+                for lo in (0, 128):
+                    q, k, v = pair_of(g, sub, lo)
                     do = mixed[sub, pl.ds(pl.multiple_of(g * 256 + lo, 128), 128)]
                     kk = both(k)
-                    sc = nt(q, kk) * head_scale + bias[...]
-                    pr = softmax(sc)
-                    dp = nt(do, both(v))
+                    pr = probabilities(q, kk)
+                    full = nt(both(v), do)
                     ds = []
                     for h in range(2):
-                        d = dp[:, h * 128 : h * 128 + 128]
-                        ds.append((pr[h] * (d - jnp.sum(d * pr[h], axis=-1, keepdims=True))).astype(jnp.bfloat16))
-                    ds = jnp.concatenate(ds, axis=1)
-                    pl_low = jnp.concatenate([x.astype(jnp.bfloat16) for x in pr], axis=1)
-                    dq = mm(ds, kk) * head_scale
-                    dk = tn(ds, q)
-                    dv = tn(pl_low, do)
+                        d = compact(full, h)
+                        ds.append(pr[h] * (d - jnp.sum(d * pr[h], axis=0, keepdims=True)))
+                    ds = spread(ds)
+                    dq = tn(ds, kk) * head_scale
+                    dk = mm(ds, q)
+                    dv = mm(spread(pr), do)
                     qkv[g, sub, lo : lo + 128] = dq.astype(jnp.bfloat16)
                     qkv[g, sub, 256 + lo : 384 + lo] = (
                         jnp.where(lane_low, dk[:128], dk[128:]) * head_scale
                     ).astype(jnp.bfloat16)
                     qkv[g, sub, 512 + lo : 640 + lo] = jnp.where(lane_low, dv[:128], dv[128:]).astype(jnp.bfloat16)
             return 0
-        lax.fori_loop(0, 4, rows_step, 0)
+        lax.fori_loop(0, 2, rows_step, 0)
 
     def qkv_group(g, _):
         slot = (1 + g) % 2
@@ -609,11 +616,11 @@
         two = j % 2
 
         def rows_step(i, _):
-            rows = rows_of(i, 256)
+            rows = rows_of(i, 512)
             w_gu = wbuf[slot, :, :, :, :, :, 0:512].reshape(1024, 512)
             pre = mm(n2[rows, :], w_gu)
             gate, up = pre[:, :256], pre[:, 256:]
-            g_hid = jnp.zeros((256, 256), jnp.float32)
+            g_hid = jnp.zeros((512, 256), jnp.float32)
             for q in range(4):
                 w_q = wbuf[slot, :, :, :, :, q * 16 : q * 16 + 16, 512:768].reshape(256, 256)
                 g_hid = g_hid + nt(cot[rows, q * 256 : q * 256 + 256], w_q)
@@ -637,14 +644,14 @@
                 gn[rows, :] += back
             return 0
 
-        lax.fori_loop(0, 4, rows_step, 0)
+        lax.fori_loop(0, 2, rows_step, 0)
 
         def weight_step(m, _):
-            res = mm(n2t[rows_of(m, 256), :], n1[:, 0:512]).astype(jnp.bfloat16).reshape(2, 2, 64, 512)
-            part[two, m // 2, m % 2, :, :, :, 0:512] = res
+            res = mm(n2t[rows_of(m, 512), :], n1[:, 0:512]).astype(jnp.bfloat16).reshape(2, 2, 2, 64, 512)
+            part[two, m, :, :, :, :, 0:512] = res
             return 0
 
-        lax.fori_loop(0, 4, weight_step, 0)
+        lax.fori_loop(0, 2, weight_step, 0)
         for q in range(4):
             res = mm(hidt[...], cot[:, q * 256 : q * 256 + 256]).astype(jnp.bfloat16)
             part[two, :, :, :, :, q * 16 : q * 16 + 16, 512:768] = res.reshape(2, 2, 2, 2, 16, 256)
@@ -822,11 +829,11 @@
 
     for stage in range(4):
         for k in (CHUNKS - 2, CHUNKS - 1):
-            rs_copy(stage, k).wait_send()
+            wait_send_all(rs_copies(stage, k))
 
     def drain(k, _):
         for stage in range(4):
-            ag_copy(stage, k, False).wait_send()
+            wait_send_all(ag_copies(stage, k))
         return 0
 
     lax.fori_loop(0, CHUNKS, drain, 0)
@@ -878,7 +885,6 @@
             vm((2, 2, 2, 2, 2, 64, WIDE), bf16),
             vm((256, 1024), bf16),
             vm((128, 1024), f32),
-            vm((128, 256), f32),
             vm((16, 1024), f32),
             vm((4, 16, 1024), f32),
             vm((4, 16, 1024), f32),
@@ -895,10 +901,10 @@
             vm((2, 64, WIDE), bf16),
             vm((2, 64, WIDE), bf16),
             vm((FEED, 64, WIDE), f32),
-            dma((4, CHUNKS)),
-            dma((4, CHUNKS)),
-            dma((4, 2)),
-            dma((4, ROUNDS)),
+            dma((6, CHUNKS)),
+            dma((6, CHUNKS)),
+            dma((6, 2)),
+            dma((6, ROUNDS)),
             dma((2,)),
             dma((2,)),
             dma((4,)),

time: 366 us -> 330 us (0.902)
  Pallas kernels: 352 us -> 317 us
    pallas_call x1, Pallas kernels: 352 us -> 317 us  [call_layer(): pl.pallas_call(layer_kernel, name='layer', out_shape=(shape((1024, 1024),...]
where the time goes in v3:
time: 330 us; the launch traced here: 329 us
  Pallas kernels  317 us (96%)
  local copies, waits for them, and re-layouts  12 us (4%)
    pallas_call x1, Pallas kernels, call_layer(): pl.pallas_call(layer_kernel, name='layer', out_shape=(shape((1024, 1024),...  317 us
    unnamed x31, local copies, waits for them, and re-layouts  12 us

profile of v3, /device:TPU:0, one launch (start us, length us, event | category | flops | bytes accessed | tf_op | source)
XLA Modules:
  0.0 329.4 jit_solution(8712377323600944234)
XLA Ops:
  0.6 316.7 %layer.1 = (bf16[1024,1024]{1,0:T(8,128)(2,1)}, f32[1024,1024]{1,0:T(8,128)}, f32[128,512]{1,0:T(8,128)}, f32[32,1024]{1,0:T(8,128)}, f32[8,1024]{1,0:T(8,128)},...) custom-call(bf16[1024,1024]{1,0:T(8,128)(2,1)} %bitcast.19, ...), custom_call_target="tpu_custom_call" | custom-call | tf_op jit(solution)/shard_map/layer/pallas_call | solution.py:851
  317.3 0.0 copy-start
  317.4 3.2 copy.35
  320.6 0.0 copy-done
  320.6 0.0 copy-start.6
  320.6 0.0 copy-start.7
  320.6 0.0 copy-start.9
  320.6 0.0 copy-start.8
  320.6 0.0 copy-start.1
  320.6 2.0 copy.36
  322.6 0.0 copy-done.6
  322.6 0.0 copy-start.5
  322.6 0.0 copy-start.4
  322.6 0.7 copy.37
  323.4 0.0 copy-done.7
  323.4 0.0 copy-start.3
  323.4 0.7 copy.38
  324.0 0.0 copy-done.9
  324.0 0.6 copy.39
  324.6 0.0 copy-done.8
  324.6 0.6 copy.40
  325.2 0.0 copy-done.1
  325.2 0.9 copy.41
  326.1 0.0 copy-done.5
  326.1 0.0 copy-start.2
  326.1 0.7 copy.42
  326.8 0.0 copy-done.4
  326.8 0.9 copy.43
  327.7 0.0 copy-done.3
  327.7 0.9 copy.44
  328.6 0.0 copy-done.2
  328.6 0.9 copy.45
Async XLA Ops:
  317.3 3.2 copy-start
  320.6 2.0 copy-start.6
  320.6 2.8 copy-start.7
  320.6 3.4 %copy-start.9 = (f32[8,1024]{1,0:T(8,128)S(1)}, f32[8,1024]{1,0:T(8,128)}, u32[]{:S(2)}) copy-start(f32[8,1024]{1,0:T(8,128)} %get-tuple-element.26) | copy-start | bytes 98308
  320.6 4.0 %copy-start.8 = (f32[8,1024]{1,0:T(8,128)S(1)}, f32[8,1024]{1,0:T(8,128)}, u32[]{:S(2)}) copy-start(f32[8,1024]{1,0:T(8,128)} %get-tuple-element.27) | copy-start | bytes 98308
  320.6 4.6 %copy-start.1 = (f32[64,3072]{1,0:T(8,128)S(1)}, f32[64,3072]{1,0:T(8,128)}, u32[]{:S(2)}) copy-start(f32[64,3072]{1,0:T(8,128)} %get-tuple-element.28) | copy-start | bytes 2359300
  322.6 3.5 %copy-start.5 = (f32[64,1024]{1,0:T(8,128)S(1)}, f32[64,1024]{1,0:T(8,128)}, u32[]{:S(2)}) copy-start(f32[64,1024]{1,0:T(8,128)} %get-tuple-element.29) | copy-start | bytes 786436
  322.6 4.2 %copy-start.4 = (f32[64,2816]{1,0:T(8,128)S(1)}, f32[64,2816]{1,0:T(8,128)}, u32[]{:S(2)}) copy-start(f32[64,2816]{1,0:T(8,128)} %get-tuple-element.30) | copy-start | bytes 2162692
  323.4 4.3 %copy-start.3 = (f32[64,2816]{1,0:T(8,128)S(1)}, f32[64,2816]{1,0:T(8,128)}, u32[]{:S(2)}) copy-start(f32[64,2816]{1,0:T(8,128)} %get-tuple-element.31) | copy-start | bytes 2162692
  326.1 2.4 copy-start.2

commit v4 on v3

--- a/solution.py
+++ b/solution.py
@@ -98,13 +98,13 @@
     ctx,
     gain_one,
     gain_two,
-    cot,
+    cot_hbm,
     ctx_own,
     qkv_own,
     out_own,
-    gate_own,
-    up_own,
-    down_own,
+    gate_hbm,
+    up_hbm,
+    down_hbm,
     delay,
     lengths,
     mixed_hbm,
@@ -119,13 +119,17 @@
     dup_hbm,
     ddown_hbm,
     gathered,
+    pend,
+    cot,
+    gate_own,
+    up_own,
+    down_own,
     w_own,
     lin,
     n1,
     n1t,
     qkv,
     mixed,
-    mixt,
     aft,
     n2,
     n2t,
@@ -134,6 +138,7 @@
     wbuf,
     wtail,
     part,
+    part_own,
     hidt,
     shift,
     gacc,
@@ -162,7 +167,10 @@
     g_rs,
     own_sem,
     load_sem,
+    pend_sem,
+    half_sem,
     tok_sem,
+    in_sem,
     rim_ss,
     rim_rs,
     out_sem,
@@ -186,6 +194,14 @@
 
     tokext = n2t
     tok_copy = pltpu.make_async_copy(tok_hbm, tokext.at[16:1040], tok_sem)
+    fetches = [
+        pltpu.make_async_copy(src, dst, in_sem.at[i])
+        for i, (src, dst) in enumerate(
+            ((down_hbm, down_own), (gate_hbm, gate_own), (up_hbm, up_own), (cot_hbm, cot))
+        )
+    ]
+    for cp in fetches:
+        cp.start()
     tok_copy.start()
 
     barrier = pltpu.get_barrier_semaphore()
@@ -251,26 +267,42 @@
         for cp in copies:
             cp.wait_send()
 
-    def load_copy(k, slot):
-        return pltpu.make_async_copy(gathered.at[k], wbuf.at[slot], load_sem.at[slot])
+    class load_copy:
+        def __init__(self, k, slot):
+            self.parts = [
+                pltpu.make_async_copy(
+                    gathered.at[k, i // 2, i % 2], wbuf.at[slot, i // 2, i % 2], load_sem.at[slot, i]
+                )
+                for i in range(4)
+            ]
+
+        def start(self):
+            for cp in self.parts:
+                cp.start()
+
+        def wait(self):
+            for cp in self.parts:
+                cp.wait()
 
     def ag_tick(t):
-        for stage in range(4):
-            def step(stage=stage):
-                k = t - stage
+        for stage, lag in enumerate((0, 1, 2, 4)):
+            def step(stage=stage, lag=lag):
+                k = t - lag
                 if stage > 0:
                     wait_recv_all(ag_copies(stage - 1, k))
                 start_all(ag_copies(stage, k))
-            either(within(t, stage, stage + CHUNKS), step)
+            either(within(t, lag, lag + CHUNKS), step)
+
+    def ag_ready(k):
         def ready():
-            wait_recv_all(ag_copies(3, t - 4))
-            load_copy(t - 4, t % 2).start()
-        either(within(t, 4, 4 + CHUNKS), ready)
+            wait_recv_all(ag_copies(3, k))
+            load_copy(k, k % 2).start()
+        either(within(k, 0, CHUNKS), ready)
 
     def rs_copies(stage, r):
-        two, slot = r % 2, r % ROUNDS
+        two, slot = r % (3 if stage == 1 else 2), r % ROUNDS
         if stage == 0:
-            triples = [(part.at[two, :, :, :, 1 - c], r_c.at[two], d_c)]
+            triples = [(pend.at[r, :, :, :, 1 - c], r_c.at[two], d_c)]
         elif stage == 3:
             triples = [(v_send.at[two], r_zh.at[slot], d_zh)]
         else:
@@ -342,12 +374,28 @@
                 row, col = at + 64 * (p // 8), (p % 8) * 128
                 aft[row : row + 64, col : col + 128] = piece
 
-    def rs_tick(r, static_first=False):
+    def pend_copy(r):
+        return pltpu.make_async_copy(part.at[r % 2], pend.at[r], pend_sem.at[r % 2])
+
+    def half_copy(r):
+        return pltpu.make_async_copy(pend.at[r, :, :, :, c], part_own.at[r % 2], half_sem.at[r % 2])
+
+    def part_done(r):
+        either(within(r, 1, CHUNKS), lambda: pend_copy(r - 1).wait())
+        pend_copy(r).start()
+
+    def send_half(r):
+        either(within(r, 2, CHUNKS), lambda: wait_send_all(rs_copies(0, r - 2)))
+        start_all(rs_copies(0, r))
+        half_copy(r).start()
+
+    def rs_tick(r):
         def stage_y():
             k = r - 1
             wait_recv_all(rs_copies(0, k))
-            either(within(k, 2, CHUNKS), lambda: wait_send_all(rs_copies(1, k - 2)))
-            two, four = k % 2, k % ROUNDS
+            half_copy(k).wait()
+            either(within(k, 3, CHUNKS), lambda: wait_send_all(rs_copies(1, k - 3)))
+            two, three = k % 2, k % 3
 
             def piece(i, _):
                 a, b = i // 2, i % 2
@@ -355,48 +403,41 @@
                     SPLIT, ((b, 1 - y), (1 - zl, b)), ((b, y), (zl, b))
                 ):
                     for out, (m, n) in ((t_send, send), (t_keep, keep)):
-                        out[two, i, low:high] = add(
-                            part[two, a, m, n, c, low:high], r_c[two, a, m, n, low:high]
-                        ).astype(jnp.bfloat16)
+                        out[three, i, low:high] = part_own[two, a, m, n, low:high] + r_c[two, a, m, n, low:high]
                 return 0
 
             lax.fori_loop(0, 4, piece, 0)
             start_all(rs_copies(1, k))
         either(within(r, 1, CHUNKS + 1), stage_y)
-        either(within(r, 0, CHUNKS), lambda: start_all(rs_copies(0, r)))
+        either(within(r, 0, CHUNKS), lambda: send_half(r))
 
         def stage_zl():
-            k = r - 2
+            k = r - 3
             wait_recv_all(rs_copies(1, k))
             either(within(k, 2, CHUNKS), lambda: wait_send_all(rs_copies(2, k - 2)))
-            two, four = k % 2, k % ROUNDS
+            two, three, slot = k % 2, k % 3, k % ROUNDS
             for a in range(2):
                 for (low, high), mine in zip(SPLIT, (zl, y)):
                     for out, at in ((u_send, a * 2 + 1 - mine), (u_keep, a * 2 + mine)):
-                        out[two, a, low:high] = add(
-                            t_keep[two, at, low:high], r_y[four, at, low:high]
-                        ).astype(jnp.bfloat16)
+                        out[two, a, low:high] = t_keep[three, at, low:high] + r_y[slot, at, low:high]
             start_all(rs_copies(2, k))
-        either(within(r, 2, CHUNKS + 2), stage_zl)
+        either(within(r, 3, CHUNKS + 3), stage_zl)
 
         def stage_zh():
-            k = r - 3
+            k = r - 4
             wait_recv_all(rs_copies(2, k))
             either(within(k, 2, CHUNKS), lambda: wait_send_all(rs_copies(3, k - 2)))
-            two, four = k % 2, k % ROUNDS
-            v_send[two] = add(u_keep[two, 1 - zh], r_zl[four, 1 - zh]).astype(jnp.bfloat16)
-            v_keep[two] = add(u_keep[two, zh], r_zl[four, zh]).astype(jnp.bfloat16)
+            two, slot = k % 2, k % ROUNDS
+            v_send[two] = u_keep[two, 1 - zh] + r_zl[slot, 1 - zh]
+            v_keep[two] = u_keep[two, zh] + r_zl[slot, zh]
             start_all(rs_copies(3, k))
-        either(within(r, 3, CHUNKS + 3), stage_zh)
+        either(within(r, 4, CHUNKS + 4), stage_zh)
 
         def last():
-            k = r - 4
+            k = r - 5
             wait_recv_all(rs_copies(3, k))
             place_result(k, add(v_keep[k % 2], r_zh[k % ROUNDS]))
-        either(within(r, 4, CHUNKS + 4), last)
-
-    def part_free(r):
-        either(within(r, 2, CHUNKS), lambda: wait_send_all(rs_copies(0, r - 2)))
+        either(within(r, 5, CHUNKS + 5), last)
 
     rim_copy = remote(tok_hbm.at[1008:1024], tokext.at[0:16], rim_ss.at[0], rim_rs.at[0], d_next)
     halo_copy = remote(oacc.at[0:16], oacc.at[1024:1040], rim_ss.at[1], rim_rs.at[1], d_prev)
@@ -442,6 +483,8 @@
     ag_tick(0)
     own_copy(0, 6, 0).wait()
     ag_tick(1)
+    for cp in fetches[:2]:
+        cp.wait()
     for j in range(FEED):
         for q in range(4):
             w_own[6 + j, q * 16 : q * 16 + 16, 512:768] = down_own[
@@ -449,10 +492,12 @@
             ]
     pack_feed(gate_own, 0)
     ag_tick(2)
+    fetches[2].wait()
     pack_feed(up_own, 256)
     own_copy(6, CHUNKS, 1).start()
     ag_tick(3)
     ag_tick(4)
+    ag_ready(0)
     own_copy(6, CHUNKS, 1).wait()
 
     load_copy(0, 0).wait()
@@ -463,12 +508,11 @@
         shift[:, h * half : (h + 1) * half] = mm(ctx[...], w_half)
     xsend[0] = shift[...].astype(jnp.bfloat16)
 
-    def x_copy(i):
-        return remote(xsend.at[i], xrecv.at[i], x_ss.at[i], x_rs.at[i], d_x)
-
-    x_copy(0).start()
+    x_copy = remote(xsend.at[0], xrecv.at[0], x_ss.at[0], x_rs.at[0], d_x)
+    x_copy.start()
     ag_tick(5)
-    x_copy(0).wait_recv()
+    ag_ready(1)
+    x_copy.wait_recv()
     shift[...] = shift[...] + xrecv[0].astype(jnp.float32)
 
     def rows_of(i, size):
@@ -582,8 +626,9 @@
             return 0
 
         lax.fori_loop(0, 4, rows_step, 0)
+        ag_tick(6 + g)
         attn_fwd(g)
-        ag_tick(6 + g)
+        ag_ready(2 + g)
         return 0
 
     lax.fori_loop(0, 4, qkv_group, 0)
@@ -598,25 +643,27 @@
         x = jnp.concatenate([a, b], axis=1)
         aft[rows, :] = x
         oacc[rows, :] = x
+        gn[rows, :] = jnp.zeros((256, 1024), jnp.float32)
         x3 = x.reshape(32, 8, 1024)
         r = lax.rsqrt(jnp.mean(x3 * x3, axis=-1, keepdims=True) + epsilon)
         n = (x3 * r * gain_two[...].astype(jnp.float32)[None]).reshape(256, 1024).astype(jnp.bfloat16)
         n2[rows, :] = n
         n2t[0:1024, rows] = n.T
-        mixt[:, rows] = m.T
         return 0
 
-    lax.fori_loop(0, 4, after, 0)
+    lax.fori_loop(0, 2, after, 0)
     ag_tick(10)
+    lax.fori_loop(2, 4, after, 0)
+    ag_ready(6)
+    fetches[3].wait()
 
     def feed(j, _):
         slot = j % 2
         load_copy(6 + j, slot).wait()
-        part_free(j)
         two = j % 2
 
-        def rows_step(i, _):
-            rows = rows_of(i, 512)
+        def rows_step(i):
+            rows = slice(i * 512, i * 512 + 512)
             w_gu = wbuf[slot, :, :, :, :, :, 0:512].reshape(1024, 512)
             pre = mm(n2[rows, :], w_gu)
             gate, up = pre[:, :256], pre[:, 256:]
@@ -636,15 +683,11 @@
             n1[rows, 0:512] = both_g
             hidt[:, rows] = hid.T
             back = nt(both_g, w_gu)
-            @pl.when(j == 0)
-            def _():
-                gn[rows, :] = back
-            @pl.when(j > 0)
-            def _():
-                gn[rows, :] += back
-            return 0
-
-        lax.fori_loop(0, 2, rows_step, 0)
+            gn[rows, :] += back
+
+        for i in range(2):
+            rows_step(i)
+        ag_tick(11 + j)
 
         def weight_step(m, _):
             res = mm(n2t[rows_of(m, 512), :], n1[:, 0:512]).astype(jnp.bfloat16).reshape(2, 2, 2, 64, 512)
@@ -652,11 +695,12 @@
             return 0
 
         lax.fori_loop(0, 2, weight_step, 0)
+        ag_ready(7 + j)
         for q in range(4):
             res = mm(hidt[...], cot[:, q * 256 : q * 256 + 256]).astype(jnp.bfloat16)
             part[two, :, :, :, :, q * 16 : q * 16 + 16, 512:768] = res.reshape(2, 2, 2, 2, 16, 256)
-        ag_tick(11 + j)
-        rs_tick(j)
+        part_done(j)
+        pl.when(j % 2 == 1)(lambda: rs_tick(j // 2))
         return 0
 
     lax.fori_loop(0, FEED, feed, 0)
@@ -666,8 +710,10 @@
     def norm2_back(i, _):
         rows = rows_of(i, 128)
         n2t[rows, :] = oacc[rows, :].astype(jnp.bfloat16)
+        n1[:, rows] = mixed[rows, :].T
         x = aft[rows, :].reshape(16, 8, 1024)
         g = gn[rows, :].reshape(16, 8, 1024)
+        gn[rows, :] = jnp.zeros((128, 1024), jnp.float32)
         r = lax.rsqrt(jnp.mean(x * x, axis=-1, keepdims=True) + epsilon)
         unit = x * r
         gacc[8:16, :] += jnp.sum(g * unit, axis=0)
@@ -681,16 +727,16 @@
     lax.fori_loop(0, 8, norm2_back, 0)
     mixed_copy = pltpu.make_async_copy(n2t.at[0:1024], mixed_hbm, out_sem.at[0])
     mixed_copy.start()
-
-    part_free(11)
+    rs_tick(5)
+
 
     def out_weight_step(m, _):
-        res = mm(mixt[rows_of(m, 256), :], n2[:, 0:WIDE]).astype(jnp.bfloat16)
+        res = mm(n1[rows_of(m, 256), :], n2[:, 0:WIDE]).astype(jnp.bfloat16)
         part[1, m // 2, m % 2] = res.reshape(2, 2, 64, WIDE)
         return 0
 
     lax.fori_loop(0, 4, out_weight_step, 0)
-    rs_tick(11)
+    part_done(11)
 
     def mixed_back(i, _):
         rows = rows_of(i, 256)
@@ -702,11 +748,12 @@
     load_copy(5, 1).wait()
     lax.fori_loop(0, 4, mixed_back, 0)
     load_copy(2, 1).start()
+    rs_tick(6)
 
     def qkv_back(g, _):
         slot = g % 2
         attn_bwd(g)
-        part_free(12 + g)
+        rs_tick(7 + 2 * g)
         two = g % 2
 
         def weight_step(m, _):
@@ -715,21 +762,17 @@
             return 0
 
         lax.fori_loop(0, 4, weight_step, 0)
-        rs_tick(12 + g)
+        part_done(12 + g)
 
         def rows_step(i, _):
             rows = rows_of(i, 256)
             back = nt(qkv[g, rows, :], wbuf[slot].reshape(1024, WIDE))
-            @pl.when(g == 0)
-            def _():
-                gn[rows, :] = back
-            @pl.when(g > 0)
-            def _():
-                gn[rows, :] += back
+            gn[rows, :] += back
             return 0
 
         load_copy(1 + g, slot).wait()
         lax.fori_loop(0, 4, rows_step, 0)
+        rs_tick(8 + 2 * g)
         pl.when(g < 2)(lambda: load_copy(3 + g, slot).start())
         pl.when(g == 2)(lambda: load_copy(0, 0).start())
         return 0
@@ -747,38 +790,46 @@
         back = r * (gu - unit * jnp.mean(gu * unit, axis=-1, keepdims=True))
         total = oacc[rows, :].reshape(16, 8, 1024) + back
         oacc[rows, :] = total.reshape(128, 1024)
-        shift[rows_of(i, 16), :] = jnp.sum(total, axis=1)
+        few = rows_of(i, 16)
+        g_frame = jnp.sum(total, axis=1)
+        shift[few, :] = g_frame
+        xsend[1, few, :] = g_frame.astype(jnp.bfloat16)
+        x_piece(i).start()
         return 0
+
+    def x_piece(i):
+        few = rows_of(i, 16)
+        return remote(xsend.at[1, few], xrecv.at[1, few], x_ss.at[1 + i], x_rs.at[1 + i], d_x)
 
     lax.fori_loop(0, 8, norm1_back, 0)
     pl.when(has_prev)(lambda: halo_copy.start())
-    xsend[1] = shift[...].astype(jnp.bfloat16)
-    x_copy(1).start()
-
     def gain_copy(i):
         return remote(gsend.at[i], grecv.at[i], g_ss.at[i], g_rs.at[i], partners[i])
 
     gsend[0] = gacc[...]
     gain_copy(0).start()
 
+    pend_copy(15).wait()
+    rs_tick(15)
     load_copy(0, 0).wait()
-    part_free(16)
 
     def out_tail_step(m, _):
-        res = mm(mixt[rows_of(m, 256), :], n2[:, WIDE:1024]).astype(jnp.bfloat16)
+        res = mm(n1[rows_of(m, 256), :], n2[:, WIDE:1024]).astype(jnp.bfloat16)
         part[0, m // 2, m % 2, :, :, :, 512:768] = res.reshape(2, 2, 64, 256)
         return 0
 
     lax.fori_loop(0, 4, out_tail_step, 0)
 
-    x_copy(1).wait_recv()
+    for i in range(8):
+        x_piece(i).wait_recv()
     g_low = (shift[...] + xrecv[1].astype(jnp.float32)).astype(jnp.bfloat16)
     ctx_t = ctx[...].T
     for h in range(2):
         gh = g_low[:, h * 512 : (h + 1) * 512]
         res = mm(ctx_t, gh).astype(jnp.bfloat16).reshape(2, 2, 2, 2, 32, 512)
         part[0, :, :, :, :, h * 32 : h * 32 + 32, 0:512] = res
-    rs_tick(16)
+    pend_copy(16).start()
+    pend_copy(16).wait()
     w0 = wbuf[0, :, :, :, :, 0:32, 0:512].reshape(512, 512)
     w1 = wbuf[0, :, :, :, :, 32:64, 0:512].reshape(512, 512)
     dctx[...] = nt(g_low[:, :512], w0) + nt(g_low[:, 512:], w1)
@@ -796,6 +847,7 @@
         gn[rows, :] = x.reshape(128, 1024)
         return 0
 
+    rs_tick(16)
     dtok_copy = pltpu.make_async_copy(gn, dtok_hbm, out_sem.at[1])
     feed_out = [out_copy(pair, 2 + i) for i, pair in enumerate(feed_copies())]
     for i in range(4):
@@ -808,6 +860,8 @@
             dgain_one[...] = total[0:8]
             dgain_two[...] = total[8:16]
         rs_tick(17 + i)
+        if i == 3:
+            rs_tick(21)
         if i == 0:
             unpack_feed()
             for cp in feed_out:
@@ -824,11 +878,12 @@
 
     for i in range(4):
         gain_copy(i).wait_send()
-    for i in range(2):
-        x_copy(i).wait_send()
+    x_copy.wait_send()
+    for i in range(8):
+        x_piece(i).wait_send()
 
     for stage in range(4):
-        for k in (CHUNKS - 2, CHUNKS - 1):
+        for k in range(CHUNKS - (3 if stage == 1 else 2), CHUNKS):
             wait_send_all(rs_copies(stage, k))
 
     def drain(k, _):
@@ -864,16 +919,20 @@
             shape((64, 2816), f32),
             shape((176, 1024), f32),
             shape((CHUNKS, 2, 2, 2, 2, 64, WIDE), bf16),
+            shape((CHUNKS, 2, 2, 2, 2, 64, WIDE), bf16),
         ),
-        in_specs=[in_hbm] + [in_vmem] * 10 + [in_smem] * 2,
-        out_specs=(in_hbm, in_hbm, in_vmem, in_hbm, in_vmem, in_vmem) + (in_hbm,) * 6,
+        in_specs=[in_hbm] + [in_vmem] * 3 + [in_hbm] + [in_vmem] * 3 + [in_hbm] * 3 + [in_smem] * 2,
+        out_specs=(in_hbm, in_hbm, in_vmem, in_hbm, in_vmem, in_vmem) + (in_hbm,) * 7,
         scratch_shapes=[
+            vm((1024, 1024), bf16),
+            vm((64, 2816), bf16),
+            vm((64, 2816), bf16),
+            vm((176, 1024), bf16),
             vm((CHUNKS, 64, WIDE), bf16),
             vm((1024, 1024), f32),
             vm((1024, 1024), bf16),
             vm((1024, 1024), bf16),
             vm((4, 1024, WIDE), bf16),
-            vm((1024, 1024), bf16),
             vm((1024, 1024), bf16),
             vm((1024, 1024), f32),
             vm((1024, 1024), bf16),
@@ -883,6 +942,7 @@
             vm((2, 2, 2, 2, 2, 64, WIDE), bf16),
             vm((1024, 256), bf16),
             vm((2, 2, 2, 2, 2, 64, WIDE), bf16),
+            vm((2, 2, 2, 2, 64, WIDE), bf16),
             vm((256, 1024), bf16),
             vm((128, 1024), f32),
             vm((16, 1024), f32),
@@ -894,8 +954,8 @@
             vm((ROUNDS, 4, 64, WIDE), bf16),
             vm((ROUNDS, 2, 64, WIDE), bf16),
             vm((ROUNDS, 64, WIDE), bf16),
-            vm((2, 4, 64, WIDE), bf16),
-            vm((2, 4, 64, WIDE), bf16),
+            vm((3, 4, 64, WIDE), bf16),
+            vm((3, 4, 64, WIDE), bf16),
             vm((2, 2, 64, WIDE), bf16),
             vm((2, 2, 64, WIDE), bf16),
             vm((2, 64, WIDE), bf16),
@@ -903,15 +963,18 @@
             vm((FEED, 64, WIDE), f32),
             dma((6, CHUNKS)),
             dma((6, CHUNKS)),
-            dma((6, 2)),
+            dma((6, 3)),
             dma((6, ROUNDS)),
-            dma((2,)),
-            dma((2,)),
+            dma((9,)),
+            dma((9,)),
             dma((4,)),
             dma((4,)),
             dma((2,)),
+            dma((2, 4)),
+            dma((2,)),
             dma((2,)),
             dma,
+            dma((4,)),
             dma((2,)),
             dma((2,)),
             dma((14,)),
@@ -920,6 +983,35 @@
             collective_id=0, has_side_effects=True, vmem_limit_bytes=63 * 1024 * 1024
         ),
     )(tok, ctx, gain_one, gain_two, cot, *weights, delay, lengths)
+
+
+def copy_kernel(*refs):
+    n = (len(refs) - 2) // 3
+    srcs, dsts, held, in_sem, out_sem = refs[:n], refs[n : 2 * n], refs[2 * n : 3 * n], refs[-2], refs[-1]
+    ins = [pltpu.make_async_copy(srcs[i], held[i], in_sem.at[i]) for i in range(n)]
+    outs = [pltpu.make_async_copy(held[i], dsts[i], out_sem.at[i]) for i in range(n)]
+    for cp in ins:
+        cp.start()
+    for cp_in, cp_out in zip(ins, outs):
+        cp_in.wait()
+        cp_out.start()
+    for cp in outs:
+        cp.wait()
+
+
+def copy_all(arrays):
+    n = len(arrays)
+    hbm = pl.BlockSpec(memory_space=pltpu.HBM)
+    return pl.pallas_call(
+        copy_kernel,
+        name="outputs",
+        out_shape=tuple(jax.ShapeDtypeStruct(a.shape, a.dtype) for a in arrays),
+        in_specs=[hbm] * n,
+        out_specs=(hbm,) * n,
+        scratch_shapes=[pltpu.VMEM(a.shape, a.dtype) for a in arrays]
+        + [pltpu.SemaphoreType.DMA((n,)), pltpu.SemaphoreType.DMA((n,))],
+        compiler_params=pltpu.CompilerParams(vmem_limit_bytes=63 * 1024 * 1024),
+    )(*arrays)
 
 
 def body_kernel(
@@ -950,7 +1042,10 @@
         delay,
         lengths,
     )
-    d_qkv, d_out, d_gate, d_up, d_down, _ = grads
+    mixed_out, d_tokens, d_context, d_ctx, d_gain_one, d_gain_two, *grads = copy_all(
+        (mixed_out, d_tokens, d_context, d_ctx, d_gain_one, d_gain_two, *grads[:-2])
+    )
+    d_qkv, d_out, d_gate, d_up, d_down = grads
     return (
         mixed_out.reshape(tokens.shape),
         d_tokens.reshape(tokens.shape),

time: 330 us -> 307 us (0.930)
  local copies, waits for them, and re-layouts: 12 us -> 0 us
  Pallas kernels: 317 us -> 306 us
    pallas_call x1, Pallas kernels: 317 us -> 299 us  [call_layer(): pl.pallas_call(layer_kernel, name='layer', out_shape=(shape((1024, 1024),...]
    unnamed x31 -> x0, local copies, waits for them, and re-layouts: 12 us -> none
    pallas_call x0 -> x1, Pallas kernels: none -> 6.74 us  [copy_all(): pl.pallas_call(copy_kernel, name='outputs', out_shape=tuple((jax.ShapeDty...]
where the time goes in v4:
time: 307 us; the launch traced here: 306 us
  Pallas kernels  306 us (100%)
    pallas_call x1, Pallas kernels, call_layer(): pl.pallas_call(layer_kernel, name='layer', out_shape=(shape((1024, 1024),...  299 us
    pallas_call x1, Pallas kernels, copy_all(): pl.pallas_call(copy_kernel, name='outputs', out_shape=tuple((jax.ShapeDty...  6.74 us

profile of v4, /device:TPU:0, one launch (start us, length us, event | category | flops | bytes accessed | tf_op | source)
XLA Modules:
  0.0 306.4 jit_solution(13656942096862551653)
XLA Ops:
  0.6 298.9 %layer.1 = (bf16[1024,1024]{1,0:T(8,128)(2,1)}, f32[1024,1024]{1,0:T(8,128)}, f32[128,512]{1,0:T(8,128)}, f32[32,1024]{1,0:T(8,128)}, f32[8,1024]{1,0:T(8,128)},...) custom-call(bf16[1024,1024]{1,0:T(8,128)(2,1)} %bitcast.18, ...), custom_call_target="tpu_custom_call" | custom-call | tf_op jit(solution)/shard_map/layer/pallas_call | solution.py:906
  299.5 6.7 %outputs.1 = (bf16[1024,1024]{1,0:T(8,128)(2,1)}, f32[1024,1024]{1,0:T(8,128)}, f32[128,512]{1,0:T(8,128)}, f32[32,1024]{1,0:T(8,128)}, f32[8,1024]{1,0:T(8,128)...) custom-call(bf16[1024,1024]{1,0:T(8,128)(2,1)} %get-tuple-element.33, ...), custom_call_target="tpu_custom_call" | custom-call | tf_op jit(solution)/shard_map/outputs/pallas_call | solution.py:1005

commit v5 on v4

--- a/solution.py
+++ b/solution.py
@@ -63,6 +63,7 @@
 FEED = 11
 WIDE = 768
 ROUNDS = 5
+FAR_ROUNDS = 7
 MOST = 48
 SPLIT = ((0, MOST), (MOST, 64))
 
@@ -284,14 +285,16 @@
             for cp in self.parts:
                 cp.wait()
 
-    def ag_tick(t):
-        for stage, lag in enumerate((0, 1, 2, 4)):
-            def step(stage=stage, lag=lag):
-                k = t - lag
-                if stage > 0:
-                    wait_recv_all(ag_copies(stage - 1, k))
-                start_all(ag_copies(stage, k))
-            either(within(t, lag, lag + CHUNKS), step)
+    def ag_step(stage, k):
+        def go():
+            if stage > 0:
+                wait_recv_all(ag_copies(stage - 1, k))
+            start_all(ag_copies(stage, k))
+        either(within(k, 0, CHUNKS), go)
+
+    def ag_tick(t, gap=1):
+        for stage in range(3):
+            ag_step(stage, t - gap * stage)
 
     def ag_ready(k):
         def ready():
@@ -300,7 +303,7 @@
         either(within(k, 0, CHUNKS), ready)
 
     def rs_copies(stage, r):
-        two, slot = r % (3 if stage == 1 else 2), r % ROUNDS
+        two, slot = r % (2 if stage == 0 else 3), r % (FAR_ROUNDS if stage == 3 else ROUNDS)
         if stage == 0:
             triples = [(pend.at[r, :, :, :, 1 - c], r_c.at[two], d_c)]
         elif stage == 3:
@@ -414,30 +417,30 @@
         def stage_zl():
             k = r - 3
             wait_recv_all(rs_copies(1, k))
-            either(within(k, 2, CHUNKS), lambda: wait_send_all(rs_copies(2, k - 2)))
-            two, three, slot = k % 2, k % 3, k % ROUNDS
+            either(within(k, 3, CHUNKS), lambda: wait_send_all(rs_copies(2, k - 3)))
+            three, slot = k % 3, k % ROUNDS
             for a in range(2):
                 for (low, high), mine in zip(SPLIT, (zl, y)):
                     for out, at in ((u_send, a * 2 + 1 - mine), (u_keep, a * 2 + mine)):
-                        out[two, a, low:high] = t_keep[three, at, low:high] + r_y[slot, at, low:high]
+                        out[three, a, low:high] = t_keep[three, at, low:high] + r_y[slot, at, low:high]
             start_all(rs_copies(2, k))
         either(within(r, 3, CHUNKS + 3), stage_zl)
 
         def stage_zh():
-            k = r - 4
+            k = r - 5
             wait_recv_all(rs_copies(2, k))
-            either(within(k, 2, CHUNKS), lambda: wait_send_all(rs_copies(3, k - 2)))
-            two, slot = k % 2, k % ROUNDS
-            v_send[two] = u_keep[two, 1 - zh] + r_zl[slot, 1 - zh]
-            v_keep[two] = u_keep[two, zh] + r_zl[slot, zh]
+            either(within(k, 3, CHUNKS), lambda: wait_send_all(rs_copies(3, k - 3)))
+            three, slot = k % 3, k % ROUNDS
+            v_send[three] = u_keep[three, 1 - zh] + r_zl[slot, 1 - zh]
+            v_keep[three] = u_keep[three, zh] + r_zl[slot, zh]
             start_all(rs_copies(3, k))
-        either(within(r, 4, CHUNKS + 4), stage_zh)
+        either(within(r, 5, CHUNKS + 5), stage_zh)
 
         def last():
-            k = r - 5
+            k = r - 7
             wait_recv_all(rs_copies(3, k))
-            place_result(k, add(v_keep[k % 2], r_zh[k % ROUNDS]))
-        either(within(r, 5, CHUNKS + 5), last)
+            place_result(k, add(v_keep[k % 3], r_zh[k % FAR_ROUNDS]))
+        either(within(r, 7, CHUNKS + 7), last)
 
     rim_copy = remote(tok_hbm.at[1008:1024], tokext.at[0:16], rim_ss.at[0], rim_rs.at[0], d_next)
     halo_copy = remote(oacc.at[0:16], oacc.at[1024:1040], rim_ss.at[1], rim_rs.at[1], d_prev)
@@ -496,9 +499,10 @@
     pack_feed(up_own, 256)
     own_copy(6, CHUNKS, 1).start()
     ag_tick(3)
-    ag_tick(4)
+    ag_step(3, 0)
     ag_ready(0)
     own_copy(6, CHUNKS, 1).wait()
+    ag_tick(4)
 
     load_copy(0, 0).wait()
     wtail[...] = wbuf[0, :, :, :, :, :, 512:768].reshape(1024, 256)
@@ -511,7 +515,12 @@
     x_copy = remote(xsend.at[0], xrecv.at[0], x_ss.at[0], x_rs.at[0], d_x)
     x_copy.start()
     ag_tick(5)
+    ag_step(3, 1)
     ag_ready(1)
+    ag_tick(6)
+    ag_step(0, 7)
+    ag_step(0, 8)
+    ag_step(1, 6)
     x_copy.wait_recv()
     shift[...] = shift[...] + xrecv[0].astype(jnp.float32)
 
@@ -626,7 +635,8 @@
             return 0
 
         lax.fori_loop(0, 4, rows_step, 0)
-        ag_tick(6 + g)
+        ag_step(3, 2 + g)
+        ag_tick(9 + g, 2)
         attn_fwd(g)
         ag_ready(2 + g)
         return 0
@@ -652,7 +662,8 @@
         return 0
 
     lax.fori_loop(0, 2, after, 0)
-    ag_tick(10)
+    ag_step(3, 6)
+    ag_tick(13, 2)
     lax.fori_loop(2, 4, after, 0)
     ag_ready(6)
     fetches[3].wait()
@@ -687,7 +698,8 @@
 
         for i in range(2):
             rows_step(i)
-        ag_tick(11 + j)
+        ag_step(3, 7 + j)
+        ag_tick(14 + j, 2)
 
         def weight_step(m, _):
             res = mm(n2t[rows_of(m, 512), :], n1[:, 0:512]).astype(jnp.bfloat16).reshape(2, 2, 2, 64, 512)
@@ -700,7 +712,7 @@
             res = mm(hidt[...], cot[:, q * 256 : q * 256 + 256]).astype(jnp.bfloat16)
             part[two, :, :, :, :, q * 16 : q * 16 + 16, 512:768] = res.reshape(2, 2, 2, 2, 16, 256)
         part_done(j)
-        pl.when(j % 2 == 1)(lambda: rs_tick(j // 2))
+        pl.when(jnp.logical_or(j % 2 == 1, j == FEED - 1))(lambda: rs_tick(j // 2))
         return 0
 
     lax.fori_loop(0, FEED, feed, 0)
@@ -727,7 +739,7 @@
     lax.fori_loop(0, 8, norm2_back, 0)
     mixed_copy = pltpu.make_async_copy(n2t.at[0:1024], mixed_hbm, out_sem.at[0])
     mixed_copy.start()
-    rs_tick(5)
+    rs_tick(6)
 
 
     def out_weight_step(m, _):
@@ -748,12 +760,13 @@
     load_copy(5, 1).wait()
     lax.fori_loop(0, 4, mixed_back, 0)
     load_copy(2, 1).start()
-    rs_tick(6)
+    rs_tick(7)
 
     def qkv_back(g, _):
         slot = g % 2
         attn_bwd(g)
-        rs_tick(7 + 2 * g)
+        pend_copy(11 + g).wait()
+        rs_tick(8 + 2 * g)
         two = g % 2
 
         def weight_step(m, _):
@@ -762,7 +775,7 @@
             return 0
 
         lax.fori_loop(0, 4, weight_step, 0)
-        part_done(12 + g)
+        pend_copy(12 + g).start()
 
         def rows_step(i, _):
             rows = rows_of(i, 256)
@@ -772,7 +785,7 @@
 
         load_copy(1 + g, slot).wait()
         lax.fori_loop(0, 4, rows_step, 0)
-        rs_tick(8 + 2 * g)
+        pl.when(g < 3)(lambda: rs_tick(9 + 2 * g))
         pl.when(g < 2)(lambda: load_copy(3 + g, slot).start())
         pl.when(g == 2)(lambda: load_copy(0, 0).start())
         return 0
@@ -849,6 +862,7 @@
 
     rs_tick(16)
     dtok_copy = pltpu.make_async_copy(gn, dtok_hbm, out_sem.at[1])
+    last_out = [out_copy(pair, 9 + i) for i, pair in enumerate(out_copies())]
     feed_out = [out_copy(pair, 2 + i) for i, pair in enumerate(feed_copies())]
     for i in range(4):
         gain_copy(i).wait_recv()
@@ -860,8 +874,6 @@
             dgain_one[...] = total[0:8]
             dgain_two[...] = total[8:16]
         rs_tick(17 + i)
-        if i == 3:
-            rs_tick(21)
         if i == 0:
             unpack_feed()
             for cp in feed_out:
@@ -870,8 +882,13 @@
             lax.fori_loop(0, 8, dtok, 0)
             dtok_copy.start()
 
-    last_out = [out_copy(pair, 9 + i) for i, pair in enumerate(out_copies())]
-    for cp in last_out:
+    rs_tick(21)
+    rs_tick(22)
+    for cp in last_out[2:]:
+        cp.start()
+    rs_tick(23)
+
+    for cp in last_out[:2]:
         cp.start()
     pl.when(has_next)(lambda: rim_copy.wait_send())
     pl.when(has_prev)(lambda: halo_copy.wait_send())
@@ -883,7 +900,7 @@
         x_piece(i).wait_send()
 
     for stage in range(4):
-        for k in range(CHUNKS - (3 if stage == 1 else 2), CHUNKS):
+        for k in range(CHUNKS - (2 if stage == 0 else 3), CHUNKS):
             wait_send_all(rs_copies(stage, k))
 
     def drain(k, _):
@@ -953,18 +970,18 @@
             vm((2, 2, 2, 2, 64, WIDE), bf16),
             vm((ROUNDS, 4, 64, WIDE), bf16),
             vm((ROUNDS, 2, 64, WIDE), bf16),
-            vm((ROUNDS, 64, WIDE), bf16),
+            vm((FAR_ROUNDS, 64, WIDE), bf16),
             vm((3, 4, 64, WIDE), bf16),
             vm((3, 4, 64, WIDE), bf16),
-            vm((2, 2, 64, WIDE), bf16),
-            vm((2, 2, 64, WIDE), bf16),
-            vm((2, 64, WIDE), bf16),
-            vm((2, 64, WIDE), bf16),
+            vm((3, 2, 64, WIDE), bf16),
+            vm((3, 2, 64, WIDE), bf16),
+            vm((3, 64, WIDE), bf16),
+            vm((3, 64, WIDE), bf16),
             vm((FEED, 64, WIDE), f32),
             dma((6, CHUNKS)),
             dma((6, CHUNKS)),
             dma((6, 3)),
-            dma((6, ROUNDS)),
+            dma((6, FAR_ROUNDS)),
             dma((9,)),
             dma((9,)),
             dma((4,)),

time: 307 us -> 302 us (0.984)
  Pallas kernels: 306 us -> 300 us
    pallas_call x1, Pallas kernels: 299 us -> 294 us  [call_layer(): pl.pallas_call(layer_kernel, name='layer', out_shape=(shape((1024, 1024),...]
where the time goes in v5:
time: 302 us; the launch traced here: 301 us
  Pallas kernels  300 us (99%)
    pallas_call x1, Pallas kernels, call_layer(): pl.pallas_call(layer_kernel, name='layer', out_shape=(shape((1024, 1024),...  294 us
    pallas_call x1, Pallas kernels, copy_all(): pl.pallas_call(copy_kernel, name='outputs', out_shape=tuple((jax.ShapeDty...  6.74 us

profile of v5, /device:TPU:0, one launch (start us, length us, event | category | flops | bytes accessed | tf_op | source)
XLA Modules:
  0.0 301.2 jit_solution(9586902894964509668)
XLA Ops:
  0.6 293.7 %layer.1 = (bf16[1024,1024]{1,0:T(8,128)(2,1)}, f32[1024,1024]{1,0:T(8,128)}, f32[128,512]{1,0:T(8,128)}, f32[32,1024]{1,0:T(8,128)}, f32[8,1024]{1,0:T(8,128)},...) custom-call(bf16[1024,1024]{1,0:T(8,128)(2,1)} %bitcast.18, ...), custom_call_target="tpu_custom_call" | custom-call | tf_op jit(solution)/shard_map/layer/pallas_call | solution.py:923
  294.3 6.7 %outputs.1 = (bf16[1024,1024]{1,0:T(8,128)(2,1)}, f32[1024,1024]{1,0:T(8,128)}, f32[128,512]{1,0:T(8,128)}, f32[32,1024]{1,0:T(8,128)}, f32[8,1024]{1,0:T(8,128)...) custom-call(bf16[1024,1024]{1,0:T(8,128)(2,1)} %get-tuple-element.33, ...), custom_call_target="tpu_custom_call" | custom-call | tf_op jit(solution)/shard_map/outputs/pallas_call | solution.py:1022

commit v6 on v5

--- a/solution.py
+++ b/solution.py
@@ -64,8 +64,11 @@
 WIDE = 768
 ROUNDS = 5
 FAR_ROUNDS = 7
-MOST = 48
-SPLIT = ((0, MOST), (MOST, 64))
+SPLIT = ((0, 48), (48, 64))
+HALVES = ((0, 32), (32, 64))
+WHOLE = ((0, 64),)
+GATHER_HALVES = 6
+REDUCE_HALVES = 17
 
 
 def mm(a, b):
@@ -238,14 +241,15 @@
             src_ref=src, dst_ref=dst, send_sem=ss, recv_sem=rs, device_id=device, device_id_type=MESH
         )
 
-    def ag_copies(stage, k):
+    def ag_copies(stage, k, split):
+        low, high = (slice(*rows) for rows in split)
         if stage == 0:
             triples = [(w_own.at[k], gathered.at[k, zh, zl, y, c], d_zh)]
         elif stage == 1:
-            near, side = gathered.at[k, :, zl, y, c, 0:MOST], gathered.at[k, :, zl, y, c, MOST:64]
+            near, side = gathered.at[k, :, zl, y, c, low], gathered.at[k, :, zl, y, c, high]
             triples = [(near, near, d_zl), (side, side, d_y)]
         elif stage == 2:
-            side, near = gathered.at[k, :, :, y, c, 0:MOST], gathered.at[k, :, zl, :, c, MOST:64]
+            side, near = gathered.at[k, :, :, y, c, low], gathered.at[k, :, zl, :, c, high]
             triples = [(side, side, d_y), (near, near, d_zl)]
         else:
             own = gathered.at[k, :, :, :, c]
@@ -256,6 +260,22 @@
             for i, (src, dst, device) in enumerate(triples)
         ]
 
+    def choose(k, bound, under, above, fn):
+        if isinstance(k, int):
+            fn(under if k < bound else above)
+        else:
+            pl.when(k < bound)(lambda: fn(under))
+            pl.when(k >= bound)(lambda: fn(above))
+
+    def ag_do(act, stage, k):
+        if stage in (0, 3):
+            act(ag_copies(stage, k, SPLIT))
+        else:
+            choose(k, GATHER_HALVES, SPLIT, HALVES, lambda split: act(ag_copies(stage, k, split)))
+
+    def by_split(r, fn):
+        choose(r, REDUCE_HALVES, SPLIT, HALVES, fn)
+
     def start_all(copies):
         for cp in copies:
             cp.start()
@@ -288,8 +308,8 @@
     def ag_step(stage, k):
         def go():
             if stage > 0:
-                wait_recv_all(ag_copies(stage - 1, k))
-            start_all(ag_copies(stage, k))
+                ag_do(wait_recv_all, stage - 1, k)
+            ag_do(start_all, stage, k)
         either(within(k, 0, CHUNKS), go)
 
     def ag_tick(t, gap=1):
@@ -298,11 +318,11 @@
 
     def ag_ready(k):
         def ready():
-            wait_recv_all(ag_copies(3, k))
+            ag_do(wait_recv_all, 3, k)
             load_copy(k, k % 2).start()
         either(within(k, 0, CHUNKS), ready)
 
-    def rs_copies(stage, r):
+    def rs_copies(stage, r, split):
         two, slot = r % (2 if stage == 0 else 3), r % (FAR_ROUNDS if stage == 3 else ROUNDS)
         if stage == 0:
             triples = [(pend.at[r, :, :, :, 1 - c], r_c.at[two], d_c)]
@@ -313,13 +333,19 @@
             devices = ((d_y, d_zl), (d_zl, d_y))[stage - 1]
             triples = [
                 (src.at[two, :, low:high], dst.at[slot, :, low:high], device)
-                for (low, high), device in zip(SPLIT, devices)
+                for (low, high), device in zip(split, devices)
             ]
         first = (0, 1, 3, 5)[stage]
         return [
             remote(src, dst, rs_ss.at[first + i, two], rs_rs.at[first + i, slot], device)
             for i, (src, dst, device) in enumerate(triples)
         ]
+
+    def rs_do(act, stage, r):
+        if stage in (0, 3):
+            act(rs_copies(stage, r, SPLIT))
+        else:
+            by_split(r, lambda split: act(rs_copies(stage, r, split)))
 
     def add(a, b):
         return a.astype(jnp.float32) + b.astype(jnp.float32)
@@ -388,57 +414,62 @@
         pend_copy(r).start()
 
     def send_half(r):
-        either(within(r, 2, CHUNKS), lambda: wait_send_all(rs_copies(0, r - 2)))
-        start_all(rs_copies(0, r))
+        either(within(r, 2, CHUNKS), lambda: rs_do(wait_send_all, 0, r - 2))
+        rs_do(start_all, 0, r)
         half_copy(r).start()
 
     def rs_tick(r):
         def stage_y():
             k = r - 1
-            wait_recv_all(rs_copies(0, k))
+            rs_do(wait_recv_all, 0, k)
             half_copy(k).wait()
-            either(within(k, 3, CHUNKS), lambda: wait_send_all(rs_copies(1, k - 3)))
+            either(within(k, 3, CHUNKS), lambda: rs_do(wait_send_all, 1, k - 3))
             two, three = k % 2, k % 3
 
-            def piece(i, _):
-                a, b = i // 2, i % 2
-                for (low, high), send, keep in zip(
-                    SPLIT, ((b, 1 - y), (1 - zl, b)), ((b, y), (zl, b))
-                ):
-                    for out, (m, n) in ((t_send, send), (t_keep, keep)):
-                        out[three, i, low:high] = part_own[two, a, m, n, low:high] + r_c[two, a, m, n, low:high]
-                return 0
-
-            lax.fori_loop(0, 4, piece, 0)
-            start_all(rs_copies(1, k))
+            def pieces(split):
+                def piece(i, _):
+                    a, b = i // 2, i % 2
+                    for (low, high), send, keep in zip(split, ((b, 1 - y), (1 - zl, b)), ((b, y), (zl, b))):
+                        for out, (m, n) in ((t_send, send), (t_keep, keep)):
+                            out[three, i, low:high] = part_own[two, a, m, n, low:high] + r_c[two, a, m, n, low:high]
+                    return 0
+
+                lax.fori_loop(0, 4, piece, 0)
+
+            by_split(k, pieces)
+            rs_do(start_all, 1, k)
         either(within(r, 1, CHUNKS + 1), stage_y)
         either(within(r, 0, CHUNKS), lambda: send_half(r))
 
         def stage_zl():
             k = r - 3
-            wait_recv_all(rs_copies(1, k))
-            either(within(k, 3, CHUNKS), lambda: wait_send_all(rs_copies(2, k - 3)))
+            rs_do(wait_recv_all, 1, k)
+            either(within(k, 3, CHUNKS), lambda: rs_do(wait_send_all, 2, k - 3))
             three, slot = k % 3, k % ROUNDS
-            for a in range(2):
-                for (low, high), mine in zip(SPLIT, (zl, y)):
-                    for out, at in ((u_send, a * 2 + 1 - mine), (u_keep, a * 2 + mine)):
-                        out[three, a, low:high] = t_keep[three, at, low:high] + r_y[slot, at, low:high]
-            start_all(rs_copies(2, k))
+
+            def pieces(split):
+                for a in range(2):
+                    for (low, high), mine in zip(split, (zl, y)):
+                        for out, at in ((u_send, a * 2 + 1 - mine), (u_keep, a * 2 + mine)):
+                            out[three, a, low:high] = t_keep[three, at, low:high] + r_y[slot, at, low:high]
+
+            by_split(k, pieces)
+            rs_do(start_all, 2, k)
         either(within(r, 3, CHUNKS + 3), stage_zl)
 
         def stage_zh():
             k = r - 5
-            wait_recv_all(rs_copies(2, k))
-            either(within(k, 3, CHUNKS), lambda: wait_send_all(rs_copies(3, k - 3)))
+            rs_do(wait_recv_all, 2, k)
+            either(within(k, 3, CHUNKS), lambda: rs_do(wait_send_all, 3, k - 3))
             three, slot = k % 3, k % ROUNDS
             v_send[three] = u_keep[three, 1 - zh] + r_zl[slot, 1 - zh]
             v_keep[three] = u_keep[three, zh] + r_zl[slot, zh]
-            start_all(rs_copies(3, k))
+            rs_do(start_all, 3, k)
         either(within(r, 5, CHUNKS + 5), stage_zh)
 
         def last():
             k = r - 7
-            wait_recv_all(rs_copies(3, k))
+            rs_do(wait_recv_all, 3, k)
             place_result(k, add(v_keep[k % 3], r_zh[k % FAR_ROUNDS]))
         either(within(r, 7, CHUNKS + 7), last)
 
@@ -712,7 +743,8 @@
             res = mm(hidt[...], cot[:, q * 256 : q * 256 + 256]).astype(jnp.bfloat16)
             part[two, :, :, :, :, q * 16 : q * 16 + 16, 512:768] = res.reshape(2, 2, 2, 2, 16, 256)
         part_done(j)
-        pl.when(jnp.logical_or(j % 2 == 1, j == FEED - 1))(lambda: rs_tick(j // 2))
+        pl.when(jnp.logical_and(j % 2 == 1, j < 6))(lambda: rs_tick(j // 2))
+        pl.when(j >= 6)(lambda: rs_tick(j - 3))
         return 0
 
     lax.fori_loop(0, FEED, feed, 0)
@@ -739,7 +771,7 @@
     lax.fori_loop(0, 8, norm2_back, 0)
     mixed_copy = pltpu.make_async_copy(n2t.at[0:1024], mixed_hbm, out_sem.at[0])
     mixed_copy.start()
-    rs_tick(6)
+    rs_tick(8)
 
 
     def out_weight_step(m, _):
@@ -760,13 +792,13 @@
     load_copy(5, 1).wait()
     lax.fori_loop(0, 4, mixed_back, 0)
     load_copy(2, 1).start()
-    rs_tick(7)
+    rs_tick(9)
 
     def qkv_back(g, _):
         slot = g % 2
         attn_bwd(g)
         pend_copy(11 + g).wait()
-        rs_tick(8 + 2 * g)
+        rs_tick(10 + g + g // 2)
         two = g % 2
 
         def weight_step(m, _):
@@ -785,7 +817,7 @@
 
         load_copy(1 + g, slot).wait()
         lax.fori_loop(0, 4, rows_step, 0)
-        pl.when(g < 3)(lambda: rs_tick(9 + 2 * g))
+        pl.when(g == 1)(lambda: rs_tick(12))
         pl.when(g < 2)(lambda: load_copy(3 + g, slot).start())
         pl.when(g == 2)(lambda: load_copy(0, 0).start())
         return 0
@@ -901,11 +933,11 @@
 
     for stage in range(4):
         for k in range(CHUNKS - (2 if stage == 0 else 3), CHUNKS):
-            wait_send_all(rs_copies(stage, k))
+            rs_do(wait_send_all, stage, k)
 
     def drain(k, _):
         for stage in range(4):
-            wait_send_all(ag_copies(stage, k))
+            ag_do(wait_send_all, stage, k)
         return 0
 
     lax.fori_loop(0, CHUNKS, drain, 0)

time: 302 us -> 296 us (0.980)
  Pallas kernels: 300 us -> 295 us
    pallas_call x1, Pallas kernels: 294 us -> 288 us  [call_layer(): pl.pallas_call(layer_kernel, name='layer', out_shape=(shape((1024, 1024),...]
where the time goes in v6:
time: 296 us
  Pallas kernels  295 us (100%)
    pallas_call x1, Pallas kernels, call_layer(): pl.pallas_call(layer_kernel, name='layer', out_shape=(shape((1024, 1024),...  288 us
    pallas_call x1, Pallas kernels, copy_all(): pl.pallas_call(copy_kernel, name='outputs', out_shape=tuple((jax.ShapeDty...  6.74 us

profile of v6, /device:TPU:0, one launch (start us, length us, event | category | flops | bytes accessed | tf_op | source)
XLA Modules:
  0.0 295.6 jit_solution(6044172862840903656)
XLA Ops:
  0.6 288.0 %layer.1 = (bf16[1024,1024]{1,0:T(8,128)(2,1)}, f32[1024,1024]{1,0:T(8,128)}, f32[128,512]{1,0:T(8,128)}, f32[32,1024]{1,0:T(8,128)}, f32[8,1024]{1,0:T(8,128)},...) custom-call(bf16[1024,1024]{1,0:T(8,128)(2,1)} %bitcast.18, ...), custom_call_target="tpu_custom_call" | custom-call | tf_op jit(solution)/shard_map/layer/pallas_call | solution.py:955
  288.7 6.7 %outputs.1 = (bf16[1024,1024]{1,0:T(8,128)(2,1)}, f32[1024,1024]{1,0:T(8,128)}, f32[128,512]{1,0:T(8,128)}, f32[32,1024]{1,0:T(8,128)}, f32[8,1024]{1,0:T(8,128)...) custom-call(bf16[1024,1024]{1,0:T(8,128)(2,1)} %get-tuple-element.33, ...), custom_call_target="tpu_custom_call" | custom-call | tf_op jit(solution)/shard_map/outputs/pallas_call | solution.py:1054

commit v7 on v6

--- a/solution.py
+++ b/solution.py
@@ -546,12 +546,10 @@
     x_copy = remote(xsend.at[0], xrecv.at[0], x_ss.at[0], x_rs.at[0], d_x)
     x_copy.start()
     ag_tick(5)
+    for k in (6, 7, 8):
+        ag_step(0, k)
     ag_step(3, 1)
     ag_ready(1)
-    ag_tick(6)
-    ag_step(0, 7)
-    ag_step(0, 8)
-    ag_step(1, 6)
     x_copy.wait_recv()
     shift[...] = shift[...] + xrecv[0].astype(jnp.float32)
 
@@ -580,7 +578,11 @@
 
     tok_copy.wait()
     pl.when(has_prev)(lambda: rim_copy.wait_recv())
-    lax.fori_loop(0, 8, norm1, 0)
+    lax.fori_loop(0, 4, norm1, 0)
+    ag_step(1, 5)
+    ag_step(2, 4)
+    lax.fori_loop(4, 8, norm1, 0)
+    ag_step(1, 6)
 
     lane_low = lax.broadcasted_iota(jnp.int32, (128, 128), 1) < 64
     head_scale = HEAD ** (-0.5)

time: 296 us -> 296 us (level)
  no operation moved by 1% of the time
where the time goes in v7:
time: 296 us
  Pallas kernels  295 us (100%)
    pallas_call x1, Pallas kernels, call_layer(): pl.pallas_call(layer_kernel, name='layer', out_shape=(shape((1024, 1024),...  288 us
    pallas_call x1, Pallas kernels, copy_all(): pl.pallas_call(copy_kernel, name='outputs', out_shape=tuple((jax.ShapeDty...  6.74 us

profile of v7, /device:TPU:0, one launch (start us, length us, event | category | flops | bytes accessed | tf_op | source)
XLA Modules:
  0.0 295.6 jit_solution(3966604856293664143)
XLA Ops:
  0.6 288.0 %layer.1 = (bf16[1024,1024]{1,0:T(8,128)(2,1)}, f32[1024,1024]{1,0:T(8,128)}, f32[128,512]{1,0:T(8,128)}, f32[32,1024]{1,0:T(8,128)}, f32[8,1024]{1,0:T(8,128)},...) custom-call(bf16[1024,1024]{1,0:T(8,128)(2,1)} %bitcast.18, ...), custom_call_target="tpu_custom_call" | custom-call | tf_op jit(solution)/shard_map/layer/pallas_call | solution.py:957
  288.7 6.7 %outputs.1 = (bf16[1024,1024]{1,0:T(8,128)(2,1)}, f32[1024,1024]{1,0:T(8,128)}, f32[128,512]{1,0:T(8,128)}, f32[32,1024]{1,0:T(8,128)}, f32[8,1024]{1,0:T(8,128)...) custom-call(bf16[1024,1024]{1,0:T(8,128)(2,1)} %get-tuple-element.33, ...), custom_call_target="tpu_custom_call" | custom-call | tf_op jit(solution)/shard_map/outputs/pallas_call | solution.py:1056

commit v8 on v7

--- a/solution.py
+++ b/solution.py
@@ -853,6 +853,16 @@
     def gain_copy(i):
         return remote(gsend.at[i], grecv.at[i], g_ss.at[i], g_rs.at[i], partners[i])
 
+    def gain_step(i):
+        gain_copy(i).wait_recv()
+        total = gsend[i] + grecv[i]
+        if i < 3:
+            gsend[i + 1] = total
+            gain_copy(i + 1).start()
+        else:
+            dgain_one[...] = total[0:8]
+            dgain_two[...] = total[8:16]
+
     gsend[0] = gacc[...]
     gain_copy(0).start()
 
@@ -866,6 +876,7 @@
         return 0
 
     lax.fori_loop(0, 4, out_tail_step, 0)
+    gain_step(0)
 
     for i in range(8):
         x_piece(i).wait_recv()
@@ -898,24 +909,19 @@
     dtok_copy = pltpu.make_async_copy(gn, dtok_hbm, out_sem.at[1])
     last_out = [out_copy(pair, 9 + i) for i, pair in enumerate(out_copies())]
     feed_out = [out_copy(pair, 2 + i) for i, pair in enumerate(feed_copies())]
-    for i in range(4):
-        gain_copy(i).wait_recv()
-        if i < 3:
-            gsend[i + 1] = gsend[i] + grecv[i]
-            gain_copy(i + 1).start()
-        else:
-            total = gsend[i] + grecv[i]
-            dgain_one[...] = total[0:8]
-            dgain_two[...] = total[8:16]
-        rs_tick(17 + i)
-        if i == 0:
-            unpack_feed()
-            for cp in feed_out:
-                cp.start()
-            pl.when(has_next)(lambda: halo_copy.wait_recv())
-            lax.fori_loop(0, 8, dtok, 0)
-            dtok_copy.start()
-
+    pl.when(has_next)(lambda: halo_copy.wait_recv())
+    lax.fori_loop(0, 8, dtok, 0)
+    dtok_copy.start()
+    gain_step(1)
+    rs_tick(17)
+    gain_step(2)
+    unpack_feed()
+    for cp in feed_out:
+        cp.start()
+    gain_step(3)
+    rs_tick(18)
+    rs_tick(19)
+    rs_tick(20)
     rs_tick(21)
     rs_tick(22)
     for cp in last_out[2:]:

time: 296 us -> 296 us (level)
  no operation moved by 1% of the time
where the time goes in v8:
time: 296 us
  Pallas kernels  295 us (100%)
    pallas_call x1, Pallas kernels, call_layer(): pl.pallas_call(layer_kernel, name='layer', out_shape=(shape((1024, 1024),...  288 us
    pallas_call x1, Pallas kernels, copy_all(): pl.pallas_call(copy_kernel, name='outputs', out_shape=tuple((jax.ShapeDty...  6.74 us

profile of v8, /device:TPU:0, one launch (start us, length us, event | category | flops | bytes accessed | tf_op | source)
XLA Modules:
  0.0 295.6 jit_solution(10628470354875352609)
XLA Ops:
  0.6 288.1 %layer.1 = (bf16[1024,1024]{1,0:T(8,128)(2,1)}, f32[1024,1024]{1,0:T(8,128)}, f32[128,512]{1,0:T(8,128)}, f32[32,1024]{1,0:T(8,128)}, f32[8,1024]{1,0:T(8,128)},...) custom-call(bf16[1024,1024]{1,0:T(8,128)(2,1)} %bitcast.18, ...), custom_call_target="tpu_custom_call" | custom-call | tf_op jit(solution)/shard_map/layer/pallas_call | solution.py:963
  288.7 6.7 %outputs.1 = (bf16[1024,1024]{1,0:T(8,128)(2,1)}, f32[1024,1024]{1,0:T(8,128)}, f32[128,512]{1,0:T(8,128)}, f32[32,1024]{1,0:T(8,128)}, f32[8,1024]{1,0:T(8,128)...) custom-call(bf16[1024,1024]{1,0:T(8,128)(2,1)} %get-tuple-element.33, ...), custom_call_target="tpu_custom_call" | custom-call | tf_op jit(solution)/shard_map/outputs/pallas_call | solution.py:1062
